TPU v7x, 32 devices: a whole 2x2x4 slice. The times are simulated.
32 devices in a mesh: row: 8 (over z, core), col: 2 (over x), depth: 2 (over y).
Axes of the slice: x: 2, y: 2, z: 4, core: 2. Of those that a mesh axis runs over, the one named last changes fastest.
Arguments:
- a_blocks: float32 [16, 16, 256, 256], P('row', ('depth', 'col')), may hold values from -6 to 6
- a_pattern: int32 [16, 16], P('row', ('depth', 'col')), may hold values from 0 to 1, as said below
- b_blocks: float32 [16, 8, 256, 256], P(('depth', 'row'), 'col'), may hold values from -0.1875 to 0.1875
- b_pattern: int32 [16, 8], P(('depth', 'row'), 'col'), may hold values from 0 to 1, as said below
- c_pattern: int32 [16, 8], P(('row', 'depth'), 'col'), may hold values 0 or 1
Outputs:
- c_blocks: float32 [16, 8, 256, 256], P(('row', 'depth'), 'col')
Inputs may be any that keep to these rules, and one draw needn't show every extreme that they name: Each block row of a_pattern holds between 1 and 4 stored blocks, and some block row holds exactly 4. Each block column of b_pattern holds between 1 and 4 stored blocks, and some block column holds exactly 4.
All inputs are finite; a program needn't handle non-finite values. No bound on the sum of `c_pattern` on one device may be relied on, other than what follows from the above.
Results may differ from a plain program's by a relative error of at most 0.000071.
Values sent between devices are 32-bit elements; how exact they have to be, the bound alone decides.
No kernel may reach another device: no remote copies, remote signals or barrier semaphores. Data moves between devices by JAX's collectives and lax.ppermute only.
A program may use at most 128 MiB of HBM per device.

v0:
```python
import jax
import jax.numpy as jnp
from jax import lax
from jax.sharding import PartitionSpec as P


def local(a_blocks, a_pattern, b_blocks, b_pattern, c_pattern):
    left = a_blocks * a_pattern[:, :, None, None].astype(jnp.float32)
    right = b_blocks * b_pattern[:, :, None, None].astype(jnp.float32)
    layer_right = lax.all_gather(right, "row", axis=0, tiled=True)
    partial_value = jnp.einsum(
        "rkab,kcbe->rcae",
        lax.all_gather(left, "col", axis=1, tiled=True),
        layer_right,
        precision=lax.Precision.HIGHEST,
    )
    product = lax.psum_scatter(partial_value, "depth", scatter_dimension=0, tiled=True)
    return product * c_pattern[:, :, None, None].astype(jnp.float32)


def solution(mesh):
    in_specs = (
        P("row", ("depth", "col"), None, None),
        P("row", ("depth", "col")),
        P(("depth", "row"), "col", None, None),
        P(("depth", "row"), "col"),
        P(("row", "depth"), "col"),
    )
    out_specs = P(("row", "depth"), "col", None, None)
    return jax.shard_map(local, mesh=mesh, in_specs=in_specs, out_specs=out_specs, check_vma=False)
```

profile of v0, /device:TPU:0, one launch (start us, length us, event | category | flops | bytes accessed | tf_op | source)
XLA Modules:
  0.0 242.8 jit_solution(18035324270290124612)
XLA Ops:
  6.5 0.0 all-gather.5.cloned.1.call-start
  6.5 0.7 convert_element_type.28
  7.2 3.2 %broadcast_multiply_fusion = f32[2,4,256,256]{3,2,1,0:T(8,128)} fusion(f32[2,4,256,256]{3,2,1,0:T(8,128)} %param.5, f32[2,4]{1,0:T(2,128)S(1)} %convert_element_type.28), kind=kLoop, calls=%fused_computation.5 | loop fusion | flops 524288 | bytes 4194336 | tf_op jit(solution)/shard_map/mul | solution.py:8
  10.4 0.0 copy-start
  10.4 0.0 all-gather.5.cloned.1.call-update
  10.4 0.0 all-gather.3.cloned.1.call-start
  10.5 1.1 copy-done
  11.6 0.3 copy.8
  12.0 0.0 copy-done.1
  12.0 1.1 broadcast_multiply_fusion.1
  13.1 0.0 all-gather.3.cloned.1.call-update
  13.2 0.0 all-reduce.3.cloned.1.call-start
  13.2 56.8 %all-gather.5.cloned.1.call-done = f32[2,8,256,256]{3,2,1,0:T(8,128)} async-done(((f32[2,4,256,256]{3,2,1,0:T(8,128)}), f32[2,8,256,256]{3,2,1,0:T(8,128)}) %all-gather.5.cloned.1.call-update) | async-done | bytes 4194320 | tf_op jit(solution)/shard_map/all_gather | solution.py:13
  70.0 83.7 %all-gather.3.cloned.1.call-done = f32[8,4,256,256]{2,3,0,1:T(8,128)} async-done(((f32[1,4,256,256]{2,3,0,1:T(8,128)}), f32[8,4,256,256]{2,3,0,1:T(8,128)}) %all-gather.3.cloned.1.call-update) | async-done | bytes 8388624 | tf_op jit(solution)/shard_map/all_gather | solution.py:10
  153.7 17.6 %fusion.3 = f32[2,4,256,256]{2,3,0,1:T(8,128)} fusion(f32[2,8,256,256]{3,2,1,0:T(8,128)} %all-gather.5.cloned.1.call-done, f32[8,4,256,256]{2,3,0,1:T(8,128)} %all-gather.3.cloned.1.call-done), kind=kOutput, calls=%fused_computation.3 | convolution fusion | flops 12884901888 | bytes 14680064 | tf_op jit(solution)/shard_map/rkab,kcbe->rcae/dot_general | solution.py:11
  171.3 0.0 copy-start.3
  171.4 0.0 copy-start.2
  171.4 0.0 all-reduce.3.cloned.1.call-update
  171.4 0.6 copy-done.3
  172.0 0.6 dynamic-slice
  172.6 0.0 copy-done.2
  172.6 60.4 %all-reduce.3.cloned.1.call-done = f32[2,4,256,256]{2,3,0,1:T(8,128)} async-done(((f32[2,4,256,256]{2,3,0,1:T(8,128)}), f32[2,4,256,256]{2,3,0,1:T(8,128)}) %all-reduce.3.cloned.1.call-update) | async-done | bytes 2097168
  233.0 2.0 dynamic-slice_multiply_fusion
  235.0 1.3 copy.9
  (3 shorter events, 0.0 us)
Async XLA Ops:
  6.5 63.5 %all-gather.5.cloned.1.call-start = ((), (), s32[]{:S(2)}) async-start(), calls=%async_computation.1 | async-start | bytes 6291456 | tf_op jit(solution)/shard_map/all_gather | solution.py:13
  10.4 1.2 copy-start
  10.4 1.6 copy-start.1
  10.4 143.3 %all-gather.3.cloned.1.call-start = ((), (), s32[]{:S(2)}) async-start(), calls=%async_computation | async-start | bytes 9437184 | tf_op jit(solution)/shard_map/all_gather | solution.py:10
  13.2 219.8 %all-reduce.3.cloned.1.call-start = ((), (), s32[]{:S(2)}) async-start(), calls=%async_computation.2 | async-start | bytes 4194304
  171.3 0.7 copy-start.3
  171.4 1.2 copy-start.2
Sparse Core Ops, SparseCore 0:
  10.6 59.4 all-gather.4
  71.6 82.0 all-gather.2
  171.5 61.4 all-reduce.2
where the time goes:
time: 243 us
  waiting for transfers between devices  201 us (83%)
  matrix products  17.6 us (7%)
  between operations  13.1 us (5%)
  other arithmetic  7.04 us (3%)
  local copies, waits for them, and re-layouts  4 us (2%)
    all_gather x1, waiting for transfers between devices, local(): layer_right = lax.all_gather(right, 'row', axis=0, tiled=True)  83.7 us
    unnamed x4, waiting for transfers between devices  60.4 us
    all_gather x1, waiting for transfers between devices, local(): lax.all_gather(left, 'col', axis=1, tiled=True)  56.8 us
    dot_general x1, matrix products, local(): jnp.einsum('rkab,kcbe->rcae', lax.all_gather(left, 'col', axis=1, tiled=T...  17.6 us
  transfers between devices with their start and end apart: 3, of which 3 were waited for; matrix products, arithmetic and copies ran while one was open for 1% of the time, Pallas kernels for 0%

commit v1 on v0

v1 whole, which is shorter than its diff:
```python
import functools

import jax
import jax.numpy as jnp
import numpy as np
from jax import lax
from jax.experimental import pallas as pl
from jax.experimental.pallas import tpu as pltpu
from jax.sharding import PartitionSpec as P

LANES = 128
F32 = jnp.float32
SMEM = pl.BlockSpec(memory_space=pltpu.SMEM)
VMEM = pl.BlockSpec(memory_space=pltpu.VMEM)
ANY = pl.BlockSpec(memory_space=pl.ANY)
PARAMS = pltpu.CompilerParams(vmem_limit_bytes=48 * 1024 * 1024)


class Plan:
    def __init__(self, mesh, a_blocks, b_blocks):
        self.nrow, self.ncol, self.ndep = (mesh.shape[name] for name in ("row", "col", "depth"))
        self.rows, self.kc, self.bs, _ = a_blocks.shape
        self.kb, self.nc, _, _ = b_blocks.shape
        assert self.kb == 1 and self.rows == self.ndep
        every = self.nrow * self.ncol * self.ndep
        self.whole = self.bs // every >= 8
        self.axes = ("row", "col", "depth") if self.whole else ("row", "depth")
        self.G = every if self.whole else self.nrow * self.ndep
        self.R = self.bs // self.G
        self.Q = self.G * self.nc
        self.W = self.kc if self.whole else self.kc * self.ncol
        self.nk = self.kc * self.ncol * self.ndep
        self.most = self.nc * (self.nk // 4)
        self.levels = sorted({min(level, self.most) for level in (2, 3, 4, 5, 6, self.most)})

    def decode(self, s):
        if self.whole:
            return s // (self.ncol * self.ndep), s // self.ndep % self.ncol, s % self.ndep
        return s // self.ndep, s * 0, s % self.ndep

    def tables(self):
        q = np.arange(self.Q)[None, :]
        s = np.arange(self.G)[:, None]
        e = np.arange(LANES)[:, None]
        row_q, col_q, dep_q = self.decode(q % self.G)
        c_q = q // self.G
        row_s, col_s, dep_s = self.decode(s)
        row_t, col_t, dep_t = self.decode(s.T)
        kk = row_q % self.W
        select = [e == rr * self.W + kk for rr in range(self.rows)]
        select += [e == self.rows * self.W + c_q, e == self.rows * self.W + self.nc + c_q]
        holds = (dep_s == dep_q) & (col_s == row_q // self.W)
        own = s == q % self.G
        same_col = col_s == col_q
        before = np.arange(self.Q)[:, None] < q
        pick = [(row_s == row_t) & (dep_s == rr) for rr in range(self.rows)]
        wide = np.concatenate(select, axis=1)
        masks = np.concatenate([holds, own, same_col], axis=0)
        return [jnp.asarray(t.astype(np.float32)) for t in (wide, masks, before, np.concatenate(pick, axis=1))]


def prepare(plan, ap, bp, cp, b_ref, out_ref):
    wide = plan.nc * plan.bs
    for c in range(plan.nc):
        out_ref[:, :, c * plan.bs : (c + 1) * plan.bs] = b_ref[0, c].reshape(plan.G, plan.R, plan.bs)
    lane = lax.broadcasted_iota(jnp.int32, (plan.R, LANES), 1)
    entries = [ap[r, k] for r in range(plan.rows) for k in range(plan.W)]
    entries += [bp[0, c] for c in range(plan.nc)] + [cp[0, c] for c in range(plan.nc)]
    tile = jnp.zeros((plan.R, LANES), F32)
    for place, value in enumerate(entries):
        tile = jnp.where(lane == place, value.astype(F32), tile)
    for s in range(plan.G):
        out_ref[s, :, wide : wide + LANES] = tile


def dot(x, y):
    return jnp.dot(x, y, preferred_element_type=F32)


def schedule(plan, p_ref, wide, masks, before, pick, table_ref, most_ref):
    G, Q = plan.G, plan.Q
    entries = dot(p_ref[:, 0, plan.nc * plan.bs :], wide[...])
    holds, own, same_col = masks[0:G], masks[G : 2 * G], masks[2 * G : 3 * G]
    stored_a = jnp.zeros((G, Q), F32)
    for rr in range(plan.rows):
        stored_a += dot(pick[:, rr * G : (rr + 1) * G], entries[:, rr * Q : (rr + 1) * Q] * holds)
    stored_b = jnp.sum(entries[:, plan.rows * Q : (plan.rows + 1) * Q] * own, axis=0, keepdims=True)
    need = stored_a * stored_b * entries[:, (plan.rows + 1) * Q :] * same_col
    rank = dot(need, before[...])
    count = jnp.sum(need, axis=1, keepdims=True)
    q = lax.broadcasted_iota(jnp.int32, (G, Q), 1).astype(F32)
    lane = lax.broadcasted_iota(jnp.int32, (G, LANES), 1)
    table = jnp.where(lane == LANES - 1, count, 0.0)
    for j in range(plan.most):
        at = jnp.sum(jnp.where(rank == float(j), need, 0.0) * q, axis=1, keepdims=True)
        table = jnp.where(lane == j, at, table)
    table_ref[...] = table.astype(jnp.int32)
    most_ref[0] = jnp.max(count).astype(jnp.int32)


def pack(plan, J, table, got_ref, out_ref):
    def body(d, carry):
        for j in range(J):
            q = table[d, j]
            start = pl.multiple_of(q // plan.G * plan.bs, plan.bs)
            out_ref[d, j] = got_ref[q % plan.G, :, pl.ds(start, plan.bs)]
        return carry

    lax.fori_loop(0, plan.G, body, 0)


def multiply(plan, J, me, table, got_ref, *refs):
    lefts, out_ref, a_scr, sems = refs[:-3], refs[-3], refs[-2], refs[-1]
    member, col, dep = me[0], me[1], me[2]
    count = table[member, LANES - 1]

    def place(j):
        q = table[member, j]
        row_s, _, dep_s = plan.decode(q % plan.G)
        dd = (dep - dep_s + plan.ndep) % plan.ndep
        dc = (col - row_s // plan.kc + plan.ncol) % plan.ncol
        return dd * plan.ncol + dc, row_s % plan.kc, q // plan.G

    for j in range(J):
        which, kk, _ = place(j)
        for n, left in enumerate(lefts):

            @pl.when((j < count) & (which == n))
            def _(left=left, n=n):
                src = left.at[dep, kk] if n == 0 else left.at[kk]
                pltpu.make_async_copy(src, a_scr.at[j], sems.at[j]).start()

    out_ref[...] = jnp.zeros_like(out_ref)
    for j in range(J):

        @pl.when(j < count)
        def _():
            pltpu.make_async_copy(lefts[1].at[0], a_scr.at[j], sems.at[j]).wait()
            _, _, c = place(j)
            right = got_ref[:, j].reshape(plan.bs, plan.bs)
            out_ref[0, c] += jnp.dot(a_scr[j], right, precision=lax.Precision.HIGHEST, preferred_element_type=F32)


def local(mesh, a_blocks, a_pattern, b_blocks, b_pattern, c_pattern):
    plan = Plan(mesh, a_blocks, b_blocks)
    G, R, bs, nc = plan.G, plan.R, plan.bs, plan.nc
    col, dep = lax.axis_index("col"), lax.axis_index("depth")
    me = jnp.stack([lax.axis_index(plan.axes), col, dep]).astype(jnp.int32)

    lefts = [a_blocks]
    for dd in range(plan.ndep):
        send = lax.dynamic_index_in_dim(a_blocks, (dep + dd) % plan.ndep, axis=0, keepdims=False)
        for dc in range(plan.ncol):
            if (dd, dc) != (0, 0):
                perm = [
                    (x * plan.ndep + y, (x + dc) % plan.ncol * plan.ndep + (y + dd) % plan.ndep)
                    for x in range(plan.ncol)
                    for y in range(plan.ndep)
                ]
                lefts.append(lax.ppermute(send, ("col", "depth"), perm))

    if not plan.whole:
        a_pattern = lax.all_gather(a_pattern, "col", axis=1, tiled=True)
    pieces = pl.pallas_call(
        functools.partial(prepare, plan),
        out_shape=jax.ShapeDtypeStruct((G, R, nc * bs + LANES), F32),
        in_specs=[SMEM, SMEM, SMEM, VMEM],
        out_specs=VMEM,
        compiler_params=PARAMS,
        name="prepare",
    )(a_pattern, b_pattern, c_pattern, b_blocks)
    got = lax.all_to_all(pieces, plan.axes, 0, 0, tiled=True)
    table, most = pl.pallas_call(
        functools.partial(schedule, plan),
        out_shape=(jax.ShapeDtypeStruct((G, LANES), jnp.int32), jax.ShapeDtypeStruct((1,), jnp.int32)),
        in_specs=[VMEM] * 5,
        out_specs=(VMEM, SMEM),
        compiler_params=PARAMS,
        name="schedule",
    )(got, *plan.tables())
    most = most[0]
    if not plan.whole:
        most = lax.pmax(most, "col")

    def branch(J, got, table, me, *lefts):
        send = pl.pallas_call(
            functools.partial(pack, plan, J),
            out_shape=jax.ShapeDtypeStruct((G, J, R, bs), F32),
            in_specs=[SMEM, VMEM],
            out_specs=VMEM,
            compiler_params=PARAMS,
            name="pack",
        )(table, got)
        blocks = lax.all_to_all(send, plan.axes, 0, 0, tiled=True)
        return pl.pallas_call(
            functools.partial(multiply, plan, J),
            out_shape=jax.ShapeDtypeStruct((1, nc, bs, bs), F32),
            in_specs=[SMEM, SMEM, VMEM] + [ANY] * len(lefts),
            out_specs=VMEM,
            scratch_shapes=[pltpu.VMEM((J, bs, bs), F32), pltpu.SemaphoreType.DMA((J,))],
            compiler_params=PARAMS,
            name="multiply",
        )(me, table, blocks, *lefts)

    index = sum((most > level).astype(jnp.int32) for level in plan.levels[:-1])
    return lax.switch(index, [functools.partial(branch, level) for level in plan.levels], got, table, me, *lefts)


def solution(mesh):
    in_specs = (
        P("row", ("depth", "col"), None, None),
        P("row", ("depth", "col")),
        P(("depth", "row"), "col", None, None),
        P(("depth", "row"), "col"),
        P(("row", "depth"), "col"),
    )
    out_specs = P(("row", "depth"), "col", None, None)
    return jax.shard_map(
        functools.partial(local, mesh), mesh=mesh, in_specs=in_specs, out_specs=out_specs, check_vma=False
    )
```

time: 243 us -> 109 us (0.45)
  waiting for transfers between devices: 201 us -> 50.2 us
  blocking collectives: 0 us -> 30.1 us
  matrix products: 17.6 us -> 0 us
  starting transfers between devices: 0.09 us -> 10.9 us
  between operations: 13.1 us -> 3.32 us
  Pallas kernels: 0 us -> 7.26 us
  other arithmetic: 7.04 us -> 0.59 us
    all_gather x2 -> x0, waiting for transfers between devices: 141 us -> none  [the longest x1 83.7 us: local(): layer_right = lax.all_gather(right, 'row', axis=0, tiled=True)]
    unnamed x4 -> x0, waiting for transfers between devices: 60.4 us -> none
    all_to_all x0 -> x1, blocking collectives: none -> 30.1 us  [branch(): blocks = lax.all_to_all(send, plan.axes, 0, 0, tiled=True)]
    ppermute x0 -> x3, waiting for transfers between devices: none -> 26.8 us  [local(): lefts.append(lax.ppermute(send, ('col', 'depth'), perm))]
    all_to_all x0 -> x1, waiting for transfers between devices: none -> 23.3 us  [local(): got = lax.all_to_all(pieces, plan.axes, 0, 0, tiled=True)]
    dot_general x1 -> x0, matrix products: 17.6 us -> none  [local(): jnp.einsum('rkab,kcbe->rcae', lax.all_gather(left, 'col', axis=1, tiled=T...]
    all_to_all x0 -> x1, starting transfers between devices: none -> 7.41 us  [local(): got = lax.all_to_all(pieces, plan.axes, 0, 0, tiled=True)]
    pallas_call x0 -> x4, Pallas kernels: none -> 7.26 us  [the longest x1 2.34 us: branch(): pl.pallas_call(functools.partial(pack, plan, J), out_shape=jax.ShapeDtype...]
  transfers between devices with their start and end apart: 3 -> 4, of which waited for: 3 -> 3; matrix products, arithmetic and copies ran while one was open for 1% -> 2% of each run, Pallas kernels for 0% -> 2%
where the time goes in v1:
time: 109 us; the launch traced here: 108 us
  waiting for transfers between devices  50.2 us (46%)
  blocking collectives  30.1 us (28%)
  starting transfers between devices  10.9 us (10%)
  Pallas kernels  7.26 us (7%)
  local copies, waits for them, and re-layouts  5.81 us (5%)
  between operations  3.32 us (3%)
    all_to_all x1, blocking collectives, branch(): blocks = lax.all_to_all(send, plan.axes, 0, 0, tiled=True)  30.1 us
    ppermute x3, waiting for transfers between devices, local(): lefts.append(lax.ppermute(send, ('col', 'depth'), perm))  26.8 us
    all_to_all x1, waiting for transfers between devices, local(): got = lax.all_to_all(pieces, plan.axes, 0, 0, tiled=True)  23.3 us
    all_to_all x1, starting transfers between devices, local(): got = lax.all_to_all(pieces, plan.axes, 0, 0, tiled=True)  7.41 us
    unnamed x22, local copies, waits for them, and re-layouts  4.21 us
    ppermute x3, starting transfers between devices, local(): lefts.append(lax.ppermute(send, ('col', 'depth'), perm))  3.49 us
    pallas_call x1, Pallas kernels, branch(): pl.pallas_call(functools.partial(pack, plan, J), out_shape=jax.ShapeDtype...  2.34 us
  transfers between devices with their start and end apart: 4, of which 3 were waited for; matrix products, arithmetic and copies ran while one was open for 2% of the time, Pallas kernels for 2%

profile of v1, /device:TPU:0, one launch (start us, length us, event | category | flops | bytes accessed | tf_op | source)
XLA Modules:
  0.0 108.4 jit_solution(8171197359414935914)
XLA Ops:
  0.0 1.2 %copy-done = f32[1,4,256,256]{3,2,1,0:T(8,128)S(1)} copy-done((f32[1,4,256,256]{3,2,1,0:T(8,128)S(1)}, f32[1,4,256,256]{3,2,1,0:T(8,128)}, u32[]{:S(2)}) %copy-start) | copy-done | bytes 1048600
  1.2 0.7 copy-done.5
  1.9 0.7 copy-done.6
  2.6 0.7 copy-done.7
  3.2 1.6 %prepare.1 = f32[32,8,1152]{2,1,0:T(8,128)} custom-call(s32[2,4]{1,0:T(2,128)S(1)} %copy-done.5, s32[1,4]{1,0:T(1,128)S(1)} %copy-done.6, s32[1,4]{1,0:T(1,128)S(1)} %copy-done.7, f32[1,4,256,256]{3,2,1,0:T(8,128)S(1)} %copy-done), custom_call_target="tpu_custom_call" | custom-call | tf_op jit(solution)/shard_map/prepare/pallas_call | solution.py:164
  4.9 7.4 %all-to-all-start.6 = ((f32[32,8,1152]{2,1,0:T(8,128)}), f32[32,8,1152]{2,1,0:T(8,128)}, u32[]{:S(2)}, u32[]{:S(2)}) async-start(f32[32,8,1152]{2,1,0:T(8,128)} %prepare.1), calls=%async_computation.6 | async-start | bytes 2359296 | tf_op jit(solution)/shard_map/all_to_all | solution.py:172
  12.3 0.0 copy-start.1
  12.3 0.0 copy-start.2
  12.3 0.0 copy-start.3
  12.4 0.0 copy-start.4
  12.4 1.6 %dynamic-slice_bitcast_fusion = (f32[4,256,256]{2,1,0:T(8,128)}, f32[4,256,256]{2,1,0:T(8,128)}) fusion(f32[2,4,256,256]{3,2,1,0:T(8,128)S(1)} %copy-done.8, s32[]{:T(128)S(6)} %select_n.21, s32[]{:T(128)S(6)} %select_n.19), kind=kLoop, calls=%fused_computation | loop fusion | bytes 4194312 | tf_op jit(solution)/shard_map/jit(dynamic_index_in_dim)/squeeze | solution.py:152
  14.0 1.7 %collective-permute-start = (f32[4,256,256]{2,1,0:T(8,128)}, f32[4,256,256]{2,1,0:T(8,128)S(1)}, u32[]{:S(2)}, u32[]{:S(2)}) collective-permute-start(f32[4,256,256]{2,1,0:T(8,128)} %get-tuple-element.144), channel_id=1, source_target_pairs={{0,2},{1,3},{2,0},{3,1},{4,6},{5,7},{6,4},{7,5},{8,10},{9,11},{10,... | collective-permute-start | bytes 3145736 | tf_op jit(solution)/shard_map/ppermute | solution.py:160
  15.7 1.5 %collective-permute-start.2 = (f32[4,256,256]{2,1,0:T(8,128)}, f32[4,256,256]{2,1,0:T(8,128)}, u32[]{:S(2)}, u32[]{:S(2)}) collective-permute-start(f32[4,256,256]{2,1,0:T(8,128)} %get-tuple-element.143), channel_id=1, source_target_pairs={{0,3},{1,2},{2,1},{3,0},{4,7},{5,6},{6,5},{7,4},{8,11},{9,10},{10,... | collective-permute-start | bytes 3145736 | tf_op jit(solution)/shard_map/ppermute | solution.py:160
  17.1 0.3 collective-permute-start.1
  17.5 0.6 pad_add_fusion
  18.1 23.3 %all-to-all-done.6.p_ref = f32[32,8,1152]{2,1,0:T(8,128)} async-done(((f32[32,8,1152]{2,1,0:T(8,128)}), f32[32,8,1152]{2,1,0:T(8,128)}, u32[]{:S(2)}, u32[]{:S(2)}) %all-to-all-start.6) | async-done | bytes 1179680 | tf_op jit(solution)/shard_map/all_to_all | solution.py:172
  41.4 2.2 %schedule.1 = (s32[32,128]{1,0:T(8,128)S(1)}, s32[1]{0:T(128)}) custom-call(f32[32,8,1152]{2,1,0:T(8,128)} %all-to-all-done.6.p_ref, f32[128,512]{1,0:T(8,128)S(1)} %copy-done.1, f32[96,128]{1,0:T(8,128)S(1)} %copy-done.3, f32[128,128]{1,0:T(8,128)S(1)} %copy-done.2, f32[32,64]{1,0:T(8,128)S(1)} %copy-done.4), custom_call_target="tpu_custom_call" | custom-call | tf_op jit(solution)/shard_map/schedule/pallas_call | solution.py:173
  46.8 3.8 %collective-permute-done = f32[4,256,256]{2,1,0:T(8,128)S(1)} collective-permute-done((f32[4,256,256]{2,1,0:T(8,128)}, f32[4,256,256]{2,1,0:T(8,128)S(1)}, u32[]{:S(2)}, u32[]{:S(2)}) %collective-permute-start) | collective-permute-done | bytes 1048608 | tf_op jit(solution)/shard_map/ppermute | solution.py:160
  50.6 23.0 %collective-permute-done.2 = f32[4,256,256]{2,1,0:T(8,128)} collective-permute-done((f32[4,256,256]{2,1,0:T(8,128)}, f32[4,256,256]{2,1,0:T(8,128)}, u32[]{:S(2)}, u32[]{:S(2)}) %collective-permute-start.2) | collective-permute-done | bytes 1048608 | tf_op jit(solution)/shard_map/ppermute | solution.py:160
  73.6 33.8 %conditional.1 = (f32[1,4,256,256]{3,2,1,0:T(8,128)S(1)}) conditional(s32[]{:T(128)} %bitcast, (s32[32,128]{1,0:T(8,128)S(1)}, f32[32,8,1152]{2,1,0:T(8,128)}, s32[3]{0:T(128)S(1)}, f32[2,4,256,256]{3,2,1,0:T(8,128)S(1)}, f32[4,256,256]{2,1,0:T(8,128)S(1)}, /*index=5*/f32[4,256,256]{2,1,0:T(8,128)}, ...), branch_computations={%region_0.1_spmd, %region_1.2_spmd, %region_2.3_spmd, %region_3.4_... | conditional | bytes 8388616 | solution.py:206
  73.6 2.3 %pack.8 = f32[32,4,8,256]{3,2,1,0:T(8,128)S(1)} custom-call(s32[32,128]{1,0:T(8,128)S(1)} %get-tuple-element.111.table, f32[32,8,1152]{2,1,0:T(8,128)} %get-tuple-element.112.got_ref), custom_call_target="tpu_custom_call" | custom-call | tf_op jit(solution)/shard_map/cond/branch_2_fun/pack/pallas_call | solution.py:186
  76.0 30.1 %all_to_all.31.got_ref = f32[32,4,8,256]{3,2,1,0:T(8,128)S(1)} all-to-all(f32[32,4,8,256]{3,2,1,0:T(8,128)S(1)} %pack.8), channel_id=1, replica_groups=mesh['row'=8,'col'=2,'depth'=2] {'row','col','depth'}, dimensions={0} | all-to-all | bytes 2097152 | tf_op jit(solution)/shard_map/cond/branch_2_fun/all_to_all | solution.py:194
  106.1 1.1 %multiply.8 = f32[1,4,256,256]{3,2,1,0:T(8,128)S(1)} custom-call(s32[3]{0:T(128)S(1)} %get-tuple-element.110.me, s32[32,128]{1,0:T(8,128)S(1)} %get-tuple-element.111.table, f32[32,4,8,256]{3,2,1,0:T(8,128)S(1)} %all_to_all.31.got_ref, f32[2,4,256,256]{3,2,1,0:T(8,128)S(1)} %get-tuple-element.113.refs_0_, f32[4,256,256]{2,1,0:T(8,128)S(1)} %get-tuple-element.114.refs_1_, ...), custom_call_target="tpu_custom_call" | custom-call | tf_op jit(solution)/shard_map/cond/branch_2_fun/multiply/pallas_call | solution.py:195
  107.4 1.0 copy-done.9
  (14 shorter events, 0.0 us)
Async XLA Ops:
  0.0 1.2 %copy-start = (f32[1,4,256,256]{3,2,1,0:T(8,128)S(1)}, f32[1,4,256,256]{3,2,1,0:T(8,128)}, u32[]{:S(2)}) copy-start(f32[1,4,256,256]{3,2,1,0:T(8,128)} %b_ref.1) | copy-start | bytes 3145732
  1.2 0.7 copy-start.5
  1.9 0.7 copy-start.6
  2.6 0.7 copy-start.7
  4.9 7.4 %copy-start.8 = (f32[2,4,256,256]{3,2,1,0:T(8,128)S(1)}, f32[2,4,256,256]{3,2,1,0:T(8,128)}, u32[]{:S(2)}) copy-start(f32[2,4,256,256]{3,2,1,0:T(8,128)} %param.15) | copy-start | bytes 6291460
  4.9 36.5 %all-to-all-start.6 = ((f32[32,8,1152]{2,1,0:T(8,128)}), f32[32,8,1152]{2,1,0:T(8,128)}, u32[]{:S(2)}, u32[]{:S(2)}) async-start(f32[32,8,1152]{2,1,0:T(8,128)} %prepare.1), calls=%async_computation.6 | async-start | bytes 2359296 | tf_op jit(solution)/shard_map/all_to_all | solution.py:172
  12.3 29.1 %copy-start.1 = (f32[128,512]{1,0:T(8,128)S(1)}, f32[128,512]{1,0:T(8,128)}, u32[]{:S(2)}) copy-start(f32[128,512]{1,0:T(8,128)} %constant.61.clone.wide) | copy-start | bytes 786436
  12.3 29.1 %copy-start.2 = (f32[128,128]{1,0:T(8,128)S(1)}, f32[128,128]{1,0:T(8,128)}, u32[]{:S(2)}) copy-start(f32[128,128]{1,0:T(8,128)} %constant.63.clone.before) | copy-start | bytes 196612
  12.3 29.0 %copy-start.3 = (f32[96,128]{1,0:T(8,128)S(1)}, f32[96,128]{1,0:T(8,128)}, u32[]{:S(2)}) copy-start(f32[96,128]{1,0:T(8,128)} %constant.62.clone.masks) | copy-start | bytes 147460
  12.4 29.0 %copy-start.4 = (f32[32,64]{1,0:T(8,128)S(1)}, f32[32,64]{1,0:T(8,128)}, u32[]{:S(2)}) copy-start(f32[32,64]{1,0:T(8,128)} %constant.64.clone.pick) | copy-start | bytes 24580
  14.0 36.7 %collective-permute-start = (f32[4,256,256]{2,1,0:T(8,128)}, f32[4,256,256]{2,1,0:T(8,128)S(1)}, u32[]{:S(2)}, u32[]{:S(2)}) collective-permute-start(f32[4,256,256]{2,1,0:T(8,128)} %get-tuple-element.144), channel_id=1, source_target_pairs={{0,2},{1,3},{2,0},{3,1},{4,6},{5,7},{6,4},{7,5},{8,10},{9,11},{10,... | collective-permute-start | bytes 3145736 | tf_op jit(solution)/shard_map/ppermute | solution.py:160
  15.7 57.9 %collective-permute-start.2 = (f32[4,256,256]{2,1,0:T(8,128)}, f32[4,256,256]{2,1,0:T(8,128)}, u32[]{:S(2)}, u32[]{:S(2)}) collective-permute-start(f32[4,256,256]{2,1,0:T(8,128)} %get-tuple-element.143), channel_id=1, source_target_pairs={{0,3},{1,2},{2,1},{3,0},{4,7},{5,6},{6,5},{7,4},{8,11},{9,10},{10,... | collective-permute-start | bytes 3145736 | tf_op jit(solution)/shard_map/ppermute | solution.py:160
  17.1 56.5 %collective-permute-start.1 = (f32[4,256,256]{2,1,0:T(8,128)}, f32[4,256,256]{2,1,0:T(8,128)}, u32[]{:S(2)}, u32[]{:S(2)}) collective-permute-start(f32[4,256,256]{2,1,0:T(8,128)} %get-tuple-element.143), channel_id=1, source_target_pairs={{0,1},{1,0},{2,3},{3,2},{4,5},{5,4},{6,7},{7,6},{8,9},{9,8},{10,11... | collective-permute-start | bytes 3145736 | tf_op jit(solution)/shard_map/ppermute | solution.py:160
  41.4 32.2 %copy-start.10 = (s32[3]{0:T(128)S(1)}, s32[3]{0:T(128)}, u32[]{:S(2)}) copy-start(s32[3]{0:T(128)} %pad_add_fusion) | copy-start | bytes 40
  107.4 1.0 copy-start.9

commit v2 on v0

v2 whole, which is shorter than its diff:
```python
import functools

import jax
import jax.numpy as jnp
import numpy as np
from jax import lax
from jax.experimental import pallas as pl
from jax.experimental.pallas import tpu as pltpu
from jax.sharding import PartitionSpec as P

LANES = 128
F32 = jnp.float32
BF16 = jnp.bfloat16
I32 = jnp.int32
SMEM = pl.BlockSpec(memory_space=pltpu.SMEM)
VMEM = pl.BlockSpec(memory_space=pltpu.VMEM)
HBM = pl.BlockSpec(memory_space=pltpu.HBM)
DMA = pltpu.SemaphoreType.DMA
PARAMS = pltpu.CompilerParams(vmem_limit_bytes=48 * 1024 * 1024)


class Plan:
    def __init__(self, mesh, a_blocks, b_blocks):
        self.nrow, self.ncol, self.ndep = (mesh.shape[name] for name in ("row", "col", "depth"))
        self.rows, self.kc, self.bs, _ = a_blocks.shape
        self.kb, self.nc, _, _ = b_blocks.shape
        assert self.kb == 1 and self.rows == self.ndep and self.nrow % 2 == 0
        every = self.nrow * self.ncol * self.ndep
        self.whole = self.bs // every >= 8
        self.axes = ("row", "col", "depth") if self.whole else ("row", "depth")
        self.G = every if self.whole else self.nrow * self.ndep
        self.stride = self.G // self.nrow
        self.R = self.bs // self.G
        self.Q = self.G * self.nc
        self.W = self.kc if self.whole else self.kc * self.ncol
        self.nk = self.kc * self.ncol * self.ndep
        self.most = 2 * self.nc * (self.nk // 4)
        self.J = 3 * self.nk // 16
        self.slots = self.nc - 1 if self.whole else self.nc
        self.waves = 2 if self.whole else self.kc
        assert self.G & (self.G - 1) == 0 and self.nc & (self.nc - 1) == 0
        self.g_bits, self.q_bits = self.G.bit_length() - 1, self.Q.bit_length() - 1
        self.others = [(dd, dc) for dd in range(self.ndep) for dc in range(self.ncol) if (dd, dc) != (0, 0)]

    def member(self, value):
        return (value >> 1) & (self.G - 1)

    def column(self, value):
        return (value >> (1 + self.g_bits)) & (self.nc - 1)

    def slot(self, value):
        return value >> (1 + self.q_bits)

    def decode(self, s):
        if self.whole:
            return s // (self.ncol * self.ndep), s // self.ndep % self.ncol, s % self.ndep
        return s // self.ndep, s * 0, s % self.ndep

    def tables(self):
        q = np.arange(self.Q)[None, :]
        s = np.arange(self.G)[:, None]
        e = np.arange(LANES)[:, None]
        row_q, col_q, dep_q = self.decode(q % self.G)
        c_q = q // self.G
        row_s, col_s, dep_s = self.decode(s)
        row_t, col_t, dep_t = self.decode(s.T)
        b0 = self.rows * self.W
        select = [e == rr * self.W + row_q % self.W for rr in range(self.rows)]
        select += [e == b0 + c_q, e == b0 + self.nc + c_q, (e >= b0) & (e < b0 + c_q)]
        holds = (dep_s == dep_q) & (col_s == row_q // self.W)
        masks = [holds, s == q % self.G, col_s == col_q]
        before = np.arange(self.Q)[:, None] < q
        k = np.arange(LANES)[None, :]
        inner = (dep_q * self.nrow + row_q).T == k
        first = inner & (c_q.T == 0) & (col_q.T == 0)
        chunk = (k.T < k) & (k.T // self.kc == k // self.kc) & (k < self.nk)
        pick = [(row_s == row_t) & (dep_s == rr) for rr in range(self.rows)]
        pick += [(row_s // 2 == row_t // 2) & (col_s == col_t) & (dep_s == dep_t)]
        groups = [np.concatenate(select, 1), np.concatenate(masks, 0), before]
        far = (k // self.kc != dep_s * self.ncol + col_s) | (not self.whole)
        groups += [np.concatenate([inner, first], 1), np.concatenate([chunk, far], 0), np.concatenate(pick, 1)]
        return [jnp.asarray(t.astype(np.float32), BF16) for t in groups]


def dot(x, y):
    return jnp.dot(x.astype(BF16), y.astype(BF16), preferred_element_type=F32)


def dot_high(x, y):
    x_high, y_high = x.astype(BF16), y.astype(BF16)
    x_low, y_low = (x - x_high.astype(F32)).astype(BF16), (y - y_high.astype(F32)).astype(BF16)
    return dot(x_high, y_low) + dot(x_low, y_high) + dot(x_high, y_high)


def entry_row(plan, entries):
    row = entries[0:1]
    for r in range(1, plan.rows):
        row += pltpu.roll(entries[r : r + 1], r * plan.W, 1)
    return row


def entry(row, place):
    lane = lax.broadcasted_iota(I32, row.shape, 1)
    return jnp.sum(jnp.where(lane == place, row, 0)) != 0


def prepare(plan, entries, b_hbm, out_ref, sems):
    def piece(c, j):
        return pltpu.make_async_copy(b_hbm.at[c], out_ref.at[:, :, pl.ds(j * plan.bs, plan.bs)], sems.at[j])

    row = entry_row(plan, entries)
    count = jnp.int32(0)
    for c in range(plan.nc):
        stored = entry(row, plan.rows * plan.W + c)
        for j in range(min(c + 1, plan.slots)):

            @pl.when(stored & (count == j))
            def _(c=c, j=j):
                piece(c, j).start()

        count += stored.astype(I32)

    tile = jnp.broadcast_to(row.astype(F32)[None], (plan.G, plan.R, LANES))
    out_ref[:, :, plan.slots * plan.bs :] = tile
    for j in range(plan.slots):

        @pl.when(count > j)
        def _(j=j):
            piece(0, j).wait()


def stage(plan, wave, entries, a_hbm, *refs):
    outs, sems = refs[:-1], refs[-1]
    col, dep = lax.axis_index("col"), lax.axis_index("depth")
    row = entry_row(plan, entries)
    start = 0 if plan.whole else col * plan.kc
    stored = [[entry(row, r * plan.W + start + kk) for kk in range(plan.kc)] for r in range(plan.rows)]

    def each(act):
        for r in range(plan.rows):
            count = jnp.int32(0)
            for kk in range(plan.kc):
                for dd, out in enumerate(outs):

                    @pl.when(stored[r][kk] & (count == wave) & ((dep + dd) % plan.ndep == r))
                    def _(r=r, kk=kk, out=out):
                        act(pltpu.make_async_copy(a_hbm.at[r, kk], out, sems.at[r]))

                count += stored[r][kk].astype(I32)

    each(lambda copy: copy.start())
    each(lambda copy: copy.wait())


def stage_needed(plan, wave, left, a_hbm, *refs):
    outs, sems = refs[:-1], refs[-1]
    row, col, dep = lax.axis_index("row"), lax.axis_index("col"), lax.axis_index("depth")

    def each(act):
        for o, out in enumerate(outs):
            dd, dc = plan.others[o]
            to_dep, to_col = (dep + dd) % plan.ndep, (col + dc) % plan.ncol
            member = (row * plan.ncol + to_col) * plan.ndep + to_dep
            for kk in range(plan.kc):

                @pl.when(left[member, dep * plan.nrow + col * plan.kc + kk] == wave)
                def _(o=o, kk=kk, out=out, to_dep=to_dep):
                    act(pltpu.make_async_copy(a_hbm.at[to_dep, kk], out, sems.at[o]))

    each(lambda copy: copy.start())
    each(lambda copy: copy.wait())


def needs(plan, tile, wide, masks, before, inner, chunk, pick):
    G, Q, rows = plan.G, plan.Q, plan.rows
    entries = dot(tile, wide[...])
    holds, own, same_col = masks[0:G], masks[G : 2 * G], masks[2 * G : 3 * G]
    stored_a = jnp.zeros((G, Q), F32)
    for rr in range(rows):
        stored_a += dot(pick[:, rr * G : (rr + 1) * G], entries[:, rr * Q : (rr + 1) * Q] * holds)
    b0 = rows * Q
    stored_b = jnp.sum(entries[:, b0 : b0 + Q] * own, axis=0, keepdims=True)
    slot = jnp.sum(entries[:, b0 + 2 * Q : b0 + 3 * Q] * own, axis=0, keepdims=True)
    need = stored_a * stored_b * entries[:, b0 + Q : b0 + 2 * Q] * same_col
    both = jnp.minimum(dot(pick[:, rows * G :], need), 1.0)
    rank = dot(both, before[...])
    before_k, far = chunk[0:LANES], chunk[LANES:]
    left = jnp.minimum(dot(need, inner[:, :LANES]), 1.0)
    place = dot(dot(stored_a, inner[:, LANES:]), before_k)
    if plan.whole:
        late = jnp.where(place > 0, left, 0.0)
        place = jnp.where(place > 0, jnp.where(late > 0, 1.0 + dot(late, before_k), -1.0), 0.0)
    name = slot * float(Q) + lax.broadcasted_iota(I32, (1, Q), 1).astype(F32)
    most = jnp.max(jnp.sum(both, axis=1, keepdims=True))
    lost = jnp.max(need * jnp.where(slot >= plan.slots, 1.0, 0.0))
    waves = jnp.max(left * far * (place + 1.0))
    return need, both, rank, name, place, most, lost, waves


def list_blocks(plan, count, need, both, rank, name):
    lane = lax.broadcasted_iota(I32, (plan.G, LANES), 1)
    value = both * name * 2.0 + need
    table = jnp.zeros((plan.G, LANES), F32)
    for j in range(count):
        at = jnp.sum(jnp.where(rank == float(j), value, 0.0) * both, axis=1, keepdims=True)
        table = jnp.where(lane == j, at, table)
    return table.astype(I32)


def fill(plan, again, base, table, got_ref, out_ref):
    def body(d, carry):
        core = (d // plan.stride) & 1
        for p in range(plan.J):
            value = table[d, base + 2 * p + core]
            slot = plan.column(value) if again else plan.slot(value)
            start = pl.multiple_of(slot * plan.bs, plan.bs)
            out_ref[d, p] = got_ref[plan.member(value), :, pl.ds(start, plan.bs)]
        return carry

    lax.fori_loop(0, plan.G, body, 0, unroll=4)


def schedule(plan, got_ref, *refs):
    tables, (out_ref, table_ref, left_ref, state_ref, scratch, sem) = refs[:6], refs[-6:]
    tile = got_ref[:, 0, plan.slots * plan.bs :]
    need, both, rank, name, place, most, lost, waves = needs(plan, tile, *tables)
    table_ref[...] = list_blocks(plan, 2 * plan.J, need, both, rank, name)
    copy = pltpu.make_async_copy(table_ref, scratch, sem.at[0])
    copy.start()
    left_ref[...] = place.astype(I32)
    more = most > 2 * plan.J
    wave = waves > plan.waves
    again = (lost > 0) | (waves > plan.waves + 1) | (wave & more)
    state_ref[0] = jnp.where(again, 3, jnp.where(wave, 2, jnp.where(more, 1, 0)))
    copy.wait()
    fill(plan, False, 0, scratch, got_ref, out_ref)


def relist(plan, tile_ref, *refs):
    tables, (table_ref, rounds_ref) = refs[:-2], refs[-2:]
    need, both, rank, name, _, most, _, _ = needs(plan, tile_ref[:, 0, :], *tables)
    table_ref[...] = list_blocks(plan, plan.most, need, both, rank, name)
    rounds_ref[0] = (most.astype(I32) + 2 * plan.J - 1) // (2 * plan.J)


def pack(plan, again, turn, table, got_ref, out_ref):
    fill(plan, again, turn[0] * (2 * plan.J), table, got_ref, out_ref)


def multiply(plan, again, waves, first, turn, table, left, mine, theirs, a_hbm, *refs):
    lefts, refs = refs[: waves * len(plan.others)], refs[waves * len(plan.others) :]
    start_refs, (out_hbm, a_scr, right, total, sems, out_sem) = refs[:-6], refs[-6:]
    col, dep = lax.axis_index("col"), lax.axis_index("depth")
    member = lax.axis_index(plan.axes)
    core = (member // plan.stride) & 1
    base = 0 if first else turn[0] * (2 * plan.J)
    listed = [table[member, base + j] for j in range(2 * plan.J)]

    def copy(src, j):
        return pltpu.make_async_copy(src, a_scr.at[j], sems.at[j])

    ready = []
    for j, value in enumerate(listed):
        row_s, _, dep_s = plan.decode(plan.member(value))
        dd = (dep - dep_s + plan.ndep) % plan.ndep
        dc = (col - row_s // plan.kc + plan.ncol) % plan.ncol
        kk = row_s % plan.kc
        wave = jnp.int32(0) if again else left[member, dep_s * plan.nrow + row_s]
        ready.append((value & 1 == 1) & (((dd == 0) & (dc == 0)) | (wave < waves)))
        for n, (xd, xc) in enumerate([(0, 0)] + plan.others):
            here = ready[j] & (dd == xd) & (dc == xc)
            for w in range(waves if n else 1):

                @pl.when(here & (wave == w) if n else here)
                def _(n=n, j=j, kk=kk, w=w):
                    src = lefts[w * len(plan.others) + n - 1]
                    copy(a_hbm.at[dep, kk] if n == 0 else src.at[kk] if again else src, j).start()

    if first:
        total[...] = jnp.zeros_like(total)
    else:
        begin = pltpu.make_async_copy(start_refs[0].at[0], total, out_sem.at[0])
        begin.start()
        begin.wait()
    for j, value in enumerate(listed):

        @pl.when(ready[j])
        def _(j=j, value=value):
            @pl.when(core == j % 2)
            def _():
                right[...] = mine[:, j // 2].reshape(plan.bs, plan.bs)

            @pl.when(core != j % 2)
            def _():
                right[...] = theirs[:, j // 2].reshape(plan.bs, plan.bs)

            copy(a_hbm.at[0, 0], j).wait()
            c = plan.column(value)
            total[c] += dot_high(a_scr[j], right[...])

    end = pltpu.make_async_copy(total, out_hbm.at[0], out_sem.at[0])
    end.start()
    end.wait()


def call(kernel, out_shape, in_specs, out_specs, scratch=(), **kwargs):
    return pl.pallas_call(
        kernel,
        out_shape=out_shape,
        in_specs=in_specs,
        out_specs=out_specs,
        scratch_shapes=scratch,
        compiler_params=PARAMS,
        name=kernel.func.__name__,
        **kwargs,
    )


def local(mesh, a_blocks, a_pattern, b_blocks, b_pattern, c_pattern):
    plan = Plan(mesh, a_blocks, b_blocks)
    G, R, J, bs, nc = plan.G, plan.R, plan.J, plan.bs, plan.nc
    listing = jax.ShapeDtypeStruct((G, LANES), I32)
    flag = jax.ShapeDtypeStruct((1,), I32)
    sending = jax.ShapeDtypeStruct((G, J, R, bs), F32)

    def exchange(pieces):
        return lax.all_to_all(pieces, plan.axes, 0, 0, tiled=True)

    def shift(staged):
        def perm(dd, dc):
            for x in range(plan.ncol):
                for y in range(plan.ndep):
                    yield x * plan.ndep + y, (x + dc) % plan.ncol * plan.ndep + (y + dd) % plan.ndep

        return [lax.ppermute(x, ("col", "depth"), list(perm(*by))) for x, by in zip(staged, plan.others)]

    def wave_of(kernel, given, a_blocks, distinct):
        out = call(
            kernel,
            (jax.ShapeDtypeStruct((bs, bs), F32),) * distinct,
            [SMEM if kernel.func is stage_needed else VMEM, HBM],
            (VMEM,) * distinct,
            [DMA((distinct,))],
        )(given, a_blocks)
        return shift(out if kernel.func is stage_needed else [out[dd] for dd, _ in plan.others])

    def swap(mine):
        return lax.ppermute(mine, "row", [(i, i ^ 1) for i in range(plan.nrow)])

    def product(again, turn, table, left, mine, theirs, a_blocks, lefts, start=None):
        starts = [] if start is None else [start]
        return call(
            functools.partial(multiply, plan, again, len(lefts) // len(plan.others), start is None),
            jax.ShapeDtypeStruct((1, nc, bs, bs), F32),
            [SMEM, SMEM, SMEM, VMEM, VMEM] + [HBM] * (1 + len(lefts) + len(starts)),
            HBM,
            [
                pltpu.VMEM((2 * J, bs, bs), F32),
                pltpu.VMEM((bs, bs), F32),
                pltpu.VMEM((nc, bs, bs), F32),
                DMA((2 * J,)),
                DMA((1,)),
            ],
        )(turn, table, left, mine, theirs, a_blocks, *lefts, *starts)

    if not plan.whole:
        a_pattern = lax.all_gather(a_pattern, "col", axis=1, tiled=True)
    b0 = plan.rows * plan.W
    entries = jnp.pad(b_pattern, ((0, plan.rows - 1), (b0, LANES - b0 - nc)))
    entries += jnp.pad(c_pattern, ((0, plan.rows - 1), (b0 + nc, LANES - b0 - 2 * nc)))
    entries += jnp.pad(a_pattern, ((0, 0), (0, LANES - plan.W)))

    b_pieces = b_blocks.reshape(nc, G, R, bs)
    width = plan.slots * bs + LANES
    pieces = call(
        functools.partial(prepare, plan),
        jax.ShapeDtypeStruct((G, R, width), F32),
        [VMEM, HBM],
        VMEM,
        [DMA((plan.slots,))],
    )(entries, b_pieces)
    got = exchange(pieces)
    early = 1 if plan.whole else plan.waves
    lefts = []
    for wave in range(early):
        lefts += wave_of(functools.partial(stage, plan, wave), entries, a_blocks, plan.ndep)

    tables = plan.tables()
    beside = lefts
    send, table, left, state = call(
        functools.partial(schedule, plan),
        (sending, listing, listing, flag),
        [VMEM] * (1 + len(tables)) + [HBM] * len(beside),
        (VMEM, VMEM, VMEM, SMEM),
        [pltpu.SMEM((G, LANES), I32), DMA((1,))],
    )(got, *tables, *beside)
    mine = exchange(send)
    if plan.whole:
        late = wave_of(functools.partial(stage_needed, plan, 1), left, a_blocks, len(plan.others))
        mine, late = lax.optimization_barrier((mine, late))
        lefts = lefts + late
    theirs = swap(mine)
    c_blocks = product(False, state, table, left, mine, theirs, a_blocks, lefts)

    def rounds(again, got, pieces, left, a_blocks, lefts, first, c_blocks):
        table, total = call(
            functools.partial(relist, plan),
            (listing, flag),
            [pl.BlockSpec((G, R, LANES), lambda i: (0, 0, plan.slots * bs // LANES))]
            + [pl.BlockSpec(t.shape, lambda i: (0, 0)) for t in tables],
            (VMEM, SMEM),
            grid=(1,),
        )(got, *tables)
        total = total[0] if plan.whole else lax.pmax(total[0], "col")

        def body(turn, c_blocks):
            turn = jnp.reshape(turn, (1,))
            send = call(functools.partial(pack, plan, again), sending, [SMEM, SMEM, VMEM], VMEM)(turn, table, pieces)
            mine = exchange(send)
            return product(again, turn, table, left, mine, swap(mine), a_blocks, lefts, c_blocks)

        return lax.fori_loop(first, total, body, c_blocks)

    def done(c_blocks, *_):
        return c_blocks

    def more_rounds(c_blocks, mine, theirs, got, table, left, a_blocks, b_pieces, *lefts):
        return rounds(False, got, got, left, a_blocks, lefts, 1, c_blocks)

    def more_waves(c_blocks, mine, theirs, got, table, left, a_blocks, b_pieces, *lefts):
        if plan.whole:
            lefts += tuple(wave_of(functools.partial(stage_needed, plan, 2), left, a_blocks, len(plan.others)))
        return product(False, jnp.zeros((1,), I32), table, left, mine, theirs, a_blocks, lefts)

    def anew(c_blocks, mine, theirs, got, table, left, a_blocks, b_pieces, *lefts):
        pieces = exchange(b_pieces.transpose(1, 2, 0, 3).reshape(G, R, nc * bs))
        dep = lax.axis_index("depth")
        raw = [lax.dynamic_index_in_dim(a_blocks, (dep + dd) % plan.ndep, keepdims=False) for dd, _ in plan.others]
        return rounds(True, got, pieces, left, a_blocks, shift(raw), 0, jnp.zeros_like(c_blocks))

    index = state[0] if plan.whole else lax.pmax(state[0], "col")
    branches = [done, more_rounds, more_waves, anew]
    return lax.switch(index, branches, c_blocks, mine, theirs, got, table, left, a_blocks, b_pieces, *lefts)


def solution(mesh):
    in_specs = (
        P("row", ("depth", "col"), None, None),
        P("row", ("depth", "col")),
        P(("depth", "row"), "col", None, None),
        P(("depth", "row"), "col"),
        P(("row", "depth"), "col"),
    )
    out_specs = P(("row", "depth"), "col", None, None)
    return jax.shard_map(
        functools.partial(local, mesh), mesh=mesh, in_specs=in_specs, out_specs=out_specs, check_vma=False
    )
```

time: 243 us -> 73.5 us (0.30)
  waiting for transfers between devices: 201 us -> 40 us
  starting transfers between devices: 0.09 us -> 20 us
  matrix products: 17.6 us -> 0 us
  between operations: 13.1 us -> 0.96 us
  Pallas kernels: 0 us -> 10.6 us
  other arithmetic: 7.04 us -> 0.77 us
  local copies, waits for them, and re-layouts: 4 us -> 0.02 us
    all_gather x2 -> x0, waiting for transfers between devices: 141 us -> none  [the longest x1 83.7 us: local(): layer_right = lax.all_gather(right, 'row', axis=0, tiled=True)]
    unnamed x4 -> x0, waiting for transfers between devices: 60.4 us -> none
    ppermute x0 -> x7, waiting for transfers between devices: none -> 40 us  [the longest x6 38.4 us: shift(): lax.ppermute(x, ('col', 'depth'), list(perm(*by)))]
    dot_general x1 -> x0, matrix products: 17.6 us -> none  [local(): jnp.einsum('rkab,kcbe->rcae', lax.all_gather(left, 'col', axis=1, tiled=T...]
    all_to_all x0 -> x2, starting transfers between devices: none -> 12.9 us  [exchange(): return lax.all_to_all(pieces, plan.axes, 0, 0, tiled=True)]
    pallas_call x0 -> x5, Pallas kernels: none -> 10.6 us  [the longest x1 3.94 us: local(): call(functools.partial(schedule, plan), (sending, listing, listing, flag)...]
    ppermute x0 -> x7, starting transfers between devices: none -> 7.11 us  [the longest x6 7.11 us: shift(): lax.ppermute(x, ('col', 'depth'), list(perm(*by)))]
    mul x3 -> x0, other arithmetic: 6.35 us -> none  [the longest x1 3.2 us: local(): left = a_blocks * a_pattern[:, :, None, None].astype(jnp.float32)]
  transfers between devices with their start and end apart: 3 -> 9, of which waited for: 3 -> 6; matrix products, arithmetic and copies ran while one was open for 1% -> 0% of each run, Pallas kernels for 0% -> 3%
where the time goes in v2:
time: 73.5 us; the launch traced here: 72.6 us
  waiting for transfers between devices  40 us (54%)
  starting transfers between devices  20 us (27%)
  Pallas kernels  10.6 us (14%)
  between operations  0.96 us (1%)
  other arithmetic  0.77 us (1%)
    ppermute x6, waiting for transfers between devices, shift(): lax.ppermute(x, ('col', 'depth'), list(perm(*by)))  38.4 us
    all_to_all x2, starting transfers between devices, exchange(): return lax.all_to_all(pieces, plan.axes, 0, 0, tiled=True)  12.9 us
    ppermute x6, starting transfers between devices, shift(): lax.ppermute(x, ('col', 'depth'), list(perm(*by)))  7.11 us
    pallas_call x1, Pallas kernels, local(): call(functools.partial(schedule, plan), (sending, listing, listing, flag)...  3.94 us
    pallas_call x1, Pallas kernels, product(): call(functools.partial(multiply, plan, again, len(lefts) // len(plan.othe...  3.28 us
    pallas_call x2, Pallas kernels, wave_of(): call(kernel, (jax.ShapeDtypeStruct((bs, bs), F32),) * distinct, [SMEM if...  2.18 us
    ppermute x1, waiting for transfers between devices, swap(): return lax.ppermute(mine, 'row', [(i, i ^ 1) for i in range(plan.nrow)])  1.6 us
  transfers between devices with their start and end apart: 9, of which 6 were waited for; matrix products, arithmetic and copies ran while one was open for 0% of the time, Pallas kernels for 3%

profile of v2, /device:TPU:0, one launch (start us, length us, event | category | flops | bytes accessed | tf_op | source)
XLA Modules:
  0.0 72.6 jit_solution(7989323713408827690)
XLA Ops:
  0.0 0.8 %pad_add_fusion.entries = s32[2,128]{1,0:T(2,128)S(1)} fusion(s32[2,4]{1,0:T(2,128)} %param.20, s32[1,4]{1,0:T(1,128)} %param.23, s32[1,4]{1,0:T(1,128)} %param.22), kind=kLoop, calls=%fused_computation.2 | loop fusion | flops 512 | bytes 1088 | tf_op jit(solution)/shard_map/add | solution.py:371
  0.8 1.2 %prepare.1 = f32[32,8,896]{2,1,0:T(8,128)} custom-call(s32[2,128]{1,0:T(2,128)S(1)} %pad_add_fusion.entries, f32[4,32,8,256]{3,2,1,0:T(8,128)} %bitcast.17), custom_call_target="tpu_custom_call" | custom-call | tf_op jit(solution)/shard_map/prepare/pallas_call | solution.py:375
  2.0 0.0 copy-start.8
  2.0 0.0 copy-start.9
  2.0 0.0 copy-start.10
  2.0 8.2 %all-to-all-start.3 = ((f32[32,8,896]{2,1,0:T(8,128)}), f32[32,8,896]{2,1,0:T(8,128)S(1)}, u32[]{:S(2)}, u32[]{:S(2)}) async-start(f32[32,8,896]{2,1,0:T(8,128)} %prepare.1), calls=%async_computation.3 | async-start | bytes 1835008 | tf_op jit(solution)/shard_map/all_to_all | solution.py:327
  10.2 1.2 %stage.1 = (f32[256,256]{1,0:T(8,128)S(1)}, f32[256,256]{1,0:T(8,128)S(1)}) custom-call(s32[2,128]{1,0:T(2,128)S(1)} %pad_add_fusion.entries, f32[2,4,256,256]{3,2,1,0:T(8,128)} %a_hbm.5), custom_call_target="tpu_custom_call" | custom-call | tf_op jit(solution)/shard_map/stage/pallas_call | solution.py:338
  11.5 1.7 %collective-permute-start.10 = (f32[256,256]{1,0:T(8,128)S(1)}, f32[256,256]{1,0:T(8,128)S(1)}, u32[]{:S(2)}, u32[]{:S(2)}) collective-permute-start(f32[256,256]{1,0:T(8,128)S(1)} %get-tuple-element.264), channel_id=1, source_target_pairs={{0,3},{1,2},{2,1},{3,0},{4,7},{5,6},{6,5},{7,4},{8,11},{9,10},{10,... | collective-permute-start | bytes 786440 | tf_op jit(solution)/shard_map/ppermute | solution.py:335
  13.2 0.6 collective-permute-start.9
  13.8 1.2 %collective-permute-start.8 = (f32[256,256]{1,0:T(8,128)S(1)}, f32[256,256]{1,0:T(8,128)S(1)}, u32[]{:S(2)}, u32[]{:S(2)}) collective-permute-start(f32[256,256]{1,0:T(8,128)S(1)} %get-tuple-element.263), channel_id=1, source_target_pairs={{0,2},{1,3},{2,0},{3,1},{4,6},{5,7},{6,4},{7,5},{8,10},{9,11},{10,... | collective-permute-start | bytes 786440 | tf_op jit(solution)/shard_map/ppermute | solution.py:335
  15.0 13.7 %collective-permute-done.10.refs_8_.refs_2_ = f32[256,256]{1,0:T(8,128)S(1)} collective-permute-done((f32[256,256]{1,0:T(8,128)S(1)}, f32[256,256]{1,0:T(8,128)S(1)}, u32[]{:S(2)}, u32[]{:S(2)}) %collective-permute-start.10) | collective-permute-done | bytes 262176 | tf_op jit(solution)/shard_map/ppermute | solution.py:335
  28.8 5.4 %collective-permute-done.9.refs_7_.refs_1_ = f32[256,256]{1,0:T(8,128)S(1)} collective-permute-done((f32[256,256]{1,0:T(8,128)S(1)}, f32[256,256]{1,0:T(8,128)S(1)}, u32[]{:S(2)}, u32[]{:S(2)}) %collective-permute-start.9) | collective-permute-done | bytes 262176 | tf_op jit(solution)/shard_map/ppermute | solution.py:335
  34.2 0.3 collective-permute-done.8.refs_6_.refs_0_
  34.5 3.9 %schedule.1 = (f32[32,3,8,256]{3,2,1,0:T(8,128)}, s32[32,128]{1,0:T(8,128)}, s32[32,128]{1,0:T(8,128)S(1)}, s32[1]{0:T(128)}) custom-call(f32[32,8,896]{2,1,0:T(8,128)S(1)} %all-to-all-done.3.got_ref, bf16[128,640]{1,0:T(8,128)(2,1)S(1)} %copy-done.8, bf16[96,128]{1,0:T(8,128)(2,1)} %constant.63.clone.refs_1_, bf16[128,128]{1,0:T(8,128)(2,1)S(1)} %copy-done.10, ...), custom_call_target="tpu_custom_call" | custom-call | tf_op jit(solution)/shard_map/schedule/pallas_call | solution.py:390
  38.5 4.6 %all-to-all-start.4 = ((f32[32,3,8,256]{3,2,1,0:T(8,128)}), f32[32,3,8,256]{3,2,1,0:T(8,128)S(1)}, u32[]{:S(2)}, u32[]{:S(2)}) async-start(f32[32,3,8,256]{3,2,1,0:T(8,128)} %get-tuple-element.268), calls=%async_computation.4 | async-start | bytes 1572864 | tf_op jit(solution)/shard_map/all_to_all | solution.py:327
  43.1 0.9 %stage_needed.3 = (f32[256,256]{1,0:T(8,128)S(1)}, f32[256,256]{1,0:T(8,128)S(1)}, f32[256,256]{1,0:T(8,128)S(1)}) custom-call(s32[32,128]{1,0:T(8,128)S(1)} %get-tuple-element.267.left, f32[2,4,256,256]{3,2,1,0:T(8,128)} %a_hbm.5), custom_call_target="tpu_custom_call" | custom-call | tf_op jit(solution)/shard_map/stage_needed/pallas_call | solution.py:338
  44.1 1.8 %collective-permute-start.11 = (f32[256,256]{1,0:T(8,128)S(1)}, f32[256,256]{1,0:T(8,128)S(1)}, u32[]{:S(2)}, u32[]{:S(2)}) collective-permute-start(f32[256,256]{1,0:T(8,128)S(1)} %get-tuple-element.269), channel_id=1, source_target_pairs={{0,2},{1,3},{2,0},{3,1},{4,6},{5,7},{6,4},{7,5},{8,10},{9,11},{10,... | collective-permute-start | bytes 786440 | tf_op jit(solution)/shard_map/ppermute | solution.py:335
  45.9 1.5 %collective-permute-start.12 = (f32[256,256]{1,0:T(8,128)S(1)}, f32[256,256]{1,0:T(8,128)S(1)}, u32[]{:S(2)}, u32[]{:S(2)}) collective-permute-start(f32[256,256]{1,0:T(8,128)S(1)} %get-tuple-element.270), channel_id=1, source_target_pairs={{0,1},{1,0},{2,3},{3,2},{4,5},{5,4},{6,7},{7,6},{8,9},{9,8},{10,11... | collective-permute-start | bytes 786440 | tf_op jit(solution)/shard_map/ppermute | solution.py:335
  47.4 0.3 collective-permute-start.13
  47.6 11.8 %collective-permute-done.11.refs_3_ = f32[256,256]{1,0:T(8,128)S(1)} collective-permute-done((f32[256,256]{1,0:T(8,128)S(1)}, f32[256,256]{1,0:T(8,128)S(1)}, u32[]{:S(2)}, u32[]{:S(2)}) %collective-permute-start.11) | collective-permute-done | bytes 262176 | tf_op jit(solution)/shard_map/ppermute | solution.py:335
  59.4 7.1 %collective-permute-done.13.refs_5_ = f32[256,256]{1,0:T(8,128)S(1)} collective-permute-done((f32[256,256]{1,0:T(8,128)S(1)}, f32[256,256]{1,0:T(8,128)S(1)}, u32[]{:S(2)}, u32[]{:S(2)}) %collective-permute-start.13) | collective-permute-done | bytes 262176 | tf_op jit(solution)/shard_map/ppermute | solution.py:335
  67.2 1.6 %collective-permute-done.14.theirs = f32[32,3,8,256]{3,2,1,0:T(8,128)S(1)} collective-permute-done((f32[32,3,8,256]{3,2,1,0:T(8,128)S(1)}, f32[32,3,8,256]{3,2,1,0:T(8,128)S(1)}, u32[]{:S(2)}, u32[]{:S(2)}) %collective-permute-start.14) | collective-permute-done | bytes 786464 | tf_op jit(solution)/shard_map/ppermute | solution.py:348
  68.8 3.3 %multiply.5 = f32[1,4,256,256]{3,2,1,0:T(8,128)} custom-call(s32[1]{0:T(128)} %get-tuple-element.265.turn, s32[32,128]{1,0:T(8,128)} %get-tuple-element.266.table, s32[32,128]{1,0:T(8,128)S(1)} %get-tuple-element.267.left, f32[32,3,8,256]{3,2,1,0:T(8,128)S(1)} %all-to-all-done.4.mine, f32[32,3,8,256]{3,2,1,0:T(8,128)S(1)} %collective-permute-done.14.theirs, ...), custom_call_target="tpu_custom_call" | custom-call | tf_op jit(solution)/shard_map/multiply/pallas_call | solution.py:352
  72.1 0.2 conditional.1
  (7 shorter events, 0.0 us)
Async XLA Ops:
  2.0 32.6 %copy-start.8 = (bf16[128,640]{1,0:T(8,128)(2,1)S(1)}, bf16[128,640]{1,0:T(8,128)(2,1)}, u32[]{:S(2)}) copy-start(bf16[128,640]{1,0:T(8,128)(2,1)} %constant.62.clone.refs_0_) | copy-start | bytes 491524
  2.0 32.5 %copy-start.9 = (bf16[128,256]{1,0:T(8,128)(2,1)S(1)}, bf16[128,256]{1,0:T(8,128)(2,1)}, u32[]{:S(2)}) copy-start(bf16[128,256]{1,0:T(8,128)(2,1)} %constant.65.clone.refs_3_) | copy-start | bytes 196612
  2.0 32.5 %copy-start.10 = (bf16[128,128]{1,0:T(8,128)(2,1)S(1)}, bf16[128,128]{1,0:T(8,128)(2,1)}, u32[]{:S(2)}) copy-start(bf16[128,128]{1,0:T(8,128)(2,1)} %constant.64.clone.refs_2_) | copy-start | bytes 98308
  2.0 32.5 %all-to-all-start.3 = ((f32[32,8,896]{2,1,0:T(8,128)}), f32[32,8,896]{2,1,0:T(8,128)S(1)}, u32[]{:S(2)}, u32[]{:S(2)}) async-start(f32[32,8,896]{2,1,0:T(8,128)} %prepare.1), calls=%async_computation.3 | async-start | bytes 1835008 | tf_op jit(solution)/shard_map/all_to_all | solution.py:327
  11.5 17.3 %collective-permute-start.10 = (f32[256,256]{1,0:T(8,128)S(1)}, f32[256,256]{1,0:T(8,128)S(1)}, u32[]{:S(2)}, u32[]{:S(2)}) collective-permute-start(f32[256,256]{1,0:T(8,128)S(1)} %get-tuple-element.264), channel_id=1, source_target_pairs={{0,3},{1,2},{2,1},{3,0},{4,7},{5,6},{6,5},{7,4},{8,11},{9,10},{10,... | collective-permute-start | bytes 786440 | tf_op jit(solution)/shard_map/ppermute | solution.py:335
  13.2 20.9 %collective-permute-start.9 = (f32[256,256]{1,0:T(8,128)S(1)}, f32[256,256]{1,0:T(8,128)S(1)}, u32[]{:S(2)}, u32[]{:S(2)}) collective-permute-start(f32[256,256]{1,0:T(8,128)S(1)} %get-tuple-element.264), channel_id=1, source_target_pairs={{0,1},{1,0},{2,3},{3,2},{4,5},{5,4},{6,7},{7,6},{8,9},{9,8},{10,11... | collective-permute-start | bytes 786440 | tf_op jit(solution)/shard_map/ppermute | solution.py:335
  13.8 20.7 %collective-permute-start.8 = (f32[256,256]{1,0:T(8,128)S(1)}, f32[256,256]{1,0:T(8,128)S(1)}, u32[]{:S(2)}, u32[]{:S(2)}) collective-permute-start(f32[256,256]{1,0:T(8,128)S(1)} %get-tuple-element.263), channel_id=1, source_target_pairs={{0,2},{1,3},{2,0},{3,1},{4,6},{5,7},{6,4},{7,5},{8,10},{9,11},{10,... | collective-permute-start | bytes 786440 | tf_op jit(solution)/shard_map/ppermute | solution.py:335
  38.5 28.1 %all-to-all-start.4 = ((f32[32,3,8,256]{3,2,1,0:T(8,128)}), f32[32,3,8,256]{3,2,1,0:T(8,128)S(1)}, u32[]{:S(2)}, u32[]{:S(2)}) async-start(f32[32,3,8,256]{3,2,1,0:T(8,128)} %get-tuple-element.268), calls=%async_computation.4 | async-start | bytes 1572864 | tf_op jit(solution)/shard_map/all_to_all | solution.py:327
  44.1 15.3 %collective-permute-start.11 = (f32[256,256]{1,0:T(8,128)S(1)}, f32[256,256]{1,0:T(8,128)S(1)}, u32[]{:S(2)}, u32[]{:S(2)}) collective-permute-start(f32[256,256]{1,0:T(8,128)S(1)} %get-tuple-element.269), channel_id=1, source_target_pairs={{0,2},{1,3},{2,0},{3,1},{4,6},{5,7},{6,4},{7,5},{8,10},{9,11},{10,... | collective-permute-start | bytes 786440 | tf_op jit(solution)/shard_map/ppermute | solution.py:335
  45.9 13.5 %collective-permute-start.12 = (f32[256,256]{1,0:T(8,128)S(1)}, f32[256,256]{1,0:T(8,128)S(1)}, u32[]{:S(2)}, u32[]{:S(2)}) collective-permute-start(f32[256,256]{1,0:T(8,128)S(1)} %get-tuple-element.270), channel_id=1, source_target_pairs={{0,1},{1,0},{2,3},{3,2},{4,5},{5,4},{6,7},{7,6},{8,9},{9,8},{10,11... | collective-permute-start | bytes 786440 | tf_op jit(solution)/shard_map/ppermute | solution.py:335
  47.4 19.2 %collective-permute-start.13 = (f32[256,256]{1,0:T(8,128)S(1)}, f32[256,256]{1,0:T(8,128)S(1)}, u32[]{:S(2)}, u32[]{:S(2)}) collective-permute-start(f32[256,256]{1,0:T(8,128)S(1)} %get-tuple-element.271), channel_id=1, source_target_pairs={{0,3},{1,2},{2,1},{3,0},{4,7},{5,6},{6,5},{7,4},{8,11},{9,10},{10,... | collective-permute-start | bytes 786440 | tf_op jit(solution)/shard_map/ppermute | solution.py:335
  66.5 2.3 %collective-permute-start.14 = (f32[32,3,8,256]{3,2,1,0:T(8,128)S(1)}, f32[32,3,8,256]{3,2,1,0:T(8,128)S(1)}, u32[]{:S(2)}, u32[]{:S(2)}) collective-permute-start(f32[32,3,8,256]{3,2,1,0:T(8,128)S(1)} %all-to-all-done.4.mine), channel_id=1, source_target_pairs={{0,4},{4,0},{8,12},{12,8},{16,20},{20,16},{24,28},{28,24},{1,5},{5... | collective-permute-start | bytes 2359304 | tf_op jit(solution)/shard_map/ppermute | solution.py:348

commit v3 on v2

v3 whole, which is shorter than its diff:
```python
import functools

import jax
import jax.numpy as jnp
import numpy as np
from jax import lax
from jax.experimental import pallas as pl
from jax.experimental.pallas import tpu as pltpu
from jax.sharding import PartitionSpec as P

LANES = 128
F32 = jnp.float32
BF16 = jnp.bfloat16
I32 = jnp.int32
SMEM = pl.BlockSpec(memory_space=pltpu.SMEM)
VMEM = pl.BlockSpec(memory_space=pltpu.VMEM)
HBM = pl.BlockSpec(memory_space=pltpu.HBM)
DMA = pltpu.SemaphoreType.DMA
PARAMS = pltpu.CompilerParams(vmem_limit_bytes=48 * 1024 * 1024)


class Plan:
    def __init__(self, mesh, a_blocks, b_blocks):
        self.nrow, self.ncol, self.ndep = (mesh.shape[name] for name in ("row", "col", "depth"))
        self.rows, self.kc, self.bs, _ = a_blocks.shape
        self.kb, self.nc, _, _ = b_blocks.shape
        assert self.kb == 1 and self.rows == self.ndep and self.nrow % 2 == 0
        every = self.nrow * self.ncol * self.ndep
        self.whole = self.bs // every >= 8
        self.axes = ("row", "col", "depth") if self.whole else ("row", "depth")
        self.G = every if self.whole else self.nrow * self.ndep
        self.stride = self.G // self.nrow
        self.R = self.bs // self.G
        self.Q = self.G * self.nc
        self.W = self.kc if self.whole else self.kc * self.ncol
        self.nk = self.kc * self.ncol * self.ndep
        self.J = 3 * self.nk // 16
        self.slots = self.nc - 1 if self.whole else self.nc
        self.waves = 2 if self.whole else self.kc
        assert self.G & (self.G - 1) == 0 and self.nc & (self.nc - 1) == 0
        self.g_bits, self.q_bits = self.G.bit_length() - 1, self.Q.bit_length() - 1
        self.others = [(dd, dc) for dd in range(self.ndep) for dc in range(self.ncol) if (dd, dc) != (0, 0)]

    def member(self, value):
        return (value >> 2) & (self.G - 1)

    def column(self, value):
        return (value >> (2 + self.g_bits)) & (self.nc - 1)

    def slot(self, value):
        return value >> (2 + self.q_bits)

    def listed(self, rows, p, member):
        per = LANES // self.G
        return rows[p // per, p % per * self.G + member]

    def decode(self, s):
        if self.whole:
            return s // (self.ncol * self.ndep), s // self.ndep % self.ncol, s % self.ndep
        return s // self.ndep, s * 0, s % self.ndep

    def tables(self):
        q = np.arange(self.Q)[None, :]
        s = np.arange(self.G)[:, None]
        e = np.arange(LANES)[:, None]
        row_q, col_q, dep_q = self.decode(q % self.G)
        c_q = q // self.G
        row_s, col_s, dep_s = self.decode(s)
        row_t, col_t, dep_t = self.decode(s.T)
        b0 = self.rows * self.W
        select = [e == rr * self.W + row_q % self.W for rr in range(self.rows)]
        select += [e == b0 + c_q, e == b0 + self.nc + c_q, (e >= b0) & (e < b0 + c_q)]
        holds = (dep_s == dep_q) & (col_s == row_q // self.W)
        masks = [holds, s == q % self.G, col_s == col_q]
        before = np.arange(self.Q)[:, None] < q
        k = np.arange(LANES)[None, :]
        inner = (dep_q * self.nrow + row_q).T == k
        first = inner & (c_q.T == 0) & (col_q.T == 0)
        chunk = (k.T < k) & (k.T // self.kc == k // self.kc) & (k < self.nk)
        pick = [(row_s == row_t) & (dep_s == rr) for rr in range(self.rows)]
        pick += [(row_s ^ 1 == row_t) & (col_s == col_t) & (dep_s == dep_t)]
        groups = [np.concatenate(select, 1), np.concatenate(masks, 0), before, np.concatenate(pick, 1)]
        far = (k // self.kc != dep_s * self.ncol + col_s) | (not self.whole)
        groups += [np.concatenate([inner, first], 1), np.concatenate([chunk, far], 0)]
        return [jnp.asarray(t.astype(np.float32), BF16) for t in groups]


def dot(x, y):
    return jnp.dot(x.astype(BF16), y.astype(BF16), preferred_element_type=F32)


def dot_high(x, y):
    x_high, y_high = x.astype(BF16), y.astype(BF16)
    x_low, y_low = (x - x_high.astype(F32)).astype(BF16), (y - y_high.astype(F32)).astype(BF16)
    return dot(x_high, y_low) + dot(x_low, y_high) + dot(x_high, y_high)


def entry_row(plan, entries):
    row = entries[0:1]
    for r in range(1, plan.rows):
        row += pltpu.roll(entries[r : r + 1], r * plan.W, 1)
    return row


def entry(row, place):
    lane = lax.broadcasted_iota(I32, row.shape, 1)
    return jnp.sum(jnp.where(lane == place, row, 0)) != 0


def prepare(plan, entries, b_hbm, out_ref, sems):
    def piece(c, j):
        return pltpu.make_async_copy(b_hbm.at[c], out_ref.at[:, :, pl.ds(j * plan.bs, plan.bs)], sems.at[j])

    row = entry_row(plan, entries)
    count = jnp.int32(0)
    for c in range(plan.nc):
        stored = entry(row, plan.rows * plan.W + c)
        for j in range(min(c + 1, plan.slots)):

            @pl.when(stored & (count == j))
            def _(c=c, j=j):
                piece(c, j).start()

        count += stored.astype(I32)

    tile = jnp.broadcast_to(row.astype(F32)[None], (plan.G, plan.R, LANES))
    out_ref[:, :, plan.slots * plan.bs :] = tile
    for j in range(plan.slots):

        @pl.when(count > j)
        def _(j=j):
            piece(0, j).wait()


def stage(plan, wave, entries, a_hbm, *refs):
    outs, sems = refs[:-1], refs[-1]
    col, dep = lax.axis_index("col"), lax.axis_index("depth")
    row = entry_row(plan, entries)
    start = 0 if plan.whole else col * plan.kc
    stored = [[entry(row, r * plan.W + start + kk) for kk in range(plan.kc)] for r in range(plan.rows)]

    def each(act):
        for r in range(plan.rows):
            count = jnp.int32(0)
            for kk in range(plan.kc):
                for dd, out in enumerate(outs):

                    @pl.when(stored[r][kk] & (count == wave) & ((dep + dd) % plan.ndep == r))
                    def _(r=r, kk=kk, out=out):
                        act(pltpu.make_async_copy(a_hbm.at[r, kk], out, sems.at[r]))

                count += stored[r][kk].astype(I32)

    each(lambda copy: copy.start())
    each(lambda copy: copy.wait())


def needs(plan, tile, wide, masks, before, pick):
    G, Q, rows = plan.G, plan.Q, plan.rows
    entries = dot(tile, wide[...])
    holds, own, same_col = masks[0:G], masks[G : 2 * G], masks[2 * G : 3 * G]
    stored_a = jnp.zeros((G, Q), F32)
    for rr in range(rows):
        stored_a += dot(pick[:, rr * G : (rr + 1) * G], entries[:, rr * Q : (rr + 1) * Q] * holds)
    b0 = rows * Q
    stored_b = jnp.sum(entries[:, b0 : b0 + Q] * own, axis=0, keepdims=True)
    slot = jnp.sum(entries[:, b0 + 2 * Q : b0 + 3 * Q] * own, axis=0, keepdims=True)
    need = stored_a * stored_b * entries[:, b0 + Q : b0 + 2 * Q] * same_col
    partner = dot(pick[:, rows * G :], need)
    both = jnp.maximum(need, partner)
    return need, partner, both, dot(both, before[...]), slot, stored_a


def list_blocks(plan, base, need, partner, both, rank, slot, out):
    G, Q, per = plan.G, plan.Q, LANES // plan.G
    q = lax.broadcasted_iota(I32, (1, Q), 1).astype(F32)
    value = 4.0 * both * (slot * float(Q) + q) + 2.0 * partner + need
    member = lax.broadcasted_iota(I32, (G, LANES), 0)
    lane = lax.broadcasted_iota(I32, (G, LANES), 1)
    turn = rank - ((member[:, :1] >> (plan.stride.bit_length() - 1)) & 1).astype(F32) - base
    for n in range(out.shape[0]):
        row = jnp.zeros((G, LANES), F32)
        for p in range(n * per, min((n + 1) * per, plan.J)):
            at = jnp.sum(jnp.where(turn == 2.0 * p, value, 0.0), axis=1, keepdims=True)
            row = jnp.where(lane == p % per * G + member, at, row)
        out[n : n + 1] = jnp.sum(row, axis=0, keepdims=True).astype(I32)


def fill(plan, again, rows, got_ref, out_ref):
    for p in range(plan.J):

        def body(d, carry, p=p):
            value = plan.listed(rows, p, d)
            slot = plan.column(value) if again else plan.slot(value)
            start = pl.multiple_of(slot * plan.bs, plan.bs)
            out_ref[d, p] = got_ref[plan.member(value), :, pl.ds(start, plan.bs)]
            return carry

        lax.fori_loop(0, plan.G, body, 0, unroll=8)


def schedule(plan, again, turn, tile_ref, got_ref, *refs):
    tables, (out_ref, rows_ref, scratch, sem) = refs[:4], refs[-4:]
    base = (turn[0] * (2 * plan.J)).astype(F32)
    need, partner, both, rank, slot, _ = needs(plan, tile_ref[:, 0, tile_ref.shape[2] - LANES :], *tables)
    list_blocks(plan, base, need, partner, both, rank, slot, rows_ref)
    copy = pltpu.make_async_copy(rows_ref, scratch, sem.at[0])
    copy.start()
    copy.wait()
    fill(plan, again, scratch, got_ref, out_ref)


def settle(plan, wave, got_ref, *refs):
    tables, (inner, chunk, a_hbm), refs = refs[:4], refs[4:7], refs[7:]
    outs, (waves_ref, state_ref, zero_hbm, place_ref, place_smem, zero, sems, zero_sems) = refs[:-8], refs[-8:]
    zero[...] = jnp.zeros_like(zero)
    clear = [pltpu.make_async_copy(zero, zero_hbm.at[0, c], zero_sems.at[c]) for c in range(plan.nc)]
    for copy in clear:
        copy.start()
    need, _, both, _, slot, stored_a = needs(plan, got_ref[:, 0, got_ref.shape[2] - LANES :], *tables)
    before, far = chunk[0:LANES], chunk[LANES:]
    left = jnp.minimum(dot(need, inner[:, :LANES]), 1.0)
    place = dot(dot(stored_a, inner[:, LANES:]), before)
    if plan.whole:
        late = jnp.where(place > 0, left, 0.0)
        place = jnp.where(place > 0, jnp.where(late > 0, 1.0 + dot(late, before), -1.0), 0.0)
    place_ref[...] = place.astype(I32)
    fetch = pltpu.make_async_copy(place_ref, place_smem, sems.at[len(outs)])
    fetch.start()
    member = lax.axis_index(plan.axes)
    mine = lax.broadcasted_iota(I32, place.shape, 0) == member
    waves_ref[...] = jnp.sum(jnp.where(mine, place, 0.0), axis=0, keepdims=True).astype(I32)
    rounds = (jnp.max(jnp.sum(both, axis=1, keepdims=True)).astype(I32) + 2 * plan.J - 1) // (2 * plan.J)
    lost = jnp.max(need * jnp.where(slot >= plan.slots, 1.0, 0.0)) > 0
    waves = jnp.max(left * far * (place + 1.0))
    easy = jnp.where(lost, 3, jnp.where(rounds > 1, 1, 0))
    hard = jnp.where((waves > plan.waves + 1) | (easy > 0), 4, 2)
    state_ref[0] = jnp.where(waves > plan.waves, hard, easy)
    state_ref[1] = rounds

    row, col, dep = lax.axis_index("row"), lax.axis_index("col"), lax.axis_index("depth")

    def each(act):
        for o, out in enumerate(outs):
            dd, dc = plan.others[o]
            to_dep, to_col = (dep + dd) % plan.ndep, (col + dc) % plan.ncol
            to = (row * plan.ncol + to_col) * plan.ndep + to_dep
            for kk in range(plan.kc):

                @pl.when(place_smem[to, dep * plan.nrow + col * plan.kc + kk] == wave)
                def _(o=o, kk=kk, out=out, to_dep=to_dep):
                    act(pltpu.make_async_copy(a_hbm.at[to_dep, kk], out, sems.at[o]))

    fetch.wait()
    each(lambda copy: copy.start())
    each(lambda copy: copy.wait())
    for copy in clear:
        copy.wait()


def multiply(plan, raw, waves, first, rows, left, mine, theirs, a_hbm, *refs):
    lefts, refs = refs[: waves * len(plan.others)], refs[waves * len(plan.others) :]
    _, out_hbm, a_scr, right, total, sems, out_sems = refs
    col, dep = lax.axis_index("col"), lax.axis_index("depth")
    member = lax.axis_index(plan.axes)
    listed = [plan.listed(rows, p, member) for p in range(plan.J)]
    listed += [plan.listed(rows, p, member ^ plan.stride) >> 1 << 1 for p in range(plan.J)]
    asked = [value & 1 for value in listed[: plan.J]] + [(value >> 1) & 1 for value in listed[plan.J :]]

    def copy(src, j):
        return pltpu.make_async_copy(src, a_scr.at[j], sems.at[j])

    ready = []
    for j, value in enumerate(listed):
        row_s, _, dep_s = plan.decode(plan.member(value))
        dd = (dep - dep_s + plan.ndep) % plan.ndep
        dc = (col - row_s // plan.kc + plan.ncol) % plan.ncol
        kk = row_s % plan.kc
        near = (dd == 0) & (dc == 0)
        wave = jnp.int32(0) if raw else left[0, dep_s * plan.nrow + row_s]
        ready.append((asked[j] == 1) & (near | (wave < waves)))

        @pl.when(ready[j])
        def _(j=j, kk=kk, dd=dd, dc=dc, near=near, wave=wave):
            @pl.when(near)
            def _():
                copy(a_hbm.at[dep, kk], j).start()

            for n, (xd, xc) in enumerate(plan.others):
                for w in range(waves):

                    @pl.when((dd == xd) & (dc == xc) & (wave == w))
                    def _(n=n, w=w):
                        src = lefts[w * len(plan.others) + n]
                        copy(src.at[kk] if raw else src, j).start()

    def block(c):
        return pltpu.make_async_copy(total.at[c], out_hbm.at[0, c], out_sems.at[c])

    column = [plan.column(value) for value in listed]
    touched = [functools.reduce(jnp.logical_or, [r & (x == c) for r, x in zip(ready, column)]) for c in range(plan.nc)]
    for c in range(plan.nc):

        @pl.when(touched[c])
        def _(c=c):
            if first:
                total[c] = jnp.zeros((plan.bs, plan.bs), F32)
            else:
                begin = pltpu.make_async_copy(out_hbm.at[0, c], total.at[c], out_sems.at[c])
                begin.start()
                begin.wait()

    for j in range(2 * plan.J):

        @pl.when(ready[j])
        def _(j=j):
            source = mine if j < plan.J else theirs
            right[...] = source[:, j % plan.J].reshape(plan.bs, plan.bs)
            copy(a_hbm.at[0, 0], j).wait()
            total[column[j]] += dot_high(a_scr[j], right[...])

    for act in (lambda copy: copy.start(), lambda copy: copy.wait()):
        for c in range(plan.nc):
            pl.when(touched[c])(lambda c=c, act=act: act(block(c)))


def call(kernel, out_shape, in_specs, out_specs, scratch=(), **kwargs):
    return pl.pallas_call(
        kernel,
        out_shape=out_shape,
        in_specs=in_specs,
        out_specs=out_specs,
        scratch_shapes=scratch,
        compiler_params=PARAMS,
        name=kernel.func.__name__,
        **kwargs,
    )


def local(mesh, a_blocks, a_pattern, b_blocks, b_pattern, c_pattern):
    plan = Plan(mesh, a_blocks, b_blocks)
    G, R, J, bs, nc = plan.G, plan.R, plan.J, plan.bs, plan.nc
    result = jax.ShapeDtypeStruct((1, nc, bs, bs), F32)
    block = jax.ShapeDtypeStruct((bs, bs), F32)
    listing = (-(-J * G // LANES), LANES)

    def exchange(pieces):
        return lax.all_to_all(pieces, plan.axes, 0, 0, tiled=True)

    def shift(staged):
        def perm(dd, dc):
            for x in range(plan.ncol):
                for y in range(plan.ndep):
                    yield x * plan.ndep + y, (x + dc) % plan.ncol * plan.ndep + (y + dd) % plan.ndep

        return [lax.ppermute(x, ("col", "depth"), list(perm(*by))) for x, by in zip(staged, plan.others)]

    def swap(mine):
        return lax.ppermute(mine, "row", [(i, i ^ 1) for i in range(plan.nrow)])

    def listed(again, turn, got, pieces):
        send, rows = call(
            functools.partial(schedule, plan, again),
            (jax.ShapeDtypeStruct((G, J, R, bs), F32), jax.ShapeDtypeStruct(listing, I32)),
            [SMEM] + [VMEM] * 6,
            (VMEM, VMEM),
            [pltpu.SMEM(listing, I32), DMA((1,))],
        )(jnp.reshape(turn, (1,)), got, pieces, *tables[:4])
        return rows, lax.all_to_all(send, plan.axes, 0, 0, tiled=True)

    def settled(wave, got, a_blocks):
        count = len(plan.others) if plan.whole else 0
        *late, waves, state, zero = call(
            functools.partial(settle, plan, wave),
            (block,) * count
            + (jax.ShapeDtypeStruct((1, LANES), I32), jax.ShapeDtypeStruct((2,), I32), result),
            [VMEM] * 7 + [HBM],
            (VMEM,) * count + (VMEM, SMEM, HBM),
            [
                pltpu.VMEM((G, LANES), I32),
                pltpu.SMEM((G, LANES), I32),
                pltpu.VMEM((bs, bs), F32),
                DMA((count + 1,)),
                DMA((nc,)),
            ],
        )(got, *tables, a_blocks)
        return shift(late), waves, state, zero

    def product(raw, first, rows, waves, mine, theirs, a_blocks, lefts, start):
        return call(
            functools.partial(multiply, plan, raw, len(lefts) // len(plan.others), first),
            result,
            [SMEM, SMEM, VMEM, VMEM] + [HBM] * (2 + len(lefts)),
            HBM,
            [
                pltpu.VMEM((2 * J, bs, bs), F32),
                pltpu.VMEM((bs, bs), F32),
                pltpu.VMEM((nc, bs, bs), F32),
                DMA((2 * J,)),
                DMA((nc,)),
            ],
            input_output_aliases={5 + len(lefts): 0},
        )(rows, waves, mine, theirs, a_blocks, *lefts, start)

    if not plan.whole:
        a_pattern = lax.all_gather(a_pattern, "col", axis=1, tiled=True)
    b0 = plan.rows * plan.W
    entries = jnp.pad(b_pattern, ((0, plan.rows - 1), (b0, LANES - b0 - nc)))
    entries += jnp.pad(c_pattern, ((0, plan.rows - 1), (b0 + nc, LANES - b0 - 2 * nc)))
    entries += jnp.pad(a_pattern, ((0, 0), (0, LANES - plan.W)))

    b_pieces = b_blocks.reshape(nc, G, R, bs)
    width = plan.slots * bs + LANES
    pieces = call(
        functools.partial(prepare, plan),
        jax.ShapeDtypeStruct((G, R, width), F32),
        [VMEM, HBM],
        VMEM,
        [DMA((plan.slots,))],
    )(entries, b_pieces)
    got = exchange(pieces)
    lefts = []
    for wave in range(1 if plan.whole else plan.waves):
        staged = call(
            functools.partial(stage, plan, wave),
            (block,) * plan.ndep,
            [VMEM, HBM],
            (VMEM,) * plan.ndep,
            [DMA((plan.rows,))],
        )(entries, a_blocks)
        lefts += shift([staged[dd] for dd, _ in plan.others])

    tables = plan.tables()
    got, lefts = lax.optimization_barrier((got, lefts))
    rows, mine = listed(False, jnp.int32(0), got, got)
    late, waves, state, zero = settled(1, got, a_blocks)
    mine, late, zero = lax.optimization_barrier((mine, late, zero))
    lefts = lefts + late
    theirs = swap(mine)
    c_blocks = product(False, True, rows, waves, mine, theirs, a_blocks, lefts, zero)

    def rounds(raw, again, got, pieces, state, waves, a_blocks, lefts, begin, c_blocks):
        total = state[1] if plan.whole else lax.pmax(state[1], "col")

        def body(turn, c_blocks):
            rows, mine = listed(again, turn, got, pieces)
            return product(raw, False, rows, waves, mine, swap(mine), a_blocks, lefts, c_blocks)

        return lax.fori_loop(begin, total, body, c_blocks)

    def spread_again(b_pieces):
        return exchange(b_pieces.transpose(1, 2, 0, 3).reshape(G, R, nc * bs))

    def done(c_blocks, *_):
        return c_blocks

    def more_rounds(c_blocks, rows, mine, theirs, got, state, waves, a_blocks, b_pieces, *lefts):
        return rounds(False, False, got, got, state, waves, a_blocks, lefts, 1, c_blocks)

    def more_waves(c_blocks, rows, mine, theirs, got, state, waves, a_blocks, b_pieces, *lefts):
        lefts += tuple(settled(2, got, a_blocks)[0])
        return product(False, True, rows, waves, mine, theirs, a_blocks, lefts, c_blocks)

    def more_pieces(c_blocks, rows, mine, theirs, got, state, waves, a_blocks, b_pieces, *lefts):
        pieces, c_blocks = spread_again(b_pieces), jnp.zeros_like(c_blocks)
        return rounds(False, True, got, pieces, state, waves, a_blocks, lefts, 0, c_blocks)

    def anew(c_blocks, rows, mine, theirs, got, state, waves, a_blocks, b_pieces, *lefts):
        pieces, c_blocks = spread_again(b_pieces), jnp.zeros_like(c_blocks)
        dep = lax.axis_index("depth")
        raw = [lax.dynamic_index_in_dim(a_blocks, (dep + dd) % plan.ndep, keepdims=False) for dd, _ in plan.others]
        return rounds(True, True, got, pieces, state, waves, a_blocks, shift(raw), 0, c_blocks)

    index = state[0] if plan.whole else lax.pmax(state[0], "col")
    branches = [done, more_rounds, more_waves, more_pieces, anew]
    return lax.switch(index, branches, c_blocks, rows, mine, theirs, got, state, waves, a_blocks, b_pieces, *lefts)


def solution(mesh):
    in_specs = (
        P("row", ("depth", "col"), None, None),
        P("row", ("depth", "col")),
        P(("depth", "row"), "col", None, None),
        P(("depth", "row"), "col"),
        P(("row", "depth"), "col"),
    )
    out_specs = P(("row", "depth"), "col", None, None)
    return jax.shard_map(
        functools.partial(local, mesh), mesh=mesh, in_specs=in_specs, out_specs=out_specs, check_vma=False
    )
```

time: 73.5 us -> 70.5 us (0.959)
  starting transfers between devices: 20 us -> 18.3 us
    all_to_all x2 -> x1, starting transfers between devices: 12.9 us -> 6.83 us  [exchange(): return lax.all_to_all(pieces, plan.axes, 0, 0, tiled=True)]
    all_to_all x0 -> x1, starting transfers between devices: none -> 3.67 us  [listed(): return (rows, lax.all_to_all(send, plan.axes, 0, 0, tiled=True))]
    ppermute x6, waiting for transfers between devices: 38.4 us -> 37.4 us  [shift(): lax.ppermute(x, ('col', 'depth'), list(perm(*by)))]
    pallas_call x1, Pallas kernels: 1.17 us -> 2.1 us  [local(): call(functools.partial(prepare, plan), jax.ShapeDtypeStruct((G, R, width)...]
    pallas_call x4, Pallas kernels: 9.41 us -> 8.57 us  [the longest x1 2.7 us: product(): call(functools.partial(multiply, plan, raw, len(lefts) // len(plan.others...]
  transfers between devices with their start and end apart: 9 -> 9, of which waited for: 6 -> 6; matrix products, arithmetic and copies ran while one was open for 0% -> 0% of each run, Pallas kernels for 3% -> 5%
where the time goes in v3:
time: 70.5 us; the launch traced here: 70.1 us
  waiting for transfers between devices  39.7 us (56%)
  starting transfers between devices  18.3 us (26%)
  Pallas kernels  10.7 us (15%)
  other arithmetic  0.77 us (1%)
    ppermute x6, waiting for transfers between devices, shift(): lax.ppermute(x, ('col', 'depth'), list(perm(*by)))  37.4 us
    ppermute x6, starting transfers between devices, shift(): lax.ppermute(x, ('col', 'depth'), list(perm(*by)))  7.81 us
    all_to_all x1, starting transfers between devices, exchange(): return lax.all_to_all(pieces, plan.axes, 0, 0, tiled=True)  6.83 us
    all_to_all x1, starting transfers between devices, listed(): return (rows, lax.all_to_all(send, plan.axes, 0, 0, tiled=True))  3.67 us
    pallas_call x1, Pallas kernels, product(): call(functools.partial(multiply, plan, raw, len(lefts) // len(plan.others...  2.7 us
    pallas_call x1, Pallas kernels, listed(): call(functools.partial(schedule, plan, again), (jax.ShapeDtypeStruct((G,...  2.4 us
    ppermute x1, waiting for transfers between devices, swap(): return lax.ppermute(mine, 'row', [(i, i ^ 1) for i in range(plan.nrow)])  2.24 us
    pallas_call x1, Pallas kernels, settled(): call(functools.partial(settle, plan, wave), (block,) * count + (jax.Shape...  2.22 us
  transfers between devices with their start and end apart: 9, of which 6 were waited for; matrix products, arithmetic and copies ran while one was open for 0% of the time, Pallas kernels for 5%

profile of v3, /device:TPU:0, one launch (start us, length us, event | category | flops | bytes accessed | tf_op | source)
XLA Modules:
  0.0 70.1 jit_solution(8240680081379690224)
XLA Ops:
  0.0 0.8 %pad_add_fusion.entries = s32[2,128]{1,0:T(2,128)S(1)} fusion(s32[2,4]{1,0:T(2,128)} %param.23, s32[1,4]{1,0:T(1,128)} %param.26, s32[1,4]{1,0:T(1,128)} %param.25), kind=kLoop, calls=%fused_computation.2 | loop fusion | flops 512 | bytes 1088 | tf_op jit(solution)/shard_map/add | solution.py:410
  0.8 2.1 %prepare.1 = f32[32,8,896]{2,1,0:T(8,128)} custom-call(s32[2,128]{1,0:T(2,128)S(1)} %pad_add_fusion.entries, f32[4,32,8,256]{3,2,1,0:T(8,128)} %bitcast.25), custom_call_target="tpu_custom_call" | custom-call | tf_op jit(solution)/shard_map/prepare/pallas_call | solution.py:414
  2.9 0.0 copy-start
  2.9 0.0 copy-start.1
  2.9 0.0 copy-start.3
  2.9 6.8 %all-to-all-start.5 = ((f32[32,8,896]{2,1,0:T(8,128)}), f32[32,8,896]{2,1,0:T(8,128)S(1)}, u32[]{:S(2)}, u32[]{:S(2)}) async-start(f32[32,8,896]{2,1,0:T(8,128)} %prepare.1), calls=%async_computation.5 | async-start | bytes 1835008 | tf_op jit(solution)/shard_map/all_to_all | solution.py:348
  9.8 1.2 %stage.1 = (f32[256,256]{1,0:T(8,128)S(1)}, f32[256,256]{1,0:T(8,128)S(1)}) custom-call(s32[2,128]{1,0:T(2,128)S(1)} %pad_add_fusion.entries, f32[2,4,256,256]{3,2,1,0:T(8,128)} %a_hbm.3), custom_call_target="tpu_custom_call" | custom-call | tf_op jit(solution)/shard_map/stage/pallas_call | solution.py:424
  11.0 1.8 %collective-permute-start.9 = (f32[256,256]{1,0:T(8,128)S(1)}, f32[256,256]{1,0:T(8,128)S(1)}, u32[]{:S(2)}, u32[]{:S(2)}) collective-permute-start(f32[256,256]{1,0:T(8,128)S(1)} %get-tuple-element.458), channel_id=1, source_target_pairs={{0,2},{1,3},{2,0},{3,1},{4,6},{5,7},{6,4},{7,5},{8,10},{9,11},{10,... | collective-permute-start | bytes 786440 | tf_op jit(solution)/shard_map/ppermute | solution.py:356
  12.9 1.4 %collective-permute-start.11 = (f32[256,256]{1,0:T(8,128)S(1)}, f32[256,256]{1,0:T(8,128)S(1)}, u32[]{:S(2)}, u32[]{:S(2)}) collective-permute-start(f32[256,256]{1,0:T(8,128)S(1)} %get-tuple-element.459), channel_id=1, source_target_pairs={{0,3},{1,2},{2,1},{3,0},{4,7},{5,6},{6,5},{7,4},{8,11},{9,10},{10,... | collective-permute-start | bytes 786440 | tf_op jit(solution)/shard_map/ppermute | solution.py:356
  14.3 0.3 collective-permute-start.10
  14.6 12.5 %collective-permute-done.9.refs_0_ = f32[256,256]{1,0:T(8,128)S(1)} collective-permute-done((f32[256,256]{1,0:T(8,128)S(1)}, f32[256,256]{1,0:T(8,128)S(1)}, u32[]{:S(2)}, u32[]{:S(2)}) %collective-permute-start.9) | collective-permute-done | bytes 262176 | tf_op jit(solution)/shard_map/ppermute | solution.py:356
  27.1 7.8 %collective-permute-done.11.refs_2_ = f32[256,256]{1,0:T(8,128)S(1)} collective-permute-done((f32[256,256]{1,0:T(8,128)S(1)}, f32[256,256]{1,0:T(8,128)S(1)}, u32[]{:S(2)}, u32[]{:S(2)}) %collective-permute-start.11) | collective-permute-done | bytes 262176 | tf_op jit(solution)/shard_map/ppermute | solution.py:356
  35.0 2.4 %schedule.4 = (f32[32,3,8,256]{3,2,1,0:T(8,128)}, s32[1,128]{1,0:T(1,128)S(1)}) custom-call(s32[1]{0:T(128)} %constant.64.clone.1.turn, f32[32,8,896]{2,1,0:T(8,128)S(1)} %all-to-all-done.5.got_ref.tile_ref, f32[32,8,896]{2,1,0:T(8,128)S(1)} %all-to-all-done.5.got_ref.tile_ref, bf16[128,640]{1,0:T(8,128)(2,1)S(1)} %copy-done, bf16[96,128]{1,0:T(8,128)(2,1)S(1)} %copy-done.2, ...), custom_call_target="tpu_custom_call" | custom-call | tf_op jit(solution)/shard_map/schedule/pallas_call | solution.py:362
  37.4 3.7 %all-to-all-start.6 = ((f32[32,3,8,256]{3,2,1,0:T(8,128)}), f32[32,3,8,256]{3,2,1,0:T(8,128)S(1)}, u32[]{:S(2)}, u32[]{:S(2)}) async-start(f32[32,3,8,256]{3,2,1,0:T(8,128)} %get-tuple-element.464), calls=%async_computation.6 | async-start | bytes 1572864 | tf_op jit(solution)/shard_map/all_to_all | solution.py:369
  41.1 2.2 %settle.3 = (f32[256,256]{1,0:T(8,128)S(1)}, f32[256,256]{1,0:T(8,128)S(1)}, f32[256,256]{1,0:T(8,128)S(1)}, s32[1,128]{1,0:T(1,128)S(1)}, s32[2]{0:T(128)S(1)}, /*index=5*/f32[1,4,256,256]{3,2,1,0:T(8,128)}) custom-call(f32[32,8,896]{2,1,0:T(8,128)S(1)} %all-to-all-done.5.got_ref.tile_ref, bf16[128,640]{1,0:T(8,128)(2,1)S(1)} %copy-done, ...), custom_call_target="tpu_custom_call" | custom-call | tf_op jit(solution)/shard_map/settle/pallas_call | solution.py:373
  43.3 2.7 %collective-permute-start.12 = (f32[256,256]{1,0:T(8,128)S(1)}, f32[256,256]{1,0:T(8,128)}, u32[]{:S(2)}, u32[]{:S(2)}) collective-permute-start(f32[256,256]{1,0:T(8,128)S(1)} %get-tuple-element.465), channel_id=1, source_target_pairs={{0,2},{1,3},{2,0},{3,1},{4,6},{5,7},{6,4},{7,5},{8,10},{9,11},{10,... | collective-permute-start | bytes 786440 | tf_op jit(solution)/shard_map/ppermute | solution.py:356
  46.0 0.6 collective-permute-start.13
  46.6 1.0 %collective-permute-start.14 = (f32[256,256]{1,0:T(8,128)S(1)}, f32[256,256]{1,0:T(8,128)}, u32[]{:S(2)}, u32[]{:S(2)}) collective-permute-start(f32[256,256]{1,0:T(8,128)S(1)} %get-tuple-element.467), channel_id=1, source_target_pairs={{0,3},{1,2},{2,1},{3,0},{4,7},{5,6},{6,5},{7,4},{8,11},{9,10},{10,... | collective-permute-start | bytes 786440 | tf_op jit(solution)/shard_map/ppermute | solution.py:356
  47.6 9.5 %collective-permute-done.12.refs_3_ = f32[256,256]{1,0:T(8,128)} collective-permute-done((f32[256,256]{1,0:T(8,128)S(1)}, f32[256,256]{1,0:T(8,128)}, u32[]{:S(2)}, u32[]{:S(2)}) %collective-permute-start.12) | collective-permute-done | bytes 262176 | tf_op jit(solution)/shard_map/ppermute | solution.py:356
  57.1 4.7 %collective-permute-done.13.refs_4_ = f32[256,256]{1,0:T(8,128)} collective-permute-done((f32[256,256]{1,0:T(8,128)S(1)}, f32[256,256]{1,0:T(8,128)}, u32[]{:S(2)}, u32[]{:S(2)}) %collective-permute-start.13) | collective-permute-done | bytes 262176 | tf_op jit(solution)/shard_map/ppermute | solution.py:356
  61.8 2.9 %collective-permute-done.14.refs_5_ = f32[256,256]{1,0:T(8,128)} collective-permute-done((f32[256,256]{1,0:T(8,128)S(1)}, f32[256,256]{1,0:T(8,128)}, u32[]{:S(2)}, u32[]{:S(2)}) %collective-permute-start.14) | collective-permute-done | bytes 262176 | tf_op jit(solution)/shard_map/ppermute | solution.py:356
  64.7 2.2 %collective-permute-done.15.theirs = f32[32,3,8,256]{3,2,1,0:T(8,128)S(1)} collective-permute-done((f32[32,3,8,256]{3,2,1,0:T(8,128)S(1)}, f32[32,3,8,256]{3,2,1,0:T(8,128)S(1)}, u32[]{:S(2)}, u32[]{:S(2)}) %collective-permute-start.15) | collective-permute-done | bytes 786464 | tf_op jit(solution)/shard_map/ppermute | solution.py:359
  67.0 2.7 %multiply.6 = f32[1,4,256,256]{3,2,1,0:T(8,128)} custom-call(s32[1,128]{1,0:T(1,128)S(1)} %get-tuple-element.462.rows, s32[1,128]{1,0:T(1,128)S(1)} %get-tuple-element.463.left, f32[32,3,8,256]{3,2,1,0:T(8,128)S(1)} %all-to-all-done.6.mine, f32[32,3,8,256]{3,2,1,0:T(8,128)S(1)} %collective-permute-done.15.theirs, ...), custom_call_target="tpu_custom_call", output_to_operand_aliasing={{}: (11, {})} | custom-call | tf_op jit(solution)/shard_map/multiply/pallas_call | solution.py:390
  69.7 0.2 conditional.1
  (13 shorter events, 0.0 us)
Async XLA Ops:
  2.9 32.1 %copy-start = (bf16[128,640]{1,0:T(8,128)(2,1)S(1)}, bf16[128,640]{1,0:T(8,128)(2,1)}, u32[]{:S(2)}) copy-start(bf16[128,640]{1,0:T(8,128)(2,1)} %constant.67.clone.refs_0_) | copy-start | bytes 491524
  2.9 32.1 %copy-start.1 = (bf16[128,128]{1,0:T(8,128)(2,1)S(1)}, bf16[128,128]{1,0:T(8,128)(2,1)}, u32[]{:S(2)}) copy-start(bf16[128,128]{1,0:T(8,128)(2,1)} %constant.69.clone.refs_2_) | copy-start | bytes 98308
  2.9 32.1 %copy-start.2 = (bf16[96,128]{1,0:T(8,128)(2,1)S(1)}, bf16[96,128]{1,0:T(8,128)(2,1)}, u32[]{:S(2)}) copy-start(bf16[96,128]{1,0:T(8,128)(2,1)} %constant.68.clone.refs_1_) | copy-start | bytes 73732
  2.9 32.1 %copy-start.3 = (bf16[32,96]{1,0:T(8,128)(2,1)S(1)}, bf16[32,96]{1,0:T(8,128)(2,1)}, u32[]{:S(2)}) copy-start(bf16[32,96]{1,0:T(8,128)(2,1)} %constant.70.clone.refs_3_) | copy-start | bytes 18436
  2.9 32.0 %all-to-all-start.5 = ((f32[32,8,896]{2,1,0:T(8,128)}), f32[32,8,896]{2,1,0:T(8,128)S(1)}, u32[]{:S(2)}, u32[]{:S(2)}) async-start(f32[32,8,896]{2,1,0:T(8,128)} %prepare.1), calls=%async_computation.5 | async-start | bytes 1835008 | tf_op jit(solution)/shard_map/all_to_all | solution.py:348
  11.0 30.1 %copy-start.4 = (bf16[128,256]{1,0:T(8,128)(2,1)S(1)}, bf16[128,256]{1,0:T(8,128)(2,1)}, u32[]{:S(2)}) copy-start(bf16[128,256]{1,0:T(8,128)(2,1)} %constant.71.clone.refs_4_) | copy-start | bytes 196612
  11.0 30.0 %copy-start.5 = (bf16[160,128]{1,0:T(8,128)(2,1)S(1)}, bf16[160,128]{1,0:T(8,128)(2,1)}, u32[]{:S(2)}) copy-start(bf16[160,128]{1,0:T(8,128)(2,1)} %constant.72.clone.refs_5_) | copy-start | bytes 122884
  11.0 16.1 %collective-permute-start.9 = (f32[256,256]{1,0:T(8,128)S(1)}, f32[256,256]{1,0:T(8,128)S(1)}, u32[]{:S(2)}, u32[]{:S(2)}) collective-permute-start(f32[256,256]{1,0:T(8,128)S(1)} %get-tuple-element.458), channel_id=1, source_target_pairs={{0,2},{1,3},{2,0},{3,1},{4,6},{5,7},{6,4},{7,5},{8,10},{9,11},{10,... | collective-permute-start | bytes 786440 | tf_op jit(solution)/shard_map/ppermute | solution.py:356
  12.9 22.0 %collective-permute-start.11 = (f32[256,256]{1,0:T(8,128)S(1)}, f32[256,256]{1,0:T(8,128)S(1)}, u32[]{:S(2)}, u32[]{:S(2)}) collective-permute-start(f32[256,256]{1,0:T(8,128)S(1)} %get-tuple-element.459), channel_id=1, source_target_pairs={{0,3},{1,2},{2,1},{3,0},{4,7},{5,6},{6,5},{7,4},{8,11},{9,10},{10,... | collective-permute-start | bytes 786440 | tf_op jit(solution)/shard_map/ppermute | solution.py:356
  14.3 20.7 %collective-permute-start.10 = (f32[256,256]{1,0:T(8,128)S(1)}, f32[256,256]{1,0:T(8,128)S(1)}, u32[]{:S(2)}, u32[]{:S(2)}) collective-permute-start(f32[256,256]{1,0:T(8,128)S(1)} %get-tuple-element.459), channel_id=1, source_target_pairs={{0,1},{1,0},{2,3},{3,2},{4,5},{5,4},{6,7},{7,6},{8,9},{9,8},{10,11... | collective-permute-start | bytes 786440 | tf_op jit(solution)/shard_map/ppermute | solution.py:356
  37.4 27.3 %all-to-all-start.6 = ((f32[32,3,8,256]{3,2,1,0:T(8,128)}), f32[32,3,8,256]{3,2,1,0:T(8,128)S(1)}, u32[]{:S(2)}, u32[]{:S(2)}) async-start(f32[32,3,8,256]{3,2,1,0:T(8,128)} %get-tuple-element.464), calls=%async_computation.6 | async-start | bytes 1572864 | tf_op jit(solution)/shard_map/all_to_all | solution.py:369
  43.3 13.8 %collective-permute-start.12 = (f32[256,256]{1,0:T(8,128)S(1)}, f32[256,256]{1,0:T(8,128)}, u32[]{:S(2)}, u32[]{:S(2)}) collective-permute-start(f32[256,256]{1,0:T(8,128)S(1)} %get-tuple-element.465), channel_id=1, source_target_pairs={{0,2},{1,3},{2,0},{3,1},{4,6},{5,7},{6,4},{7,5},{8,10},{9,11},{10,... | collective-permute-start | bytes 786440 | tf_op jit(solution)/shard_map/ppermute | solution.py:356
  46.0 15.8 %collective-permute-start.13 = (f32[256,256]{1,0:T(8,128)S(1)}, f32[256,256]{1,0:T(8,128)}, u32[]{:S(2)}, u32[]{:S(2)}) collective-permute-start(f32[256,256]{1,0:T(8,128)S(1)} %get-tuple-element.466), channel_id=1, source_target_pairs={{0,1},{1,0},{2,3},{3,2},{4,5},{5,4},{6,7},{7,6},{8,9},{9,8},{10,11... | collective-permute-start | bytes 786440 | tf_op jit(solution)/shard_map/ppermute | solution.py:356
  46.6 18.1 %collective-permute-start.14 = (f32[256,256]{1,0:T(8,128)S(1)}, f32[256,256]{1,0:T(8,128)}, u32[]{:S(2)}, u32[]{:S(2)}) collective-permute-start(f32[256,256]{1,0:T(8,128)S(1)} %get-tuple-element.467), channel_id=1, source_target_pairs={{0,3},{1,2},{2,1},{3,0},{4,7},{5,6},{6,5},{7,4},{8,11},{9,10},{10,... | collective-permute-start | bytes 786440 | tf_op jit(solution)/shard_map/ppermute | solution.py:356
  64.7 2.3 %collective-permute-start.15 = (f32[32,3,8,256]{3,2,1,0:T(8,128)S(1)}, f32[32,3,8,256]{3,2,1,0:T(8,128)S(1)}, u32[]{:S(2)}, u32[]{:S(2)}) collective-permute-start(f32[32,3,8,256]{3,2,1,0:T(8,128)S(1)} %all-to-all-done.6.mine), channel_id=1, source_target_pairs={{0,4},{4,0},{8,12},{12,8},{16,20},{20,16},{24,28},{28,24},{1,5},{5... | collective-permute-start | bytes 2359304 | tf_op jit(solution)/shard_map/ppermute | solution.py:359

commit v4 on v3

--- a/solution.py
+++ b/solution.py
@@ -16,7 +16,7 @@
 VMEM = pl.BlockSpec(memory_space=pltpu.VMEM)
 HBM = pl.BlockSpec(memory_space=pltpu.HBM)
 DMA = pltpu.SemaphoreType.DMA
-PARAMS = pltpu.CompilerParams(vmem_limit_bytes=48 * 1024 * 1024)
+PARAMS = pltpu.CompilerParams(vmem_limit_bytes=16 * 1024 * 1024)
 
 
 class Plan:
@@ -59,7 +59,7 @@
             return s // (self.ncol * self.ndep), s // self.ndep % self.ncol, s % self.ndep
         return s // self.ndep, s * 0, s % self.ndep
 
-    def tables(self):
+    def tables(self, dtype=BF16):
         q = np.arange(self.Q)[None, :]
         s = np.arange(self.G)[:, None]
         e = np.arange(LANES)[:, None]
@@ -82,7 +82,7 @@
         groups = [np.concatenate(select, 1), np.concatenate(masks, 0), before, np.concatenate(pick, 1)]
         far = (k // self.kc != dep_s * self.ncol + col_s) | (not self.whole)
         groups += [np.concatenate([inner, first], 1), np.concatenate([chunk, far], 0)]
-        return [jnp.asarray(t.astype(np.float32), BF16) for t in groups]
+        return [jnp.asarray(t.astype(np.float32), dtype) for t in groups]
 
 
 def dot(x, y):
@@ -92,7 +92,8 @@
 def dot_high(x, y):
     x_high, y_high = x.astype(BF16), y.astype(BF16)
     x_low, y_low = (x - x_high.astype(F32)).astype(BF16), (y - y_high.astype(F32)).astype(BF16)
-    return dot(x_high, y_low) + dot(x_low, y_high) + dot(x_high, y_high)
+    x_terms = jnp.concatenate([x_high, x_low, x_high], axis=1)
+    return dot(x_terms, jnp.concatenate([y_low, y_high, y_high], axis=0))
 
 
 def entry_row(plan, entries):
@@ -102,19 +103,23 @@
     return row
 
 
-def entry(row, place):
-    lane = lax.broadcasted_iota(I32, row.shape, 1)
-    return jnp.sum(jnp.where(lane == place, row, 0)) != 0
-
-
-def prepare(plan, entries, b_hbm, out_ref, sems):
+def entry_bits(row, start, count):
+    lane = lax.broadcasted_iota(I32, row.shape, 1) - start
+    return jnp.sum(jnp.where((lane >= 0) & (lane < count), row << jnp.clip(lane, 0, count - 1), 0))
+
+
+def prepare(plan, entries, b_hbm, out_hbm, blocks, tile_ref, sems, out_sems):
     def piece(c, j):
-        return pltpu.make_async_copy(b_hbm.at[c], out_ref.at[:, :, pl.ds(j * plan.bs, plan.bs)], sems.at[j])
+        return pltpu.make_async_copy(b_hbm.at[c], blocks.at[j], sems.at[j])
+
+    def out(src, j, width):
+        return pltpu.make_async_copy(src, out_hbm.at[:, :, pl.ds(j * plan.bs, width)], out_sems.at[j])
 
     row = entry_row(plan, entries)
+    bits = entry_bits(row, plan.rows * plan.W, plan.nc)
     count = jnp.int32(0)
     for c in range(plan.nc):
-        stored = entry(row, plan.rows * plan.W + c)
+        stored = (bits >> c) & 1 == 1
         for j in range(min(c + 1, plan.slots)):
 
             @pl.when(stored & (count == j))
@@ -123,13 +128,22 @@
 
         count += stored.astype(I32)
 
-    tile = jnp.broadcast_to(row.astype(F32)[None], (plan.G, plan.R, LANES))
-    out_ref[:, :, plan.slots * plan.bs :] = tile
+    tile_ref[...] = jnp.broadcast_to(row.astype(F32)[None], tile_ref.shape)
+    last = out(tile_ref, plan.slots, LANES)
+    last.start()
     for j in range(plan.slots):
 
         @pl.when(count > j)
         def _(j=j):
             piece(0, j).wait()
+            out(blocks.at[j], j, plan.bs).start()
+
+    last.wait()
+    for j in range(plan.slots):
+
+        @pl.when(count > j)
+        def _(j=j):
+            out(blocks.at[j], j, plan.bs).wait()
 
 
 def stage(plan, wave, entries, a_hbm, *refs):
@@ -137,7 +151,8 @@
     col, dep = lax.axis_index("col"), lax.axis_index("depth")
     row = entry_row(plan, entries)
     start = 0 if plan.whole else col * plan.kc
-    stored = [[entry(row, r * plan.W + start + kk) for kk in range(plan.kc)] for r in range(plan.rows)]
+    bits = [entry_bits(row, r * plan.W + start, plan.kc) for r in range(plan.rows)]
+    stored = [[(bits[r] >> kk) & 1 == 1 for kk in range(plan.kc)] for r in range(plan.rows)]
 
     def each(act):
         for r in range(plan.rows):
@@ -153,6 +168,15 @@
 
     each(lambda copy: copy.start())
     each(lambda copy: copy.wait())
+
+
+def clear(plan, _, zero_hbm, zero, sems):
+    zero[...] = jnp.zeros_like(zero)
+    copies = [pltpu.make_async_copy(zero, zero_hbm.at[0, c], sems.at[c]) for c in range(plan.nc)]
+    for copy in copies:
+        copy.start()
+    for copy in copies:
+        copy.wait()
 
 
 def needs(plan, tile, wide, masks, before, pick):
@@ -186,81 +210,81 @@
         out[n : n + 1] = jnp.sum(row, axis=0, keepdims=True).astype(I32)
 
 
-def fill(plan, again, rows, got_ref, out_ref):
-    for p in range(plan.J):
-
-        def body(d, carry, p=p):
-            value = plan.listed(rows, p, d)
-            slot = plan.column(value) if again else plan.slot(value)
-            start = pl.multiple_of(slot * plan.bs, plan.bs)
-            out_ref[d, p] = got_ref[plan.member(value), :, pl.ds(start, plan.bs)]
-            return carry
-
-        lax.fori_loop(0, plan.G, body, 0, unroll=8)
-
-
-def schedule(plan, again, turn, tile_ref, got_ref, *refs):
-    tables, (out_ref, rows_ref, scratch, sem) = refs[:4], refs[-4:]
-    base = (turn[0] * (2 * plan.J)).astype(F32)
-    need, partner, both, rank, slot, _ = needs(plan, tile_ref[:, 0, tile_ref.shape[2] - LANES :], *tables)
+def schedule(plan, turn, tile_ref, got_ref, *refs):
+    tables, rest, refs = refs[:4], refs[4:-5], refs[-5:]
+    out_ref, rows_ref, facts_ref, scratch, sem = refs
+    base = 0.0 if turn is None else (turn[0] * (2 * plan.J)).astype(F32)
+    need, partner, both, rank, slot, stored_a = needs(plan, tile_ref[:, 0, tile_ref.shape[2] - LANES :], *tables)
     list_blocks(plan, base, need, partner, both, rank, slot, rows_ref)
     copy = pltpu.make_async_copy(rows_ref, scratch, sem.at[0])
     copy.start()
+    for n, fact in enumerate((need, both, stored_a, jnp.broadcast_to(slot, need.shape))):
+        facts_ref[n] = fact
     copy.wait()
-    fill(plan, again, scratch, got_ref, out_ref)
-
-
-def settle(plan, wave, got_ref, *refs):
-    tables, (inner, chunk, a_hbm), refs = refs[:4], refs[4:7], refs[7:]
-    outs, (waves_ref, state_ref, zero_hbm, place_ref, place_smem, zero, sems, zero_sems) = refs[:-8], refs[-8:]
-    zero[...] = jnp.zeros_like(zero)
-    clear = [pltpu.make_async_copy(zero, zero_hbm.at[0, c], zero_sems.at[c]) for c in range(plan.nc)]
-    for copy in clear:
-        copy.start()
-    need, _, both, _, slot, stored_a = needs(plan, got_ref[:, 0, got_ref.shape[2] - LANES :], *tables)
+    for p in range(plan.J):
+
+        def body(d, carry, p=p):
+            value = plan.listed(scratch, p, d)
+            slot = plan.slot(value)
+            start = pl.multiple_of(jnp.minimum(slot, plan.slots - 1) * plan.bs, plan.bs)
+            out_ref[d, p] = got_ref[plan.member(value), :, pl.ds(start, plan.bs)]
+            if rest:
+
+                @pl.when(slot >= plan.slots)
+                def _():
+                    out_ref[d, p] = rest[0][plan.member(value)]
+
+            return carry
+
+        lax.fori_loop(0, plan.G, body, 0, unroll=1 if rest else 8)
+
+
+def settle(plan, wave, facts_ref, inner, chunk, a_hbm, *refs):
+    outs, (waves_ref, state_ref, place_ref, place_smem, sems) = refs[:-5], refs[-5:]
+    need, both, stored_a, slot = (facts_ref[n] for n in range(4))
     before, far = chunk[0:LANES], chunk[LANES:]
     left = jnp.minimum(dot(need, inner[:, :LANES]), 1.0)
     place = dot(dot(stored_a, inner[:, LANES:]), before)
     if plan.whole:
         late = jnp.where(place > 0, left, 0.0)
         place = jnp.where(place > 0, jnp.where(late > 0, 1.0 + dot(late, before), -1.0), 0.0)
-    place_ref[...] = place.astype(I32)
+    row, col, dep = lax.axis_index("row"), lax.axis_index("col"), lax.axis_index("depth")
+    member = lax.broadcasted_iota(I32, place.shape, 0)
+    owners = []
+    for dd, dc in plan.others[: len(outs)]:
+        to_dep, to_col = (dep + dd) % plan.ndep, (col + dc) % plan.ncol
+        owners.append((to_dep, (row * plan.ncol + to_col) * plan.ndep + to_dep))
+    for o, (_, to) in enumerate(owners):
+        place_ref[o : o + 1] = jnp.sum(jnp.where(member == to, place, 0.0), axis=0, keepdims=True).astype(I32)
     fetch = pltpu.make_async_copy(place_ref, place_smem, sems.at[len(outs)])
     fetch.start()
-    member = lax.axis_index(plan.axes)
-    mine = lax.broadcasted_iota(I32, place.shape, 0) == member
-    waves_ref[...] = jnp.sum(jnp.where(mine, place, 0.0), axis=0, keepdims=True).astype(I32)
+
+    def each(act):
+        for o, out in enumerate(outs):
+            to_dep = owners[o][0]
+            for kk in range(plan.kc):
+
+                @pl.when(place_smem[o, dep * plan.nrow + col * plan.kc + kk] == wave)
+                def _(o=o, kk=kk, out=out, to_dep=to_dep):
+                    act(pltpu.make_async_copy(a_hbm.at[to_dep, kk], out, sems.at[o]))
+
+    fetch.wait()
+    each(lambda copy: copy.start())
+    mine = jnp.where(member == lax.axis_index(plan.axes), place, 0.0)
+    waves_ref[...] = jnp.sum(mine, axis=0, keepdims=True).astype(I32)
     rounds = (jnp.max(jnp.sum(both, axis=1, keepdims=True)).astype(I32) + 2 * plan.J - 1) // (2 * plan.J)
     lost = jnp.max(need * jnp.where(slot >= plan.slots, 1.0, 0.0)) > 0
     waves = jnp.max(left * far * (place + 1.0))
     easy = jnp.where(lost, 3, jnp.where(rounds > 1, 1, 0))
-    hard = jnp.where((waves > plan.waves + 1) | (easy > 0), 4, 2)
+    hard = jnp.where((waves > plan.waves + 1) | lost, 4, 2)
     state_ref[0] = jnp.where(waves > plan.waves, hard, easy)
     state_ref[1] = rounds
-
-    row, col, dep = lax.axis_index("row"), lax.axis_index("col"), lax.axis_index("depth")
-
-    def each(act):
-        for o, out in enumerate(outs):
-            dd, dc = plan.others[o]
-            to_dep, to_col = (dep + dd) % plan.ndep, (col + dc) % plan.ncol
-            to = (row * plan.ncol + to_col) * plan.ndep + to_dep
-            for kk in range(plan.kc):
-
-                @pl.when(place_smem[to, dep * plan.nrow + col * plan.kc + kk] == wave)
-                def _(o=o, kk=kk, out=out, to_dep=to_dep):
-                    act(pltpu.make_async_copy(a_hbm.at[to_dep, kk], out, sems.at[o]))
-
-    fetch.wait()
-    each(lambda copy: copy.start())
     each(lambda copy: copy.wait())
-    for copy in clear:
-        copy.wait()
 
 
 def multiply(plan, raw, waves, first, rows, left, mine, theirs, a_hbm, *refs):
     lefts, refs = refs[: waves * len(plan.others)], refs[waves * len(plan.others) :]
-    _, out_hbm, a_scr, right, total, sems, out_sems = refs
+    _, out_hbm, a_scr, total, sems, out_sems = refs
     col, dep = lax.axis_index("col"), lax.axis_index("depth")
     member = lax.axis_index(plan.axes)
     listed = [plan.listed(rows, p, member) for p in range(plan.J)]
@@ -315,9 +339,9 @@
         @pl.when(ready[j])
         def _(j=j):
             source = mine if j < plan.J else theirs
-            right[...] = source[:, j % plan.J].reshape(plan.bs, plan.bs)
+            right = source[:, j % plan.J].reshape(plan.bs, plan.bs)
             copy(a_hbm.at[0, 0], j).wait()
-            total[column[j]] += dot_high(a_scr[j], right[...])
+            total[column[j]] += dot_high(a_scr[j], right)
 
     for act in (lambda copy: copy.start(), lambda copy: copy.wait()):
         for c in range(plan.nc):
@@ -358,33 +382,30 @@
     def swap(mine):
         return lax.ppermute(mine, "row", [(i, i ^ 1) for i in range(plan.nrow)])
 
-    def listed(again, turn, got, pieces):
-        send, rows = call(
-            functools.partial(schedule, plan, again),
-            (jax.ShapeDtypeStruct((G, J, R, bs), F32), jax.ShapeDtypeStruct(listing, I32)),
-            [SMEM] + [VMEM] * 6,
-            (VMEM, VMEM),
+    def listed(turn, got, rest, tables):
+        first = turn is None
+        return call(
+            functools.partial(schedule, plan, *(None,) * first),
+            (
+                jax.ShapeDtypeStruct((G, J, R, bs), F32),
+                jax.ShapeDtypeStruct(listing, I32),
+                jax.ShapeDtypeStruct((4, G, plan.Q), F32),
+            ),
+            [SMEM] * (not first) + [VMEM] * (6 + len(rest)),
+            (VMEM, VMEM, VMEM),
             [pltpu.SMEM(listing, I32), DMA((1,))],
-        )(jnp.reshape(turn, (1,)), got, pieces, *tables[:4])
-        return rows, lax.all_to_all(send, plan.axes, 0, 0, tiled=True)
-
-    def settled(wave, got, a_blocks):
+        )(*[] if first else [jnp.reshape(turn, (1,))], got, got, *tables[:4], *rest)
+
+    def settled(wave, facts, a_blocks, tables):
         count = len(plan.others) if plan.whole else 0
-        *late, waves, state, zero = call(
+        *sent, waves, state = call(
             functools.partial(settle, plan, wave),
-            (block,) * count
-            + (jax.ShapeDtypeStruct((1, LANES), I32), jax.ShapeDtypeStruct((2,), I32), result),
-            [VMEM] * 7 + [HBM],
-            (VMEM,) * count + (VMEM, SMEM, HBM),
-            [
-                pltpu.VMEM((G, LANES), I32),
-                pltpu.SMEM((G, LANES), I32),
-                pltpu.VMEM((bs, bs), F32),
-                DMA((count + 1,)),
-                DMA((nc,)),
-            ],
-        )(got, *tables, a_blocks)
-        return shift(late), waves, state, zero
+            (block,) * count + (jax.ShapeDtypeStruct((1, LANES), I32), jax.ShapeDtypeStruct((2,), I32)),
+            [VMEM] * 3 + [HBM],
+            (VMEM,) * count + (VMEM, SMEM),
+            [pltpu.VMEM((8, LANES), I32), pltpu.SMEM((8, LANES), I32), DMA((count + 1,))],
+        )(facts, *tables[4:], a_blocks)
+        return shift(sent), waves, state
 
     def product(raw, first, rows, waves, mine, theirs, a_blocks, lefts, start):
         return call(
@@ -394,7 +415,6 @@
             HBM,
             [
                 pltpu.VMEM((2 * J, bs, bs), F32),
-                pltpu.VMEM((bs, bs), F32),
                 pltpu.VMEM((nc, bs, bs), F32),
                 DMA((2 * J,)),
                 DMA((nc,)),
@@ -415,8 +435,13 @@
         functools.partial(prepare, plan),
         jax.ShapeDtypeStruct((G, R, width), F32),
         [VMEM, HBM],
-        VMEM,
-        [DMA((plan.slots,))],
+        HBM,
+        [
+            pltpu.VMEM((plan.slots, G, R, bs), F32),
+            pltpu.VMEM((G, R, LANES), F32),
+            DMA((plan.slots,)),
+            DMA((plan.slots + 1,)),
+        ],
     )(entries, b_pieces)
     got = exchange(pieces)
     lefts = []
@@ -431,49 +456,58 @@
         lefts += shift([staged[dd] for dd, _ in plan.others])
 
     tables = plan.tables()
-    got, lefts = lax.optimization_barrier((got, lefts))
-    rows, mine = listed(False, jnp.int32(0), got, got)
-    late, waves, state, zero = settled(1, got, a_blocks)
-    mine, late, zero = lax.optimization_barrier((mine, late, zero))
-    lefts = lefts + late
+    zero = call(
+        functools.partial(clear, plan), result, [VMEM], HBM, [pltpu.VMEM((bs, bs), F32), DMA((nc,))]
+    )(staged[0])
+    got, lefts, zero = lax.optimization_barrier((got, lefts, zero))
+    send, rows, facts = listed(None, got, [], tables)
+    mine = exchange(send)
+    sent, waves, state = settled(1, facts, a_blocks, tables)
+    mine, sent = lax.optimization_barrier((mine, sent))
+    lefts = lefts + sent
     theirs = swap(mine)
     c_blocks = product(False, True, rows, waves, mine, theirs, a_blocks, lefts, zero)
 
-    def rounds(raw, again, got, pieces, state, waves, a_blocks, lefts, begin, c_blocks):
+    again = plan.tables(F32)
+
+    def rounds(raw, rest, got, state, waves, a_blocks, lefts, begin, c_blocks):
         total = state[1] if plan.whole else lax.pmax(state[1], "col")
 
         def body(turn, c_blocks):
-            rows, mine = listed(again, turn, got, pieces)
+            send, rows, _ = listed(turn, got, rest, again)
+            mine = exchange(send)
             return product(raw, False, rows, waves, mine, swap(mine), a_blocks, lefts, c_blocks)
 
         return lax.fori_loop(begin, total, body, c_blocks)
 
-    def spread_again(b_pieces):
-        return exchange(b_pieces.transpose(1, 2, 0, 3).reshape(G, R, nc * bs))
+    def spread_rest(b_pieces):
+        return [exchange(b_pieces[plan.slots])] if plan.slots < nc else []
 
     def done(c_blocks, *_):
         return c_blocks
 
-    def more_rounds(c_blocks, rows, mine, theirs, got, state, waves, a_blocks, b_pieces, *lefts):
-        return rounds(False, False, got, got, state, waves, a_blocks, lefts, 1, c_blocks)
-
-    def more_waves(c_blocks, rows, mine, theirs, got, state, waves, a_blocks, b_pieces, *lefts):
-        lefts += tuple(settled(2, got, a_blocks)[0])
-        return product(False, True, rows, waves, mine, theirs, a_blocks, lefts, c_blocks)
-
-    def more_pieces(c_blocks, rows, mine, theirs, got, state, waves, a_blocks, b_pieces, *lefts):
-        pieces, c_blocks = spread_again(b_pieces), jnp.zeros_like(c_blocks)
-        return rounds(False, True, got, pieces, state, waves, a_blocks, lefts, 0, c_blocks)
-
-    def anew(c_blocks, rows, mine, theirs, got, state, waves, a_blocks, b_pieces, *lefts):
-        pieces, c_blocks = spread_again(b_pieces), jnp.zeros_like(c_blocks)
+    def more_rounds(c_blocks, rows, mine, theirs, got, facts, state, waves, a_blocks, b_pieces, *lefts):
+        return rounds(False, [], got, state, waves, a_blocks, lefts, 1, c_blocks)
+
+    def more_waves(c_blocks, rows, mine, theirs, got, facts, state, waves, a_blocks, b_pieces, *lefts):
+        lefts += tuple(settled(2, facts, a_blocks, again)[0])
+        c_blocks = product(False, True, rows, waves, mine, theirs, a_blocks, lefts, c_blocks)
+        return rounds(False, [], got, state, waves, a_blocks, lefts, 1, c_blocks)
+
+    def more_pieces(c_blocks, rows, mine, theirs, got, facts, state, waves, a_blocks, b_pieces, *lefts):
+        c_blocks = jnp.zeros_like(c_blocks)
+        return rounds(False, spread_rest(b_pieces), got, state, waves, a_blocks, lefts, 0, c_blocks)
+
+    def anew(c_blocks, rows, mine, theirs, got, facts, state, waves, a_blocks, b_pieces, *lefts):
+        c_blocks = jnp.zeros_like(c_blocks)
         dep = lax.axis_index("depth")
         raw = [lax.dynamic_index_in_dim(a_blocks, (dep + dd) % plan.ndep, keepdims=False) for dd, _ in plan.others]
-        return rounds(True, True, got, pieces, state, waves, a_blocks, shift(raw), 0, c_blocks)
+        return rounds(True, spread_rest(b_pieces), got, state, waves, a_blocks, shift(raw), 0, c_blocks)
 
     index = state[0] if plan.whole else lax.pmax(state[0], "col")
     branches = [done, more_rounds, more_waves, more_pieces, anew]
-    return lax.switch(index, branches, c_blocks, rows, mine, theirs, got, state, waves, a_blocks, b_pieces, *lefts)
+    kept = (rows, mine, theirs, got, facts, state, waves, a_blocks, b_pieces)
+    return lax.switch(index, branches, c_blocks, *kept, *lefts)
 
 
 def solution(mesh):

time: 70.5 us -> 70.3 us (level)
  the two profiles are of different devices: /device:TPU:0 before, /device:TPU:16 now
where the time goes in v4:
time: 70.3 us; the launch traced here: 69.4 us
  waiting for transfers between devices  39.1 us (56%)
  starting transfers between devices  18 us (26%)
  Pallas kernels  10.9 us (16%)
  other arithmetic  0.77 us (1%)
    ppermute x6, waiting for transfers between devices, shift(): lax.ppermute(x, ('col', 'depth'), list(perm(*by)))  36.8 us
    all_to_all x2, starting transfers between devices, exchange(): return lax.all_to_all(pieces, plan.axes, 0, 0, tiled=True)  10.5 us
    ppermute x6, starting transfers between devices, shift(): lax.ppermute(x, ('col', 'depth'), list(perm(*by)))  7.45 us
    pallas_call x1, Pallas kernels, product(): call(functools.partial(multiply, plan, raw, len(lefts) // len(plan.others...  3.61 us
    pallas_call x1, Pallas kernels, listed(): call(functools.partial(schedule, plan, *(None,) * first), (jax.ShapeDtype...  2.47 us
    ppermute x1, waiting for transfers between devices, swap(): return lax.ppermute(mine, 'row', [(i, i ^ 1) for i in range(plan.nrow)])  2.24 us
    pallas_call x1, Pallas kernels, settled(): call(functools.partial(settle, plan, wave), (block,) * count + (jax.Shape...  1.8 us
  transfers between devices with their start and end apart: 9, of which 6 were waited for; matrix products, arithmetic and copies ran while one was open for 0% of the time, Pallas kernels for 6%

profile of v4, /device:TPU:16, one launch (start us, length us, event | category | flops | bytes accessed | tf_op | source)
XLA Modules:
  0.0 69.4 jit_solution(14856526579219814812)
XLA Ops:
  0.0 0.8 %pad_add_fusion.entries = s32[2,128]{1,0:T(2,128)S(1)} fusion(s32[2,4]{1,0:T(2,128)} %param.31, s32[1,4]{1,0:T(1,128)} %param.34, s32[1,4]{1,0:T(1,128)} %param.33), kind=kLoop, calls=%fused_computation.4 | loop fusion | flops 512 | bytes 1088 | tf_op jit(solution)/shard_map/add | solution.py:430
  0.8 0.8 %prepare.1 = f32[32,8,896]{2,1,0:T(8,128)} custom-call(s32[2,128]{1,0:T(2,128)S(1)} %pad_add_fusion.entries, f32[4,32,8,256]{3,2,1,0:T(8,128)} %bitcast.27), custom_call_target="tpu_custom_call" | custom-call | tf_op jit(solution)/shard_map/prepare/pallas_call | solution.py:434
  1.6 6.5 %all-to-all-start.6 = ((f32[32,8,896]{2,1,0:T(8,128)}), f32[32,8,896]{2,1,0:T(8,128)S(1)}, u32[]{:S(2)}, u32[]{:S(2)}) async-start(f32[32,8,896]{2,1,0:T(8,128)} %prepare.1), calls=%async_computation.6 | async-start | bytes 1835008 | tf_op jit(solution)/shard_map/all_to_all | solution.py:372
  8.1 0.0 copy-start.5
  8.1 0.0 copy-start.6
  8.1 0.0 copy-start.7
  8.2 1.2 %stage.1 = (f32[256,256]{1,0:T(8,128)S(1)}, f32[256,256]{1,0:T(8,128)S(1)}) custom-call(s32[2,128]{1,0:T(2,128)S(1)} %pad_add_fusion.entries, f32[2,4,256,256]{3,2,1,0:T(8,128)} %a_hbm.5), custom_call_target="tpu_custom_call" | custom-call | tf_op jit(solution)/shard_map/stage/pallas_call | solution.py:449
  9.4 1.5 %collective-permute-start.10 = (f32[256,256]{1,0:T(8,128)S(1)}, f32[256,256]{1,0:T(8,128)S(1)}, u32[]{:S(2)}, u32[]{:S(2)}) collective-permute-start(f32[256,256]{1,0:T(8,128)S(1)} %get-tuple-element.564._), channel_id=1, source_target_pairs={{0,2},{1,3},{2,0},{3,1},{4,6},{5,7},{6,4},{7,5},{8,10},{9,11},{10,... | collective-permute-start | bytes 786440 | tf_op jit(solution)/shard_map/ppermute | solution.py:380
  10.9 1.5 %collective-permute-start.12 = (f32[256,256]{1,0:T(8,128)S(1)}, f32[256,256]{1,0:T(8,128)S(1)}, u32[]{:S(2)}, u32[]{:S(2)}) collective-permute-start(f32[256,256]{1,0:T(8,128)S(1)} %get-tuple-element.565), channel_id=1, source_target_pairs={{0,3},{1,2},{2,1},{3,0},{4,7},{5,6},{6,5},{7,4},{8,11},{9,10},{10,... | collective-permute-start | bytes 786440 | tf_op jit(solution)/shard_map/ppermute | solution.py:380
  12.4 0.5 collective-permute-start.11
  12.9 1.0 %clear.1.refs_6_ = f32[1,4,256,256]{3,2,1,0:T(8,128)} custom-call(f32[256,256]{1,0:T(8,128)S(1)} %get-tuple-element.564._), custom_call_target="tpu_custom_call" | custom-call | tf_op jit(solution)/shard_map/clear/pallas_call | solution.py:459
  14.0 11.5 %collective-permute-done.10.refs_0_ = f32[256,256]{1,0:T(8,128)S(1)} collective-permute-done((f32[256,256]{1,0:T(8,128)S(1)}, f32[256,256]{1,0:T(8,128)S(1)}, u32[]{:S(2)}, u32[]{:S(2)}) %collective-permute-start.10) | collective-permute-done | bytes 262176 | tf_op jit(solution)/shard_map/ppermute | solution.py:380
  25.5 7.5 %collective-permute-done.12.refs_2_ = f32[256,256]{1,0:T(8,128)S(1)} collective-permute-done((f32[256,256]{1,0:T(8,128)S(1)}, f32[256,256]{1,0:T(8,128)S(1)}, u32[]{:S(2)}, u32[]{:S(2)}) %collective-permute-start.12) | collective-permute-done | bytes 262176 | tf_op jit(solution)/shard_map/ppermute | solution.py:380
  33.0 2.5 %schedule.5 = (f32[32,3,8,256]{3,2,1,0:T(8,128)}, s32[1,128]{1,0:T(1,128)S(1)}, f32[4,32,128]{2,1,0:T(8,128)S(1)}) custom-call(f32[32,8,896]{2,1,0:T(8,128)S(1)} %all-to-all-done.6.tile_ref.got_ref, f32[32,8,896]{2,1,0:T(8,128)S(1)} %all-to-all-done.6.tile_ref.got_ref, bf16[128,640]{1,0:T(8,128)(2,1)S(1)} %copy-done, bf16[96,128]{1,0:T(8,128)(2,1)S(1)} %copy-done.6, ...), custom_call_target="tpu_custom_call" | custom-call | tf_op jit(solution)/shard_map/schedule/pallas_call | solution.py:387
  35.5 4.0 %all-to-all-start.7 = ((f32[32,3,8,256]{3,2,1,0:T(8,128)}), f32[32,3,8,256]{3,2,1,0:T(8,128)S(1)}, u32[]{:S(2)}, u32[]{:S(2)}) async-start(f32[32,3,8,256]{3,2,1,0:T(8,128)} %get-tuple-element.571), calls=%async_computation.7 | async-start | bytes 1572864 | tf_op jit(solution)/shard_map/all_to_all | solution.py:372
  39.5 1.8 %settle.3 = (f32[256,256]{1,0:T(8,128)S(1)}, f32[256,256]{1,0:T(8,128)S(1)}, f32[256,256]{1,0:T(8,128)S(1)}, s32[1,128]{1,0:T(1,128)S(1)}, s32[2]{0:T(128)S(1)}) custom-call(f32[4,32,128]{2,1,0:T(8,128)S(1)} %get-tuple-element.567.facts_ref, bf16[128,256]{1,0:T(8,128)(2,1)S(1)} %copy-done.3, bf16[160,128]{1,0:T(8,128)(2,1)S(1)} %copy-done.4, ...), custom_call_target="tpu_custom_call" | custom-call | tf_op jit(solution)/shard_map/settle/pallas_call | solution.py:401
  41.3 2.3 %collective-permute-start.13 = (f32[256,256]{1,0:T(8,128)S(1)}, f32[256,256]{1,0:T(8,128)}, u32[]{:S(2)}, u32[]{:S(2)}) collective-permute-start(f32[256,256]{1,0:T(8,128)S(1)} %get-tuple-element.572), channel_id=1, source_target_pairs={{0,2},{1,3},{2,0},{3,1},{4,6},{5,7},{6,4},{7,5},{8,10},{9,11},{10,... | collective-permute-start | bytes 786440 | tf_op jit(solution)/shard_map/ppermute | solution.py:380
  43.6 1.6 %collective-permute-start.14 = (f32[256,256]{1,0:T(8,128)S(1)}, f32[256,256]{1,0:T(8,128)}, u32[]{:S(2)}, u32[]{:S(2)}) collective-permute-start(f32[256,256]{1,0:T(8,128)S(1)} %get-tuple-element.573), channel_id=1, source_target_pairs={{0,1},{1,0},{2,3},{3,2},{4,5},{5,4},{6,7},{7,6},{8,9},{9,8},{10,11... | collective-permute-start | bytes 786440 | tf_op jit(solution)/shard_map/ppermute | solution.py:380
  45.2 10.8 %collective-permute-done.13.refs_3_ = f32[256,256]{1,0:T(8,128)} collective-permute-done((f32[256,256]{1,0:T(8,128)S(1)}, f32[256,256]{1,0:T(8,128)}, u32[]{:S(2)}, u32[]{:S(2)}) %collective-permute-start.13) | collective-permute-done | bytes 262176 | tf_op jit(solution)/shard_map/ppermute | solution.py:380
  56.0 5.1 %collective-permute-done.14.refs_4_ = f32[256,256]{1,0:T(8,128)} collective-permute-done((f32[256,256]{1,0:T(8,128)S(1)}, f32[256,256]{1,0:T(8,128)}, u32[]{:S(2)}, u32[]{:S(2)}) %collective-permute-start.14) | collective-permute-done | bytes 262176 | tf_op jit(solution)/shard_map/ppermute | solution.py:380
  61.1 1.9 %collective-permute-done.15.refs_5_ = f32[256,256]{1,0:T(8,128)} collective-permute-done((f32[256,256]{1,0:T(8,128)S(1)}, f32[256,256]{1,0:T(8,128)}, u32[]{:S(2)}, u32[]{:S(2)}) %collective-permute-start.15) | collective-permute-done | bytes 262176 | tf_op jit(solution)/shard_map/ppermute | solution.py:380
  63.0 2.2 %collective-permute-done.16.theirs = f32[32,3,8,256]{3,2,1,0:T(8,128)S(1)} collective-permute-done((f32[32,3,8,256]{3,2,1,0:T(8,128)S(1)}, f32[32,3,8,256]{3,2,1,0:T(8,128)S(1)}, u32[]{:S(2)}, u32[]{:S(2)}) %collective-permute-start.16) | collective-permute-done | bytes 786464 | tf_op jit(solution)/shard_map/ppermute | solution.py:383
  65.3 3.6 %multiply.7 = f32[1,4,256,256]{3,2,1,0:T(8,128)} custom-call(s32[1,128]{1,0:T(1,128)S(1)} %get-tuple-element.569.rows, s32[1,128]{1,0:T(1,128)S(1)} %get-tuple-element.570.left, f32[32,3,8,256]{3,2,1,0:T(8,128)S(1)} %all-to-all-done.7.mine, f32[32,3,8,256]{3,2,1,0:T(8,128)S(1)} %collective-permute-done.16.theirs, ...), custom_call_target="tpu_custom_call", output_to_operand_aliasing={{}: (11, {})} | custom-call | tf_op jit(solution)/shard_map/multiply/pallas_call | solution.py:411
  68.9 0.2 conditional.1
  (22 shorter events, 0.1 us)
Async XLA Ops:
  1.6 31.4 %all-to-all-start.6 = ((f32[32,8,896]{2,1,0:T(8,128)}), f32[32,8,896]{2,1,0:T(8,128)S(1)}, u32[]{:S(2)}, u32[]{:S(2)}) async-start(f32[32,8,896]{2,1,0:T(8,128)} %prepare.1), calls=%async_computation.6 | async-start | bytes 1835008 | tf_op jit(solution)/shard_map/all_to_all | solution.py:372
  8.1 24.9 %copy-start = (bf16[128,640]{1,0:T(8,128)(2,1)S(1)}, bf16[128,640]{1,0:T(8,128)(2,1)}, u32[]{:S(2)}) copy-start(bf16[128,640]{1,0:T(8,128)(2,1)} %constant.82.clone.refs_0_) | copy-start | bytes 491524
  8.1 24.9 %copy-start.5 = (bf16[128,128]{1,0:T(8,128)(2,1)S(1)}, bf16[128,128]{1,0:T(8,128)(2,1)}, u32[]{:S(2)}) copy-start(bf16[128,128]{1,0:T(8,128)(2,1)} %constant.84.clone.refs_2_) | copy-start | bytes 98308
  8.1 24.9 %copy-start.6 = (bf16[96,128]{1,0:T(8,128)(2,1)S(1)}, bf16[96,128]{1,0:T(8,128)(2,1)}, u32[]{:S(2)}) copy-start(bf16[96,128]{1,0:T(8,128)(2,1)} %constant.83.clone.refs_1_) | copy-start | bytes 73732
  8.1 24.9 %copy-start.7 = (bf16[32,96]{1,0:T(8,128)(2,1)S(1)}, bf16[32,96]{1,0:T(8,128)(2,1)}, u32[]{:S(2)}) copy-start(bf16[32,96]{1,0:T(8,128)(2,1)} %constant.85.clone.refs_3_) | copy-start | bytes 18436
  9.4 16.1 %collective-permute-start.10 = (f32[256,256]{1,0:T(8,128)S(1)}, f32[256,256]{1,0:T(8,128)S(1)}, u32[]{:S(2)}, u32[]{:S(2)}) collective-permute-start(f32[256,256]{1,0:T(8,128)S(1)} %get-tuple-element.564._), channel_id=1, source_target_pairs={{0,2},{1,3},{2,0},{3,1},{4,6},{5,7},{6,4},{7,5},{8,10},{9,11},{10,... | collective-permute-start | bytes 786440 | tf_op jit(solution)/shard_map/ppermute | solution.py:380
  10.9 22.1 %collective-permute-start.12 = (f32[256,256]{1,0:T(8,128)S(1)}, f32[256,256]{1,0:T(8,128)S(1)}, u32[]{:S(2)}, u32[]{:S(2)}) collective-permute-start(f32[256,256]{1,0:T(8,128)S(1)} %get-tuple-element.565), channel_id=1, source_target_pairs={{0,3},{1,2},{2,1},{3,0},{4,7},{5,6},{6,5},{7,4},{8,11},{9,10},{10,... | collective-permute-start | bytes 786440 | tf_op jit(solution)/shard_map/ppermute | solution.py:380
  12.4 20.5 %collective-permute-start.11 = (f32[256,256]{1,0:T(8,128)S(1)}, f32[256,256]{1,0:T(8,128)}, u32[]{:S(2)}, u32[]{:S(2)}) collective-permute-start(f32[256,256]{1,0:T(8,128)S(1)} %get-tuple-element.565), channel_id=1, source_target_pairs={{0,1},{1,0},{2,3},{3,2},{4,5},{5,4},{6,7},{7,6},{8,9},{9,8},{10,11... | collective-permute-start | bytes 786440 | tf_op jit(solution)/shard_map/ppermute | solution.py:380
  13.9 25.6 %copy-start.3 = (bf16[128,256]{1,0:T(8,128)(2,1)S(1)}, bf16[128,256]{1,0:T(8,128)(2,1)}, u32[]{:S(2)}) copy-start(bf16[128,256]{1,0:T(8,128)(2,1)} %constant.86.clone.inner) | copy-start | bytes 196612
  13.9 25.5 %copy-start.4 = (bf16[160,128]{1,0:T(8,128)(2,1)S(1)}, bf16[160,128]{1,0:T(8,128)(2,1)}, u32[]{:S(2)}) copy-start(bf16[160,128]{1,0:T(8,128)(2,1)} %constant.87.clone.chunk) | copy-start | bytes 122884
  35.5 27.5 %all-to-all-start.7 = ((f32[32,3,8,256]{3,2,1,0:T(8,128)}), f32[32,3,8,256]{3,2,1,0:T(8,128)S(1)}, u32[]{:S(2)}, u32[]{:S(2)}) async-start(f32[32,3,8,256]{3,2,1,0:T(8,128)} %get-tuple-element.571), calls=%async_computation.7 | async-start | bytes 1572864 | tf_op jit(solution)/shard_map/all_to_all | solution.py:372
  41.3 14.7 %collective-permute-start.13 = (f32[256,256]{1,0:T(8,128)S(1)}, f32[256,256]{1,0:T(8,128)}, u32[]{:S(2)}, u32[]{:S(2)}) collective-permute-start(f32[256,256]{1,0:T(8,128)S(1)} %get-tuple-element.572), channel_id=1, source_target_pairs={{0,2},{1,3},{2,0},{3,1},{4,6},{5,7},{6,4},{7,5},{8,10},{9,11},{10,... | collective-permute-start | bytes 786440 | tf_op jit(solution)/shard_map/ppermute | solution.py:380
  43.6 17.5 %collective-permute-start.14 = (f32[256,256]{1,0:T(8,128)S(1)}, f32[256,256]{1,0:T(8,128)}, u32[]{:S(2)}, u32[]{:S(2)}) collective-permute-start(f32[256,256]{1,0:T(8,128)S(1)} %get-tuple-element.573), channel_id=1, source_target_pairs={{0,1},{1,0},{2,3},{3,2},{4,5},{5,4},{6,7},{7,6},{8,9},{9,8},{10,11... | collective-permute-start | bytes 786440 | tf_op jit(solution)/shard_map/ppermute | solution.py:380
  45.2 17.8 %collective-permute-start.15 = (f32[256,256]{1,0:T(8,128)S(1)}, f32[256,256]{1,0:T(8,128)}, u32[]{:S(2)}, u32[]{:S(2)}) collective-permute-start(f32[256,256]{1,0:T(8,128)S(1)} %get-tuple-element.574), channel_id=1, source_target_pairs={{0,3},{1,2},{2,1},{3,0},{4,7},{5,6},{6,5},{7,4},{8,11},{9,10},{10,... | collective-permute-start | bytes 786440 | tf_op jit(solution)/shard_map/ppermute | solution.py:380
  63.0 2.3 %collective-permute-start.16 = (f32[32,3,8,256]{3,2,1,0:T(8,128)S(1)}, f32[32,3,8,256]{3,2,1,0:T(8,128)S(1)}, u32[]{:S(2)}, u32[]{:S(2)}) collective-permute-start(f32[32,3,8,256]{3,2,1,0:T(8,128)S(1)} %all-to-all-done.7.mine), channel_id=1, source_target_pairs={{0,4},{4,0},{8,12},{12,8},{16,20},{20,16},{24,28},{28,24},{1,5},{5... | collective-permute-start | bytes 2359304 | tf_op jit(solution)/shard_map/ppermute | solution.py:383
  65.3 3.6 %copy-start.8 = (f32[128,640]{1,0:T(8,128)S(1)}, f32[128,640]{1,0:T(8,128)}, u32[]{:S(2)}) copy-start(f32[128,640]{1,0:T(8,128)} %constant.88.clone) | copy-start | bytes 983044
  65.3 3.6 %copy-start.9 = (f32[128,128]{1,0:T(8,128)S(1)}, f32[128,128]{1,0:T(8,128)}, u32[]{:S(2)}) copy-start(f32[128,128]{1,0:T(8,128)} %constant.90.clone) | copy-start | bytes 196612
  65.3 3.6 %copy-start.10 = (f32[96,128]{1,0:T(8,128)S(1)}, f32[96,128]{1,0:T(8,128)}, u32[]{:S(2)}) copy-start(f32[96,128]{1,0:T(8,128)} %constant.89.clone) | copy-start | bytes 147460
  65.3 3.7 %copy-start.13 = (f32[32,96]{1,0:T(8,128)S(1)}, f32[32,96]{1,0:T(8,128)}, u32[]{:S(2)}) copy-start(f32[32,96]{1,0:T(8,128)} %constant.91.clone) | copy-start | bytes 36868

commit v5 on v4

--- a/solution.py
+++ b/solution.py
@@ -9,6 +9,7 @@
 from jax.sharding import PartitionSpec as P
 
 LANES = 128
+PARTS = 4
 F32 = jnp.float32
 BF16 = jnp.bfloat16
 I32 = jnp.int32
@@ -35,6 +36,7 @@
         self.W = self.kc if self.whole else self.kc * self.ncol
         self.nk = self.kc * self.ncol * self.ndep
         self.J = 3 * self.nk // 16
+        self.more = self.nk // 16
         self.slots = self.nc - 1 if self.whole else self.nc
         self.waves = 2 if self.whole else self.kc
         assert self.G & (self.G - 1) == 0 and self.nc & (self.nc - 1) == 0
@@ -80,8 +82,10 @@
         pick = [(row_s == row_t) & (dep_s == rr) for rr in range(self.rows)]
         pick += [(row_s ^ 1 == row_t) & (col_s == col_t) & (dep_s == dep_t)]
         groups = [np.concatenate(select, 1), np.concatenate(masks, 0), before, np.concatenate(pick, 1)]
-        far = (k // self.kc != dep_s * self.ncol + col_s) | (not self.whole)
-        groups += [np.concatenate([inner, first], 1), np.concatenate([chunk, far], 0)]
+        dd = (dep_s - k // self.kc // self.ncol) % self.ndep
+        dc = (col_s - k // self.kc % self.ncol) % self.ncol
+        away = (dd * self.ncol + dc if self.whole else np.ones_like(dd)) * (k < self.nk)
+        groups += [np.concatenate([inner, first], 1), np.concatenate([chunk, away], 0)]
         return [jnp.asarray(t.astype(np.float32), dtype) for t in groups]
 
 
@@ -195,7 +199,7 @@
     return need, partner, both, dot(both, before[...]), slot, stored_a
 
 
-def list_blocks(plan, base, need, partner, both, rank, slot, out):
+def list_blocks(plan, J, base, need, partner, both, rank, slot, out):
     G, Q, per = plan.G, plan.Q, LANES // plan.G
     q = lax.broadcasted_iota(I32, (1, Q), 1).astype(F32)
     value = 4.0 * both * (slot * float(Q) + q) + 2.0 * partner + need
@@ -204,45 +208,57 @@
     turn = rank - ((member[:, :1] >> (plan.stride.bit_length() - 1)) & 1).astype(F32) - base
     for n in range(out.shape[0]):
         row = jnp.zeros((G, LANES), F32)
-        for p in range(n * per, min((n + 1) * per, plan.J)):
+        for p in range(n * per, min((n + 1) * per, J)):
             at = jnp.sum(jnp.where(turn == 2.0 * p, value, 0.0), axis=1, keepdims=True)
             row = jnp.where(lane == p % per * G + member, at, row)
         out[n : n + 1] = jnp.sum(row, axis=0, keepdims=True).astype(I32)
 
 
-def schedule(plan, turn, tile_ref, got_ref, *refs):
-    tables, rest, refs = refs[:4], refs[4:-5], refs[-5:]
-    out_ref, rows_ref, facts_ref, scratch, sem = refs
-    base = 0.0 if turn is None else (turn[0] * (2 * plan.J)).astype(F32)
+def schedule(plan, J, base, tile_ref, got_ref, *refs):
+    tables, rest, refs = refs[:4], refs[4:-7], refs[-7:]
+    out_hbm, rows_ref, facts_ref, pieces, scratch, sem, out_sems = refs
+    start = 0.0 if base is None else base[0].astype(F32)
     need, partner, both, rank, slot, stored_a = needs(plan, tile_ref[:, 0, tile_ref.shape[2] - LANES :], *tables)
-    list_blocks(plan, base, need, partner, both, rank, slot, rows_ref)
+    list_blocks(plan, J, start, need, partner, both, rank, slot, rows_ref)
     copy = pltpu.make_async_copy(rows_ref, scratch, sem.at[0])
     copy.start()
     for n, fact in enumerate((need, both, stored_a, jnp.broadcast_to(slot, need.shape))):
         facts_ref[n] = fact
     copy.wait()
-    for p in range(plan.J):
-
-        def body(d, carry, p=p):
+
+    def take(d):
+        for p in range(J):
             value = plan.listed(scratch, p, d)
             slot = plan.slot(value)
-            start = pl.multiple_of(jnp.minimum(slot, plan.slots - 1) * plan.bs, plan.bs)
-            out_ref[d, p] = got_ref[plan.member(value), :, pl.ds(start, plan.bs)]
+            lane = pl.multiple_of(jnp.minimum(slot, plan.slots - 1) * plan.bs, plan.bs)
+            pieces[d, p] = got_ref[plan.member(value), :, pl.ds(lane, plan.bs)]
             if rest:
 
                 @pl.when(slot >= plan.slots)
                 def _():
-                    out_ref[d, p] = rest[0][plan.member(value)]
-
-            return carry
-
-        lax.fori_loop(0, plan.G, body, 0, unroll=1 if rest else 8)
-
-
-def settle(plan, wave, facts_ref, inner, chunk, a_hbm, *refs):
-    outs, (waves_ref, state_ref, place_ref, place_smem, sems) = refs[:-5], refs[-5:]
+                    pieces[d, p] = rest[0][plan.member(value)]
+
+    size = plan.G // PARTS
+    copies = []
+    for n in range(PARTS):
+        part = pl.ds(n * size, size)
+        copies.append(pltpu.make_async_copy(pieces.at[part], out_hbm.at[part], out_sems.at[n]))
+
+        @pl.loop(n * size, (n + 1) * size, unroll=1 if rest else size)
+        def _(d):
+            take(d)
+
+        copies[n].start()
+    for copy in copies:
+        copy.wait()
+
+
+def settle(plan, wave, facts_ref, rows_ref, inner, chunk, a_hbm, *refs):
+    outs, refs = refs[:-7], refs[-7:]
+    waves_ref, waves_again, rows_again, state_ref, place_ref, place_smem, sems = refs
+    rows_again[...] = rows_ref[...]
     need, both, stored_a, slot = (facts_ref[n] for n in range(4))
-    before, far = chunk[0:LANES], chunk[LANES:]
+    before, away = chunk[0:LANES], chunk[LANES:].astype(F32)
     left = jnp.minimum(dot(need, inner[:, :LANES]), 1.0)
     place = dot(dot(stored_a, inner[:, LANES:]), before)
     if plan.whole:
@@ -272,24 +288,30 @@
     each(lambda copy: copy.start())
     mine = jnp.where(member == lax.axis_index(plan.axes), place, 0.0)
     waves_ref[...] = jnp.sum(mine, axis=0, keepdims=True).astype(I32)
-    rounds = (jnp.max(jnp.sum(both, axis=1, keepdims=True)).astype(I32) + 2 * plan.J - 1) // (2 * plan.J)
+    waves_again[...] = waves_ref[...]
+    most = jnp.max(jnp.sum(both, axis=1, keepdims=True)).astype(I32)
     lost = jnp.max(need * jnp.where(slot >= plan.slots, 1.0, 0.0)) > 0
-    waves = jnp.max(left * far * (place + 1.0))
-    easy = jnp.where(lost, 3, jnp.where(rounds > 1, 1, 0))
-    hard = jnp.where((waves > plan.waves + 1) | lost, 4, 2)
+    waves = jnp.max(left * jnp.where(away > 0, 1.0, 0.0) * (place + 1.0))
+    last = left * jnp.where(place == float(plan.waves), 1.0, 0.0) * away
+    count = len(plan.others) if plan.whole else 0
+    way = jnp.int32(2 + count)
+    for o in range(count):
+        way = jnp.where(jnp.max(jnp.where(last == o + 1.0, 0.0, last)) == 0.0, 2 + o, way)
+    easy = jnp.where(lost, 3 + count, jnp.where(most > 2 * plan.J, 1, 0))
+    hard = jnp.where((waves > plan.waves + 1) | lost, 4 + count, way)
     state_ref[0] = jnp.where(waves > plan.waves, hard, easy)
-    state_ref[1] = rounds
+    state_ref[1] = most
     each(lambda copy: copy.wait())
 
 
-def multiply(plan, raw, waves, first, rows, left, mine, theirs, a_hbm, *refs):
+def multiply(plan, J, raw, waves, first, rows, left, mine, theirs, a_hbm, *refs):
     lefts, refs = refs[: waves * len(plan.others)], refs[waves * len(plan.others) :]
     _, out_hbm, a_scr, total, sems, out_sems = refs
     col, dep = lax.axis_index("col"), lax.axis_index("depth")
     member = lax.axis_index(plan.axes)
-    listed = [plan.listed(rows, p, member) for p in range(plan.J)]
-    listed += [plan.listed(rows, p, member ^ plan.stride) >> 1 << 1 for p in range(plan.J)]
-    asked = [value & 1 for value in listed[: plan.J]] + [(value >> 1) & 1 for value in listed[plan.J :]]
+    listed = [plan.listed(rows, p, member) for p in range(J)]
+    listed += [plan.listed(rows, p, member ^ plan.stride) >> 1 << 1 for p in range(J)]
+    asked = [value & 1 for value in listed[: J]] + [(value >> 1) & 1 for value in listed[J :]]
 
     def copy(src, j):
         return pltpu.make_async_copy(src, a_scr.at[j], sems.at[j])
@@ -334,12 +356,12 @@
                 begin.start()
                 begin.wait()
 
-    for j in range(2 * plan.J):
+    for j in range(2 * J):
 
         @pl.when(ready[j])
         def _(j=j):
-            source = mine if j < plan.J else theirs
-            right = source[:, j % plan.J].reshape(plan.bs, plan.bs)
+            source = mine if j < J else theirs
+            right = source[:, j % J].reshape(plan.bs, plan.bs)
             copy(a_hbm.at[0, 0], j).wait()
             total[column[j]] += dot_high(a_scr[j], right)
 
@@ -366,50 +388,52 @@
     G, R, J, bs, nc = plan.G, plan.R, plan.J, plan.bs, plan.nc
     result = jax.ShapeDtypeStruct((1, nc, bs, bs), F32)
     block = jax.ShapeDtypeStruct((bs, bs), F32)
-    listing = (-(-J * G // LANES), LANES)
 
     def exchange(pieces):
         return lax.all_to_all(pieces, plan.axes, 0, 0, tiled=True)
 
-    def shift(staged):
+    def shift(staged, only=None):
         def perm(dd, dc):
             for x in range(plan.ncol):
                 for y in range(plan.ndep):
                     yield x * plan.ndep + y, (x + dc) % plan.ncol * plan.ndep + (y + dd) % plan.ndep
 
-        return [lax.ppermute(x, ("col", "depth"), list(perm(*by))) for x, by in zip(staged, plan.others)]
+        names = range(len(staged)) if only is None else only
+        return [lax.ppermute(staged[o], ("col", "depth"), list(perm(*plan.others[o]))) for o in names]
 
     def swap(mine):
         return lax.ppermute(mine, "row", [(i, i ^ 1) for i in range(plan.nrow)])
 
-    def listed(turn, got, rest, tables):
-        first = turn is None
+    def listed(J, base, got, rest, tables):
+        first = base is None
+        listing = (-(-J * G // LANES), LANES)
         return call(
-            functools.partial(schedule, plan, *(None,) * first),
+            functools.partial(schedule, plan, J, *(None,) * first),
             (
                 jax.ShapeDtypeStruct((G, J, R, bs), F32),
                 jax.ShapeDtypeStruct(listing, I32),
                 jax.ShapeDtypeStruct((4, G, plan.Q), F32),
             ),
             [SMEM] * (not first) + [VMEM] * (6 + len(rest)),
-            (VMEM, VMEM, VMEM),
-            [pltpu.SMEM(listing, I32), DMA((1,))],
-        )(*[] if first else [jnp.reshape(turn, (1,))], got, got, *tables[:4], *rest)
-
-    def settled(wave, facts, a_blocks, tables):
+            (HBM, VMEM, VMEM),
+            [pltpu.VMEM((G, J, R, bs), F32), pltpu.SMEM(listing, I32), DMA((1,)), DMA((PARTS,))],
+        )(*[] if first else [jnp.reshape(base, (1,))], got, got, *tables[:4], *rest)
+
+    def settled(wave, facts, rows, a_blocks, tables):
         count = len(plan.others) if plan.whole else 0
-        *sent, waves, state = call(
+        line, lists = jax.ShapeDtypeStruct((1, LANES), I32), jax.ShapeDtypeStruct(rows.shape, I32)
+        *sent, waves, waves_again, rows_again, state = call(
             functools.partial(settle, plan, wave),
-            (block,) * count + (jax.ShapeDtypeStruct((1, LANES), I32), jax.ShapeDtypeStruct((2,), I32)),
-            [VMEM] * 3 + [HBM],
-            (VMEM,) * count + (VMEM, SMEM),
+            (block,) * count + (line, line, lists, jax.ShapeDtypeStruct((2,), I32)),
+            [VMEM] * 4 + [HBM],
+            (VMEM,) * count + (VMEM, VMEM, VMEM, SMEM),
             [pltpu.VMEM((8, LANES), I32), pltpu.SMEM((8, LANES), I32), DMA((count + 1,))],
-        )(facts, *tables[4:], a_blocks)
-        return shift(sent), waves, state
-
-    def product(raw, first, rows, waves, mine, theirs, a_blocks, lefts, start):
+        )(facts, rows, *tables[4:], a_blocks)
+        return sent, waves, waves_again, rows_again, state
+
+    def product(J, raw, first, rows, waves, mine, theirs, a_blocks, lefts, start):
         return call(
-            functools.partial(multiply, plan, raw, len(lefts) // len(plan.others), first),
+            functools.partial(multiply, plan, J, raw, len(lefts) // len(plan.others), first),
             result,
             [SMEM, SMEM, VMEM, VMEM] + [HBM] * (2 + len(lefts)),
             HBM,
@@ -460,25 +484,27 @@
         functools.partial(clear, plan), result, [VMEM], HBM, [pltpu.VMEM((bs, bs), F32), DMA((nc,))]
     )(staged[0])
     got, lefts, zero = lax.optimization_barrier((got, lefts, zero))
-    send, rows, facts = listed(None, got, [], tables)
+    send, rows, facts = listed(J, None, got, [], tables)
     mine = exchange(send)
-    sent, waves, state = settled(1, facts, a_blocks, tables)
+    sent, waves, waves_again, rows_again, state = settled(1, facts, rows, a_blocks, tables)
+    sent = shift(sent)
     mine, sent = lax.optimization_barrier((mine, sent))
     lefts = lefts + sent
     theirs = swap(mine)
-    c_blocks = product(False, True, rows, waves, mine, theirs, a_blocks, lefts, zero)
+    near = [pltpu.with_memory_space_constraint(x, pltpu.VMEM) for x in (mine, theirs)]
+    c_blocks = product(J, False, True, rows, waves, *near, a_blocks, lefts, zero)
 
     again = plan.tables(F32)
 
-    def rounds(raw, rest, got, state, waves, a_blocks, lefts, begin, c_blocks):
-        total = state[1] if plan.whole else lax.pmax(state[1], "col")
+    def rounds(J, begin, raw, rest, got, state, waves, a_blocks, lefts, c_blocks):
+        most = state[1] if plan.whole else lax.pmax(state[1], "col")
 
         def body(turn, c_blocks):
-            send, rows, _ = listed(turn, got, rest, again)
+            send, rows, _ = listed(J, begin + 2 * J * turn, got, rest, again)
             mine = exchange(send)
-            return product(raw, False, rows, waves, mine, swap(mine), a_blocks, lefts, c_blocks)
-
-        return lax.fori_loop(begin, total, body, c_blocks)
+            return product(J, raw, False, rows, waves, mine, swap(mine), a_blocks, lefts, c_blocks)
+
+        return lax.fori_loop(0, (jnp.maximum(most - begin, 0) + 2 * J - 1) // (2 * J), body, c_blocks)
 
     def spread_rest(b_pieces):
         return [exchange(b_pieces[plan.slots])] if plan.slots < nc else []
@@ -487,26 +513,30 @@
         return c_blocks
 
     def more_rounds(c_blocks, rows, mine, theirs, got, facts, state, waves, a_blocks, b_pieces, *lefts):
-        return rounds(False, [], got, state, waves, a_blocks, lefts, 1, c_blocks)
-
-    def more_waves(c_blocks, rows, mine, theirs, got, facts, state, waves, a_blocks, b_pieces, *lefts):
-        lefts += tuple(settled(2, facts, a_blocks, again)[0])
-        c_blocks = product(False, True, rows, waves, mine, theirs, a_blocks, lefts, c_blocks)
-        return rounds(False, [], got, state, waves, a_blocks, lefts, 1, c_blocks)
+        return rounds(plan.more, 2 * J, False, [], got, state, waves, a_blocks, lefts, c_blocks)
+
+    def more_waves(way, c_blocks, rows, mine, theirs, got, facts, state, waves, a_blocks, b_pieces, *lefts):
+        sent = settled(2, facts, rows, a_blocks, again)[0]
+        for o in range(len(sent)):
+            if way in (o, len(sent)):
+                sent[o] = shift(sent, [o])[0]
+        c_blocks = product(J, False, True, rows, waves, mine, theirs, a_blocks, lefts + tuple(sent), c_blocks)
+        return rounds(plan.more, 2 * J, False, [], got, state, waves, a_blocks, lefts + tuple(sent), c_blocks)
 
     def more_pieces(c_blocks, rows, mine, theirs, got, facts, state, waves, a_blocks, b_pieces, *lefts):
         c_blocks = jnp.zeros_like(c_blocks)
-        return rounds(False, spread_rest(b_pieces), got, state, waves, a_blocks, lefts, 0, c_blocks)
+        return rounds(J, 0, False, spread_rest(b_pieces), got, state, waves, a_blocks, lefts, c_blocks)
 
     def anew(c_blocks, rows, mine, theirs, got, facts, state, waves, a_blocks, b_pieces, *lefts):
         c_blocks = jnp.zeros_like(c_blocks)
         dep = lax.axis_index("depth")
         raw = [lax.dynamic_index_in_dim(a_blocks, (dep + dd) % plan.ndep, keepdims=False) for dd, _ in plan.others]
-        return rounds(True, spread_rest(b_pieces), got, state, waves, a_blocks, shift(raw), 0, c_blocks)
+        return rounds(J, 0, True, spread_rest(b_pieces), got, state, waves, a_blocks, shift(raw), c_blocks)
 
     index = state[0] if plan.whole else lax.pmax(state[0], "col")
-    branches = [done, more_rounds, more_waves, more_pieces, anew]
-    kept = (rows, mine, theirs, got, facts, state, waves, a_blocks, b_pieces)
+    ways = [functools.partial(more_waves, way) for way in range(len(plan.others) * plan.whole + 1)]
+    branches = [done, more_rounds, *ways, more_pieces, anew]
+    kept = (rows_again, mine, theirs, got, facts, state, waves_again, a_blocks, b_pieces)
     return lax.switch(index, branches, c_blocks, *kept, *lefts)
 
 

time: 70.3 us -> 70.5 us (level)
  the two profiles are of different devices: /device:TPU:16 before, /device:TPU:0 now
where the time goes in v5:
time: 70.5 us; the launch traced here: 70.4 us
  waiting for transfers between devices  39.9 us (57%)
  starting transfers between devices  18.1 us (26%)
  Pallas kernels  11 us (16%)
  other arithmetic  0.77 us (1%)
    ppermute x6, waiting for transfers between devices, shift(): lax.ppermute(staged[o], ('col', 'depth'), list(perm(*plan.others[o])))  37.7 us
    all_to_all x2, starting transfers between devices, exchange(): return lax.all_to_all(pieces, plan.axes, 0, 0, tiled=True)  11 us
    ppermute x6, starting transfers between devices, shift(): lax.ppermute(staged[o], ('col', 'depth'), list(perm(*plan.others[o])))  7.11 us
    pallas_call x1, Pallas kernels, product(): call(functools.partial(multiply, plan, J, raw, len(lefts) // len(plan.oth...  2.82 us
    ppermute x1, waiting for transfers between devices, swap(): return lax.ppermute(mine, 'row', [(i, i ^ 1) for i in range(plan.nrow)])  2.24 us
    pallas_call x1, Pallas kernels, listed(): call(functools.partial(schedule, plan, J, *(None,) * first), (jax.ShapeDt...  2.19 us
    pallas_call x1, Pallas kernels, local(): call(functools.partial(prepare, plan), jax.ShapeDtypeStruct((G, R, width)...  1.95 us
    pallas_call x1, Pallas kernels, settled(): call(functools.partial(settle, plan, wave), (block,) * count + (line, lin...  1.8 us
  transfers between devices with their start and end apart: 9, of which 5 were waited for; matrix products, arithmetic and copies ran while one was open for 0% of the time, Pallas kernels for 6%

profile of v5, /device:TPU:0, one launch (start us, length us, event | category | flops | bytes accessed | tf_op | source)
XLA Modules:
  0.0 70.4 jit_solution(9185770000090493115)
XLA Ops:
  0.0 0.8 %pad_add_fusion.entries = s32[2,128]{1,0:T(2,128)S(1)} fusion(s32[2,4]{1,0:T(2,128)} %param.40, s32[1,4]{1,0:T(1,128)} %param.43, s32[1,4]{1,0:T(1,128)} %param.42), kind=kLoop, calls=%fused_computation.4 | loop fusion | flops 512 | bytes 1088 | tf_op jit(solution)/shard_map/add | solution.py:454
  0.8 2.0 %prepare.1 = f32[32,8,896]{2,1,0:T(8,128)} custom-call(s32[2,128]{1,0:T(2,128)S(1)} %pad_add_fusion.entries, f32[4,32,8,256]{3,2,1,0:T(8,128)} %bitcast.41), custom_call_target="tpu_custom_call" | custom-call | tf_op jit(solution)/shard_map/prepare/pallas_call | solution.py:458
  2.7 7.3 %all-to-all-start.9 = ((f32[32,8,896]{2,1,0:T(8,128)}), f32[32,8,896]{2,1,0:T(8,128)S(1)}, u32[]{:S(2)}, u32[]{:S(2)}) async-start(f32[32,8,896]{2,1,0:T(8,128)} %prepare.1), calls=%async_computation.9 | async-start | bytes 1835008 | tf_op jit(solution)/shard_map/all_to_all | solution.py:393
  10.0 0.0 copy-start
  10.1 0.0 copy-start.12
  10.1 0.0 copy-start.13
  10.1 1.2 %stage.1 = (f32[256,256]{1,0:T(8,128)S(1)}, f32[256,256]{1,0:T(8,128)S(1)}) custom-call(s32[2,128]{1,0:T(2,128)S(1)} %pad_add_fusion.entries, f32[2,4,256,256]{3,2,1,0:T(8,128)} %a_hbm.5), custom_call_target="tpu_custom_call" | custom-call | tf_op jit(solution)/shard_map/stage/pallas_call | solution.py:473
  11.3 1.9 %collective-permute-start.16 = (f32[256,256]{1,0:T(8,128)S(1)}, f32[256,256]{1,0:T(8,128)S(1)}, u32[]{:S(2)}, u32[]{:S(2)}) collective-permute-start(f32[256,256]{1,0:T(8,128)S(1)} %get-tuple-element.1067._), channel_id=1, source_target_pairs={{0,2},{1,3},{2,0},{3,1},{4,6},{5,7},{6,4},{7,5},{8,10},{9,11},{10,... | collective-permute-start | bytes 786440 | tf_op jit(solution)/shard_map/ppermute | solution.py:402
  13.2 1.4 %collective-permute-start.18 = (f32[256,256]{1,0:T(8,128)S(1)}, f32[256,256]{1,0:T(8,128)}, u32[]{:S(2)}, u32[]{:S(2)}) collective-permute-start(f32[256,256]{1,0:T(8,128)S(1)} %get-tuple-element.1068), channel_id=1, source_target_pairs={{0,3},{1,2},{2,1},{3,0},{4,7},{5,6},{6,5},{7,4},{8,11},{9,10},{10,... | collective-permute-start | bytes 786440 | tf_op jit(solution)/shard_map/ppermute | solution.py:402
  14.6 0.3 collective-permute-start.17
  14.8 1.0 %clear.1.refs_6_ = f32[1,4,256,256]{3,2,1,0:T(8,128)} custom-call(f32[256,256]{1,0:T(8,128)S(1)} %get-tuple-element.1067._), custom_call_target="tpu_custom_call" | custom-call | tf_op jit(solution)/shard_map/clear/pallas_call | solution.py:483
  15.9 11.5 %collective-permute-done.16.refs_0_ = f32[256,256]{1,0:T(8,128)S(1)} collective-permute-done((f32[256,256]{1,0:T(8,128)S(1)}, f32[256,256]{1,0:T(8,128)S(1)}, u32[]{:S(2)}, u32[]{:S(2)}) %collective-permute-start.16) | collective-permute-done | bytes 262176 | tf_op jit(solution)/shard_map/ppermute | solution.py:402
  27.4 7.9 %collective-permute-done.18.refs_2_ = f32[256,256]{1,0:T(8,128)} collective-permute-done((f32[256,256]{1,0:T(8,128)S(1)}, f32[256,256]{1,0:T(8,128)}, u32[]{:S(2)}, u32[]{:S(2)}) %collective-permute-start.18) | collective-permute-done | bytes 262176 | tf_op jit(solution)/shard_map/ppermute | solution.py:402
  35.4 2.2 %schedule.8 = (f32[32,3,8,256]{3,2,1,0:T(8,128)}, s32[1,128]{1,0:T(1,128)S(1)}, f32[4,32,128]{2,1,0:T(8,128)S(1)}) custom-call(f32[32,8,896]{2,1,0:T(8,128)S(1)} %all-to-all-done.9.tile_ref.got_ref, f32[32,8,896]{2,1,0:T(8,128)S(1)} %all-to-all-done.9.tile_ref.got_ref, bf16[128,640]{1,0:T(8,128)(2,1)S(1)} %copy-done, bf16[96,128]{1,0:T(8,128)(2,1)S(1)} %copy-done.12, ...), custom_call_target="tpu_custom_call" | custom-call | tf_op jit(solution)/shard_map/schedule/pallas_call | solution.py:410
  37.6 3.7 %all-to-all-start.10 = ((f32[32,3,8,256]{3,2,1,0:T(8,128)}), f32[32,3,8,256]{3,2,1,0:T(8,128)S(1)}, u32[]{:S(2)}, u32[]{:S(2)}) async-start(f32[32,3,8,256]{3,2,1,0:T(8,128)} %get-tuple-element.1074), calls=%async_computation.10 | async-start | bytes 1572864 | tf_op jit(solution)/shard_map/all_to_all | solution.py:393
  41.3 1.8 %settle.9 = (f32[256,256]{1,0:T(8,128)S(1)}, f32[256,256]{1,0:T(8,128)S(1)}, f32[256,256]{1,0:T(8,128)S(1)}, s32[1,128]{1,0:T(1,128)S(1)}, s32[1,128]{1,0:T(1,128)}, /*index=5*/s32[1,128]{1,0:T(1,128)}, s32[2]{0:T(128)S(1)}) custom-call(f32[4,32,128]{2,1,0:T(8,128)S(1)} %get-tuple-element.1070.facts_ref, s32[1,128]{1,0:T(1,128)S(1)} %get-tuple-element.1071.rows_ref.rows, ...), custom_call_target="tpu_custom_call" | custom-call | tf_op jit(solution)/shard_map/settle/pallas_call | solution.py:425
  43.1 1.8 %collective-permute-start.19 = (f32[256,256]{1,0:T(8,128)S(1)}, f32[256,256]{1,0:T(8,128)}, u32[]{:S(2)}, u32[]{:S(2)}) collective-permute-start(f32[256,256]{1,0:T(8,128)S(1)} %get-tuple-element.1075), channel_id=1, source_target_pairs={{0,2},{1,3},{2,0},{3,1},{4,6},{5,7},{6,4},{7,5},{8,10},{9,11},{10,... | collective-permute-start | bytes 786440 | tf_op jit(solution)/shard_map/ppermute | solution.py:402
  44.9 1.5 %collective-permute-start.20 = (f32[256,256]{1,0:T(8,128)S(1)}, f32[256,256]{1,0:T(8,128)}, u32[]{:S(2)}, u32[]{:S(2)}) collective-permute-start(f32[256,256]{1,0:T(8,128)S(1)} %get-tuple-element.1076), channel_id=1, source_target_pairs={{0,1},{1,0},{2,3},{3,2},{4,5},{5,4},{6,7},{7,6},{8,9},{9,8},{10,11... | collective-permute-start | bytes 786440 | tf_op jit(solution)/shard_map/ppermute | solution.py:402
  46.4 0.3 collective-permute-start.21
  46.6 11.0 %collective-permute-done.19.refs_3_ = f32[256,256]{1,0:T(8,128)} collective-permute-done((f32[256,256]{1,0:T(8,128)S(1)}, f32[256,256]{1,0:T(8,128)}, u32[]{:S(2)}, u32[]{:S(2)}) %collective-permute-start.19) | collective-permute-done | bytes 262176 | tf_op jit(solution)/shard_map/ppermute | solution.py:402
  57.6 7.3 %collective-permute-done.21.refs_5_ = f32[256,256]{1,0:T(8,128)} collective-permute-done((f32[256,256]{1,0:T(8,128)S(1)}, f32[256,256]{1,0:T(8,128)}, u32[]{:S(2)}, u32[]{:S(2)}) %collective-permute-start.21) | collective-permute-done | bytes 262176 | tf_op jit(solution)/shard_map/ppermute | solution.py:402
  65.0 2.2 %collective-permute-done.22.theirs = f32[32,3,8,256]{3,2,1,0:T(8,128)S(1)} collective-permute-done((f32[32,3,8,256]{3,2,1,0:T(8,128)S(1)}, f32[32,3,8,256]{3,2,1,0:T(8,128)S(1)}, u32[]{:S(2)}, u32[]{:S(2)}) %collective-permute-start.22) | collective-permute-done | bytes 786464 | tf_op jit(solution)/shard_map/ppermute | solution.py:405
  67.2 2.8 %multiply.16 = f32[1,4,256,256]{3,2,1,0:T(8,128)} custom-call(s32[1,128]{1,0:T(1,128)S(1)} %get-tuple-element.1071.rows_ref.rows, s32[1,128]{1,0:T(1,128)S(1)} %get-tuple-element.1073.left, f32[32,3,8,256]{3,2,1,0:T(8,128)S(1)} %all-to-all-done.10.mine, f32[32,3,8,256]{3,2,1,0:T(8,128)S(1)} %collective-permute-done.22.theirs, ...), custom_call_target="tpu_custom_call", output_to_operand_aliasing={{}: (11, {})} | custom-call | tf_op jit(solution)/shard_map/multiply/pallas_call | solution.py:435
  70.0 0.2 conditional.1
  (18 shorter events, 0.0 us)
Async XLA Ops:
  2.7 32.6 %all-to-all-start.9 = ((f32[32,8,896]{2,1,0:T(8,128)}), f32[32,8,896]{2,1,0:T(8,128)S(1)}, u32[]{:S(2)}, u32[]{:S(2)}) async-start(f32[32,8,896]{2,1,0:T(8,128)} %prepare.1), calls=%async_computation.9 | async-start | bytes 1835008 | tf_op jit(solution)/shard_map/all_to_all | solution.py:393
  10.0 25.3 %copy-start = (bf16[128,640]{1,0:T(8,128)(2,1)S(1)}, bf16[128,640]{1,0:T(8,128)(2,1)}, u32[]{:S(2)}) copy-start(bf16[128,640]{1,0:T(8,128)(2,1)} %constant.267.clone.refs_0_) | copy-start | bytes 491524
  10.0 25.3 %copy-start.11 = (bf16[128,128]{1,0:T(8,128)(2,1)S(1)}, bf16[128,128]{1,0:T(8,128)(2,1)}, u32[]{:S(2)}) copy-start(bf16[128,128]{1,0:T(8,128)(2,1)} %constant.269.clone.refs_2_) | copy-start | bytes 98308
  10.1 25.3 %copy-start.12 = (bf16[96,128]{1,0:T(8,128)(2,1)S(1)}, bf16[96,128]{1,0:T(8,128)(2,1)}, u32[]{:S(2)}) copy-start(bf16[96,128]{1,0:T(8,128)(2,1)} %constant.268.clone.refs_1_) | copy-start | bytes 73732
  10.1 25.3 %copy-start.13 = (bf16[32,96]{1,0:T(8,128)(2,1)S(1)}, bf16[32,96]{1,0:T(8,128)(2,1)}, u32[]{:S(2)}) copy-start(bf16[32,96]{1,0:T(8,128)(2,1)} %constant.270.clone.refs_3_) | copy-start | bytes 18436
  11.3 16.1 %collective-permute-start.16 = (f32[256,256]{1,0:T(8,128)S(1)}, f32[256,256]{1,0:T(8,128)S(1)}, u32[]{:S(2)}, u32[]{:S(2)}) collective-permute-start(f32[256,256]{1,0:T(8,128)S(1)} %get-tuple-element.1067._), channel_id=1, source_target_pairs={{0,2},{1,3},{2,0},{3,1},{4,6},{5,7},{6,4},{7,5},{8,10},{9,11},{10,... | collective-permute-start | bytes 786440 | tf_op jit(solution)/shard_map/ppermute | solution.py:402
  13.2 22.1 %collective-permute-start.18 = (f32[256,256]{1,0:T(8,128)S(1)}, f32[256,256]{1,0:T(8,128)}, u32[]{:S(2)}, u32[]{:S(2)}) collective-permute-start(f32[256,256]{1,0:T(8,128)S(1)} %get-tuple-element.1068), channel_id=1, source_target_pairs={{0,3},{1,2},{2,1},{3,0},{4,7},{5,6},{6,5},{7,4},{8,11},{9,10},{10,... | collective-permute-start | bytes 786440 | tf_op jit(solution)/shard_map/ppermute | solution.py:402
  14.6 20.7 %collective-permute-start.17 = (f32[256,256]{1,0:T(8,128)S(1)}, f32[256,256]{1,0:T(8,128)}, u32[]{:S(2)}, u32[]{:S(2)}) collective-permute-start(f32[256,256]{1,0:T(8,128)S(1)} %get-tuple-element.1068), channel_id=1, source_target_pairs={{0,1},{1,0},{2,3},{3,2},{4,5},{5,4},{6,7},{7,6},{8,9},{9,8},{10,11... | collective-permute-start | bytes 786440 | tf_op jit(solution)/shard_map/ppermute | solution.py:402
  15.9 25.4 %copy-start.9 = (bf16[128,256]{1,0:T(8,128)(2,1)S(1)}, bf16[128,256]{1,0:T(8,128)(2,1)}, u32[]{:S(2)}) copy-start(bf16[128,256]{1,0:T(8,128)(2,1)} %constant.271.clone.inner) | copy-start | bytes 196612
  15.9 25.4 %copy-start.10 = (bf16[160,128]{1,0:T(8,128)(2,1)S(1)}, bf16[160,128]{1,0:T(8,128)(2,1)}, u32[]{:S(2)}) copy-start(bf16[160,128]{1,0:T(8,128)(2,1)} %constant.272.clone.chunk) | copy-start | bytes 122884
  37.6 27.3 %copy-start.15 = (f32[4,32,128]{2,1,0:T(8,128)}, f32[4,32,128]{2,1,0:T(8,128)S(1)}, u32[]{:S(2)}) copy-start(f32[4,32,128]{2,1,0:T(8,128)S(1)} %get-tuple-element.1070.facts_ref) | copy-start | bytes 196612
  37.6 27.3 %all-to-all-start.10 = ((f32[32,3,8,256]{3,2,1,0:T(8,128)}), f32[32,3,8,256]{3,2,1,0:T(8,128)S(1)}, u32[]{:S(2)}, u32[]{:S(2)}) async-start(f32[32,3,8,256]{3,2,1,0:T(8,128)} %get-tuple-element.1074), calls=%async_computation.10 | async-start | bytes 1572864 | tf_op jit(solution)/shard_map/all_to_all | solution.py:393
  43.1 14.6 %collective-permute-start.19 = (f32[256,256]{1,0:T(8,128)S(1)}, f32[256,256]{1,0:T(8,128)}, u32[]{:S(2)}, u32[]{:S(2)}) collective-permute-start(f32[256,256]{1,0:T(8,128)S(1)} %get-tuple-element.1075), channel_id=1, source_target_pairs={{0,2},{1,3},{2,0},{3,1},{4,6},{5,7},{6,4},{7,5},{8,10},{9,11},{10,... | collective-permute-start | bytes 786440 | tf_op jit(solution)/shard_map/ppermute | solution.py:402
  44.9 12.7 %collective-permute-start.20 = (f32[256,256]{1,0:T(8,128)S(1)}, f32[256,256]{1,0:T(8,128)}, u32[]{:S(2)}, u32[]{:S(2)}) collective-permute-start(f32[256,256]{1,0:T(8,128)S(1)} %get-tuple-element.1076), channel_id=1, source_target_pairs={{0,1},{1,0},{2,3},{3,2},{4,5},{5,4},{6,7},{7,6},{8,9},{9,8},{10,11... | collective-permute-start | bytes 786440 | tf_op jit(solution)/shard_map/ppermute | solution.py:402
  46.4 18.5 %collective-permute-start.21 = (f32[256,256]{1,0:T(8,128)S(1)}, f32[256,256]{1,0:T(8,128)}, u32[]{:S(2)}, u32[]{:S(2)}) collective-permute-start(f32[256,256]{1,0:T(8,128)S(1)} %get-tuple-element.1077), channel_id=1, source_target_pairs={{0,3},{1,2},{2,1},{3,0},{4,7},{5,6},{6,5},{7,4},{8,11},{9,10},{10,... | collective-permute-start | bytes 786440 | tf_op jit(solution)/shard_map/ppermute | solution.py:402
  64.9 2.3 %collective-permute-start.22 = (f32[32,3,8,256]{3,2,1,0:T(8,128)S(1)}, f32[32,3,8,256]{3,2,1,0:T(8,128)S(1)}, u32[]{:S(2)}, u32[]{:S(2)}) collective-permute-start(f32[32,3,8,256]{3,2,1,0:T(8,128)S(1)} %all-to-all-done.10.mine), channel_id=1, source_target_pairs={{0,4},{4,0},{8,12},{12,8},{16,20},{20,16},{24,28},{28,24},{1,5},{5... | collective-permute-start | bytes 2359304 | tf_op jit(solution)/shard_map/ppermute | solution.py:405
  67.2 2.8 %copy-start.14 = (f32[32,96]{1,0:T(8,128)S(1)}, f32[32,96]{1,0:T(8,128)}, u32[]{:S(2)}) copy-start(f32[32,96]{1,0:T(8,128)} %constant.276.clone) | copy-start | bytes 36868

commit v6 on v5

--- a/solution.py
+++ b/solution.py
@@ -253,17 +253,16 @@
         copy.wait()
 
 
-def settle(plan, wave, facts_ref, rows_ref, inner, chunk, a_hbm, *refs):
-    outs, refs = refs[:-7], refs[-7:]
-    waves_ref, waves_again, rows_again, state_ref, place_ref, place_smem, sems = refs
-    rows_again[...] = rows_ref[...]
-    need, both, stored_a, slot = (facts_ref[n] for n in range(4))
-    before, away = chunk[0:LANES], chunk[LANES:].astype(F32)
+def settle(plan, wave, facts_ref, inner, chunk, a_hbm, *refs):
+    outs, (all_ref, place_ref, place_smem, sems) = refs[:-4], refs[-4:]
+    need, stored_a = facts_ref[0], facts_ref[2]
+    before = chunk[0:LANES]
     left = jnp.minimum(dot(need, inner[:, :LANES]), 1.0)
     place = dot(dot(stored_a, inner[:, LANES:]), before)
     if plan.whole:
         late = jnp.where(place > 0, left, 0.0)
         place = jnp.where(place > 0, jnp.where(late > 0, 1.0 + dot(late, before), -1.0), 0.0)
+    all_ref[...] = place
     row, col, dep = lax.axis_index("row"), lax.axis_index("col"), lax.axis_index("depth")
     member = lax.broadcasted_iota(I32, place.shape, 0)
     owners = []
@@ -286,6 +285,15 @@
 
     fetch.wait()
     each(lambda copy: copy.start())
+    each(lambda copy: copy.wait())
+
+
+def judge(plan, facts_ref, place_ref, rows_ref, inner, chunk, _, waves_ref, waves_again, rows_again, state_ref):
+    rows_again[...] = rows_ref[...]
+    need, both, slot, place = facts_ref[0], facts_ref[1], facts_ref[3], place_ref[...]
+    away = chunk[LANES:].astype(F32)
+    left = jnp.minimum(dot(need, inner[:, :LANES]), 1.0)
+    member = lax.broadcasted_iota(I32, place.shape, 0)
     mine = jnp.where(member == lax.axis_index(plan.axes), place, 0.0)
     waves_ref[...] = jnp.sum(mine, axis=0, keepdims=True).astype(I32)
     waves_again[...] = waves_ref[...]
@@ -301,7 +309,6 @@
     hard = jnp.where((waves > plan.waves + 1) | lost, 4 + count, way)
     state_ref[0] = jnp.where(waves > plan.waves, hard, easy)
     state_ref[1] = most
-    each(lambda copy: copy.wait())
 
 
 def multiply(plan, J, raw, waves, first, rows, left, mine, theirs, a_hbm, *refs):
@@ -419,17 +426,22 @@
             [pltpu.VMEM((G, J, R, bs), F32), pltpu.SMEM(listing, I32), DMA((1,)), DMA((PARTS,))],
         )(*[] if first else [jnp.reshape(base, (1,))], got, got, *tables[:4], *rest)
 
-    def settled(wave, facts, rows, a_blocks, tables):
+    def settled(wave, facts, a_blocks, tables):
         count = len(plan.others) if plan.whole else 0
-        line, lists = jax.ShapeDtypeStruct((1, LANES), I32), jax.ShapeDtypeStruct(rows.shape, I32)
-        *sent, waves, waves_again, rows_again, state = call(
+        *sent, place = call(
             functools.partial(settle, plan, wave),
-            (block,) * count + (line, line, lists, jax.ShapeDtypeStruct((2,), I32)),
-            [VMEM] * 4 + [HBM],
-            (VMEM,) * count + (VMEM, VMEM, VMEM, SMEM),
+            (block,) * count + (jax.ShapeDtypeStruct((G, LANES), F32),),
+            [VMEM] * 3 + [HBM],
+            (VMEM,) * (count + 1),
             [pltpu.VMEM((8, LANES), I32), pltpu.SMEM((8, LANES), I32), DMA((count + 1,))],
-        )(facts, rows, *tables[4:], a_blocks)
-        return sent, waves, waves_again, rows_again, state
+        )(facts, *tables[4:], a_blocks)
+        return sent, place
+
+    def judged(facts, place, rows, tables, after):
+        line = jax.ShapeDtypeStruct((1, LANES), I32)
+        shapes = (line, line, jax.ShapeDtypeStruct(rows.shape, I32), jax.ShapeDtypeStruct((2,), I32))
+        kernel = functools.partial(judge, plan)
+        return call(kernel, shapes, [VMEM] * 6, (VMEM, VMEM, VMEM, SMEM))(facts, place, rows, *tables[4:], after)
 
     def product(J, raw, first, rows, waves, mine, theirs, a_blocks, lefts, start):
         return call(
@@ -486,7 +498,8 @@
     got, lefts, zero = lax.optimization_barrier((got, lefts, zero))
     send, rows, facts = listed(J, None, got, [], tables)
     mine = exchange(send)
-    sent, waves, waves_again, rows_again, state = settled(1, facts, rows, a_blocks, tables)
+    sent, place = settled(1, facts, a_blocks, tables)
+    waves, waves_again, rows_again, state = judged(facts, place, rows, tables, sent[0] if sent else place)
     sent = shift(sent)
     mine, sent = lax.optimization_barrier((mine, sent))
     lefts = lefts + sent
@@ -516,7 +529,7 @@
         return rounds(plan.more, 2 * J, False, [], got, state, waves, a_blocks, lefts, c_blocks)
 
     def more_waves(way, c_blocks, rows, mine, theirs, got, facts, state, waves, a_blocks, b_pieces, *lefts):
-        sent = settled(2, facts, rows, a_blocks, again)[0]
+        sent = settled(2, facts, a_blocks, again)[0]
         for o in range(len(sent)):
             if way in (o, len(sent)):
                 sent[o] = shift(sent, [o])[0]

time: 70.5 us -> 69.3 us (0.983)
  the two profiles are of different devices: /device:TPU:0 before, /device:TPU:1 now
where the time goes in v6:
time: 69.3 us; the launch traced here: 69.5 us
  waiting for transfers between devices  39.2 us (57%)
  starting transfers between devices  17.6 us (25%)
  Pallas kernels  11.3 us (16%)
  other arithmetic  0.77 us (1%)
    ppermute x6, waiting for transfers between devices, shift(): lax.ppermute(staged[o], ('col', 'depth'), list(perm(*plan.others[o])))  38.1 us
    all_to_all x2, starting transfers between devices, exchange(): return lax.all_to_all(pieces, plan.axes, 0, 0, tiled=True)  11.4 us
    ppermute x6, starting transfers between devices, shift(): lax.ppermute(staged[o], ('col', 'depth'), list(perm(*plan.others[o])))  5.43 us
    pallas_call x1, Pallas kernels, product(): call(functools.partial(multiply, plan, J, raw, len(lefts) // len(plan.oth...  3.01 us
    pallas_call x1, Pallas kernels, listed(): call(functools.partial(schedule, plan, J, *(None,) * first), (jax.ShapeDt...  2.18 us
    pallas_call x1, Pallas kernels, local(): call(functools.partial(prepare, plan), jax.ShapeDtypeStruct((G, R, width)...  1.93 us
  transfers between devices with their start and end apart: 9, of which 4 were waited for; matrix products, arithmetic and copies ran while one was open for 0% of the time, Pallas kernels for 6%

profile of v6, /device:TPU:1, one launch (start us, length us, event | category | flops | bytes accessed | tf_op | source)
XLA Modules:
  0.0 69.5 jit_solution(9121602536010079707)
XLA Ops:
  0.0 0.8 %pad_add_fusion.entries = s32[2,128]{1,0:T(2,128)S(1)} fusion(s32[2,4]{1,0:T(2,128)} %param.40, s32[1,4]{1,0:T(1,128)} %param.43, s32[1,4]{1,0:T(1,128)} %param.42), kind=kLoop, calls=%fused_computation.4 | loop fusion | flops 512 | bytes 1088 | tf_op jit(solution)/shard_map/add | solution.py:466
  0.8 1.9 %prepare.1 = f32[32,8,896]{2,1,0:T(8,128)} custom-call(s32[2,128]{1,0:T(2,128)S(1)} %pad_add_fusion.entries, f32[4,32,8,256]{3,2,1,0:T(8,128)} %bitcast.41), custom_call_target="tpu_custom_call" | custom-call | tf_op jit(solution)/shard_map/prepare/pallas_call | solution.py:470
  2.7 7.1 %all-to-all-start.9 = ((f32[32,8,896]{2,1,0:T(8,128)}), f32[32,8,896]{2,1,0:T(8,128)S(1)}, u32[]{:S(2)}, u32[]{:S(2)}) async-start(f32[32,8,896]{2,1,0:T(8,128)} %prepare.1), calls=%async_computation.9 | async-start | bytes 1835008 | tf_op jit(solution)/shard_map/all_to_all | solution.py:400
  9.8 0.0 copy-start.1
  9.8 0.0 copy-start.11
  9.9 1.3 %stage.1 = (f32[256,256]{1,0:T(8,128)S(1)}, f32[256,256]{1,0:T(8,128)S(1)}) custom-call(s32[2,128]{1,0:T(2,128)S(1)} %pad_add_fusion.entries, f32[2,4,256,256]{3,2,1,0:T(8,128)} %a_hbm.5), custom_call_target="tpu_custom_call" | custom-call | tf_op jit(solution)/shard_map/stage/pallas_call | solution.py:485
  11.1 1.4 %collective-permute-start.16 = (f32[256,256]{1,0:T(8,128)S(1)}, f32[256,256]{1,0:T(8,128)S(1)}, u32[]{:S(2)}, u32[]{:S(2)}) collective-permute-start(f32[256,256]{1,0:T(8,128)S(1)} %get-tuple-element.1068._), channel_id=1, source_target_pairs={{0,2},{1,3},{2,0},{3,1},{4,6},{5,7},{6,4},{7,5},{8,10},{9,11},{10,... | collective-permute-start | bytes 786440 | tf_op jit(solution)/shard_map/ppermute | solution.py:409
  12.5 1.0 %collective-permute-start.18 = (f32[256,256]{1,0:T(8,128)S(1)}, f32[256,256]{1,0:T(8,128)}, u32[]{:S(2)}, u32[]{:S(2)}) collective-permute-start(f32[256,256]{1,0:T(8,128)S(1)} %get-tuple-element.1069), channel_id=1, source_target_pairs={{0,3},{1,2},{2,1},{3,0},{4,7},{5,6},{6,5},{7,4},{8,11},{9,10},{10,... | collective-permute-start | bytes 786440 | tf_op jit(solution)/shard_map/ppermute | solution.py:409
  13.5 0.4 collective-permute-start.17
  13.9 1.0 %clear.1.refs_6_ = f32[1,4,256,256]{3,2,1,0:T(8,128)} custom-call(f32[256,256]{1,0:T(8,128)S(1)} %get-tuple-element.1068._), custom_call_target="tpu_custom_call" | custom-call | tf_op jit(solution)/shard_map/clear/pallas_call | solution.py:495
  14.9 10.9 %collective-permute-done.16.refs_0_ = f32[256,256]{1,0:T(8,128)S(1)} collective-permute-done((f32[256,256]{1,0:T(8,128)S(1)}, f32[256,256]{1,0:T(8,128)S(1)}, u32[]{:S(2)}, u32[]{:S(2)}) %collective-permute-start.16) | collective-permute-done | bytes 262176 | tf_op jit(solution)/shard_map/ppermute | solution.py:409
  25.8 8.7 %collective-permute-done.18.refs_2_ = f32[256,256]{1,0:T(8,128)} collective-permute-done((f32[256,256]{1,0:T(8,128)S(1)}, f32[256,256]{1,0:T(8,128)}, u32[]{:S(2)}, u32[]{:S(2)}) %collective-permute-start.18) | collective-permute-done | bytes 262176 | tf_op jit(solution)/shard_map/ppermute | solution.py:409
  34.5 2.2 %schedule.8 = (f32[32,3,8,256]{3,2,1,0:T(8,128)}, s32[1,128]{1,0:T(1,128)S(1)}, f32[4,32,128]{2,1,0:T(8,128)S(1)}) custom-call(f32[32,8,896]{2,1,0:T(8,128)S(1)} %all-to-all-done.9.tile_ref.got_ref, f32[32,8,896]{2,1,0:T(8,128)S(1)} %all-to-all-done.9.tile_ref.got_ref, bf16[128,640]{1,0:T(8,128)(2,1)S(1)} %copy-done.1, bf16[96,128]{1,0:T(8,128)(2,1)S(1)} %copy-done.12, ...), custom_call_target="tpu_custom_call" | custom-call | tf_op jit(solution)/shard_map/schedule/pallas_call | solution.py:417
  36.7 4.3 %all-to-all-start.10 = ((f32[32,3,8,256]{3,2,1,0:T(8,128)}), f32[32,3,8,256]{3,2,1,0:T(8,128)S(1)}, u32[]{:S(2)}, u32[]{:S(2)}) async-start(f32[32,3,8,256]{3,2,1,0:T(8,128)} %get-tuple-element.1077), calls=%async_computation.10 | async-start | bytes 1572864 | tf_op jit(solution)/shard_map/all_to_all | solution.py:400
  41.0 1.1 %settle.9 = (f32[256,256]{1,0:T(8,128)S(1)}, f32[256,256]{1,0:T(8,128)S(1)}, f32[256,256]{1,0:T(8,128)S(1)}, f32[32,128]{1,0:T(8,128)S(1)}) custom-call(f32[4,32,128]{2,1,0:T(8,128)S(1)} %get-tuple-element.1071.facts_ref, bf16[128,256]{1,0:T(8,128)(2,1)S(1)} %copy-done, bf16[160,128]{1,0:T(8,128)(2,1)S(1)} %copy-done.2, f32[2,4,256,256]{3,2,1,0:T(8,128)} %a_hbm.5), custom_call_target="tpu_custom_call" | custom-call | tf_op jit(solution)/shard_map/settle/pallas_call | solution.py:431
  42.1 1.5 %collective-permute-start.20 = (f32[256,256]{1,0:T(8,128)S(1)}, f32[256,256]{1,0:T(8,128)}, u32[]{:S(2)}, u32[]{:S(2)}) collective-permute-start(f32[256,256]{1,0:T(8,128)S(1)} %get-tuple-element.1078), channel_id=1, source_target_pairs={{0,1},{1,0},{2,3},{3,2},{4,5},{5,4},{6,7},{7,6},{8,9},{9,8},{10,11... | collective-permute-start | bytes 786440 | tf_op jit(solution)/shard_map/ppermute | solution.py:409
  43.6 1.2 %collective-permute-start.21 = (f32[256,256]{1,0:T(8,128)S(1)}, f32[256,256]{1,0:T(8,128)}, u32[]{:S(2)}, u32[]{:S(2)}) collective-permute-start(f32[256,256]{1,0:T(8,128)S(1)} %get-tuple-element.1079), channel_id=1, source_target_pairs={{0,3},{1,2},{2,1},{3,0},{4,7},{5,6},{6,5},{7,4},{8,11},{9,10},{10,... | collective-permute-start | bytes 786440 | tf_op jit(solution)/shard_map/ppermute | solution.py:409
  44.8 0.1 collective-permute-start.19
  44.8 18.5 %collective-permute-done.20.refs_4_ = f32[256,256]{1,0:T(8,128)} collective-permute-done((f32[256,256]{1,0:T(8,128)S(1)}, f32[256,256]{1,0:T(8,128)}, u32[]{:S(2)}, u32[]{:S(2)}) %collective-permute-start.20) | collective-permute-done | bytes 262176 | tf_op jit(solution)/shard_map/ppermute | solution.py:409
  63.4 0.8 %collective-permute-start.22 = (f32[32,3,8,256]{3,2,1,0:T(8,128)S(1)}, f32[32,3,8,256]{3,2,1,0:T(8,128)S(1)}, u32[]{:S(2)}, u32[]{:S(2)}) collective-permute-start(f32[32,3,8,256]{3,2,1,0:T(8,128)S(1)} %all-to-all-done.10.mine), channel_id=1, source_target_pairs={{0,4},{4,0},{8,12},{12,8},{16,20},{20,16},{24,28},{28,24},{1,5},{5... | collective-permute-start | bytes 2359304 | tf_op jit(solution)/shard_map/ppermute | solution.py:412
  64.2 0.9 %judge.1 = (s32[1,128]{1,0:T(1,128)S(1)}, s32[1,128]{1,0:T(1,128)}, s32[1,128]{1,0:T(1,128)}, s32[2]{0:T(128)S(1)}) custom-call(f32[4,32,128]{2,1,0:T(8,128)S(1)} %get-tuple-element.1071.facts_ref, f32[32,128]{1,0:T(8,128)S(1)} %get-tuple-element.1072.place_ref, s32[1,128]{1,0:T(1,128)S(1)} %get-tuple-element.1073.rows_ref.rows, ...), custom_call_target="tpu_custom_call" | custom-call | tf_op jit(solution)/shard_map/judge/pallas_call | solution.py:444
  65.1 1.0 %collective-permute-done.22.theirs = f32[32,3,8,256]{3,2,1,0:T(8,128)S(1)} collective-permute-done((f32[32,3,8,256]{3,2,1,0:T(8,128)S(1)}, f32[32,3,8,256]{3,2,1,0:T(8,128)S(1)}, u32[]{:S(2)}, u32[]{:S(2)}) %collective-permute-start.22) | collective-permute-done | bytes 786464 | tf_op jit(solution)/shard_map/ppermute | solution.py:412
  66.1 3.0 %multiply.16 = f32[1,4,256,256]{3,2,1,0:T(8,128)} custom-call(s32[1,128]{1,0:T(1,128)S(1)} %get-tuple-element.1073.rows_ref.rows, s32[1,128]{1,0:T(1,128)S(1)} %get-tuple-element.1076.left, f32[32,3,8,256]{3,2,1,0:T(8,128)S(1)} %all-to-all-done.10.mine, f32[32,3,8,256]{3,2,1,0:T(8,128)S(1)} %collective-permute-done.22.theirs, ...), custom_call_target="tpu_custom_call", output_to_operand_aliasing={{}: (11, {})} | custom-call | tf_op jit(solution)/shard_map/multiply/pallas_call | solution.py:447
  69.2 0.2 conditional.1
  (17 shorter events, 0.0 us)
Async XLA Ops:
  2.7 31.8 %all-to-all-start.9 = ((f32[32,8,896]{2,1,0:T(8,128)}), f32[32,8,896]{2,1,0:T(8,128)S(1)}, u32[]{:S(2)}, u32[]{:S(2)}) async-start(f32[32,8,896]{2,1,0:T(8,128)} %prepare.1), calls=%async_computation.9 | async-start | bytes 1835008 | tf_op jit(solution)/shard_map/all_to_all | solution.py:400
  9.8 24.7 %copy-start.1 = (bf16[128,640]{1,0:T(8,128)(2,1)S(1)}, bf16[128,640]{1,0:T(8,128)(2,1)}, u32[]{:S(2)}) copy-start(bf16[128,640]{1,0:T(8,128)(2,1)} %constant.267.clone.refs_0_) | copy-start | bytes 491524
  9.8 24.7 %copy-start.11 = (bf16[128,128]{1,0:T(8,128)(2,1)S(1)}, bf16[128,128]{1,0:T(8,128)(2,1)}, u32[]{:S(2)}) copy-start(bf16[128,128]{1,0:T(8,128)(2,1)} %constant.269.clone.refs_2_) | copy-start | bytes 98308
  9.8 24.7 %copy-start.12 = (bf16[96,128]{1,0:T(8,128)(2,1)S(1)}, bf16[96,128]{1,0:T(8,128)(2,1)}, u32[]{:S(2)}) copy-start(bf16[96,128]{1,0:T(8,128)(2,1)} %constant.268.clone.refs_1_) | copy-start | bytes 73732
  9.9 24.7 %copy-start.13 = (bf16[32,96]{1,0:T(8,128)(2,1)S(1)}, bf16[32,96]{1,0:T(8,128)(2,1)}, u32[]{:S(2)}) copy-start(bf16[32,96]{1,0:T(8,128)(2,1)} %constant.270.clone.refs_3_) | copy-start | bytes 18436
  11.1 14.7 %collective-permute-start.16 = (f32[256,256]{1,0:T(8,128)S(1)}, f32[256,256]{1,0:T(8,128)S(1)}, u32[]{:S(2)}, u32[]{:S(2)}) collective-permute-start(f32[256,256]{1,0:T(8,128)S(1)} %get-tuple-element.1068._), channel_id=1, source_target_pairs={{0,2},{1,3},{2,0},{3,1},{4,6},{5,7},{6,4},{7,5},{8,10},{9,11},{10,... | collective-permute-start | bytes 786440 | tf_op jit(solution)/shard_map/ppermute | solution.py:409
  12.5 22.0 %collective-permute-start.18 = (f32[256,256]{1,0:T(8,128)S(1)}, f32[256,256]{1,0:T(8,128)}, u32[]{:S(2)}, u32[]{:S(2)}) collective-permute-start(f32[256,256]{1,0:T(8,128)S(1)} %get-tuple-element.1069), channel_id=1, source_target_pairs={{0,3},{1,2},{2,1},{3,0},{4,7},{5,6},{6,5},{7,4},{8,11},{9,10},{10,... | collective-permute-start | bytes 786440 | tf_op jit(solution)/shard_map/ppermute | solution.py:409
  13.5 21.0 %collective-permute-start.17 = (f32[256,256]{1,0:T(8,128)S(1)}, f32[256,256]{1,0:T(8,128)}, u32[]{:S(2)}, u32[]{:S(2)}) collective-permute-start(f32[256,256]{1,0:T(8,128)S(1)} %get-tuple-element.1069), channel_id=1, source_target_pairs={{0,1},{1,0},{2,3},{3,2},{4,5},{5,4},{6,7},{7,6},{8,9},{9,8},{10,11... | collective-permute-start | bytes 786440 | tf_op jit(solution)/shard_map/ppermute | solution.py:409
  14.9 26.1 %copy-start = (bf16[128,256]{1,0:T(8,128)(2,1)S(1)}, bf16[128,256]{1,0:T(8,128)(2,1)}, u32[]{:S(2)}) copy-start(bf16[128,256]{1,0:T(8,128)(2,1)} %constant.271.clone.inner) | copy-start | bytes 196612
  14.9 26.1 %copy-start.2 = (bf16[160,128]{1,0:T(8,128)(2,1)S(1)}, bf16[160,128]{1,0:T(8,128)(2,1)}, u32[]{:S(2)}) copy-start(bf16[160,128]{1,0:T(8,128)(2,1)} %constant.272.clone.chunk) | copy-start | bytes 122884
  36.7 26.7 %all-to-all-start.10 = ((f32[32,3,8,256]{3,2,1,0:T(8,128)}), f32[32,3,8,256]{3,2,1,0:T(8,128)S(1)}, u32[]{:S(2)}, u32[]{:S(2)}) async-start(f32[32,3,8,256]{3,2,1,0:T(8,128)} %get-tuple-element.1077), calls=%async_computation.10 | async-start | bytes 1572864 | tf_op jit(solution)/shard_map/all_to_all | solution.py:400
  42.1 21.3 %collective-permute-start.20 = (f32[256,256]{1,0:T(8,128)S(1)}, f32[256,256]{1,0:T(8,128)}, u32[]{:S(2)}, u32[]{:S(2)}) collective-permute-start(f32[256,256]{1,0:T(8,128)S(1)} %get-tuple-element.1078), channel_id=1, source_target_pairs={{0,1},{1,0},{2,3},{3,2},{4,5},{5,4},{6,7},{7,6},{8,9},{9,8},{10,11... | collective-permute-start | bytes 786440 | tf_op jit(solution)/shard_map/ppermute | solution.py:409
  43.6 19.8 %collective-permute-start.21 = (f32[256,256]{1,0:T(8,128)S(1)}, f32[256,256]{1,0:T(8,128)}, u32[]{:S(2)}, u32[]{:S(2)}) collective-permute-start(f32[256,256]{1,0:T(8,128)S(1)} %get-tuple-element.1079), channel_id=1, source_target_pairs={{0,3},{1,2},{2,1},{3,0},{4,7},{5,6},{6,5},{7,4},{8,11},{9,10},{10,... | collective-permute-start | bytes 786440 | tf_op jit(solution)/shard_map/ppermute | solution.py:409
  44.8 18.6 %collective-permute-start.19 = (f32[256,256]{1,0:T(8,128)S(1)}, f32[256,256]{1,0:T(8,128)}, u32[]{:S(2)}, u32[]{:S(2)}) collective-permute-start(f32[256,256]{1,0:T(8,128)S(1)} %get-tuple-element.1074._), channel_id=1, source_target_pairs={{0,2},{1,3},{2,0},{3,1},{4,6},{5,7},{6,4},{7,5},{8,10},{9,11},{10,... | collective-permute-start | bytes 786440 | tf_op jit(solution)/shard_map/ppermute | solution.py:409
  63.4 2.7 %collective-permute-start.22 = (f32[32,3,8,256]{3,2,1,0:T(8,128)S(1)}, f32[32,3,8,256]{3,2,1,0:T(8,128)S(1)}, u32[]{:S(2)}, u32[]{:S(2)}) collective-permute-start(f32[32,3,8,256]{3,2,1,0:T(8,128)S(1)} %all-to-all-done.10.mine), channel_id=1, source_target_pairs={{0,4},{4,0},{8,12},{12,8},{16,20},{20,16},{24,28},{28,24},{1,5},{5... | collective-permute-start | bytes 2359304 | tf_op jit(solution)/shard_map/ppermute | solution.py:412
  66.1 3.0 %copy-start.24 = (f32[32,96]{1,0:T(8,128)S(1)}, f32[32,96]{1,0:T(8,128)}, u32[]{:S(2)}) copy-start(f32[32,96]{1,0:T(8,128)} %constant.276.clone) | copy-start | bytes 36868

commit v7 on v6

--- a/solution.py
+++ b/solution.py
@@ -113,11 +113,16 @@
 
 
 def prepare(plan, entries, b_hbm, out_hbm, blocks, tile_ref, sems, out_sems):
-    def piece(c, j):
-        return pltpu.make_async_copy(b_hbm.at[c], blocks.at[j], sems.at[j])
-
-    def out(src, j, width):
-        return pltpu.make_async_copy(src, out_hbm.at[:, :, pl.ds(j * plan.bs, width)], out_sems.at[j])
+    half = plan.G // 2
+
+    def piece(c, j, n):
+        part = pl.ds(n * half, half)
+        return pltpu.make_async_copy(b_hbm.at[c, part], blocks.at[j, part], sems.at[j, n])
+
+    def out(j, n):
+        part = pl.ds(n * half, half)
+        dst = out_hbm.at[part, :, pl.ds(j * plan.bs, plan.bs)]
+        return pltpu.make_async_copy(blocks.at[j, part], dst, out_sems.at[j, n])
 
     row = entry_row(plan, entries)
     bits = entry_bits(row, plan.rows * plan.W, plan.nc)
@@ -128,26 +133,30 @@
 
             @pl.when(stored & (count == j))
             def _(c=c, j=j):
-                piece(c, j).start()
+                piece(c, j, 0).start()
+                piece(c, j, 1).start()
 
         count += stored.astype(I32)
 
     tile_ref[...] = jnp.broadcast_to(row.astype(F32)[None], tile_ref.shape)
-    last = out(tile_ref, plan.slots, LANES)
+    lanes = pl.ds(plan.slots * plan.bs, LANES)
+    last = pltpu.make_async_copy(tile_ref, out_hbm.at[:, :, lanes], out_sems.at[plan.slots, 0])
     last.start()
     for j in range(plan.slots):
 
         @pl.when(count > j)
         def _(j=j):
-            piece(0, j).wait()
-            out(blocks.at[j], j, plan.bs).start()
+            for n in range(2):
+                piece(0, j, n).wait()
+                out(j, n).start()
 
     last.wait()
     for j in range(plan.slots):
 
         @pl.when(count > j)
         def _(j=j):
-            out(blocks.at[j], j, plan.bs).wait()
+            for n in range(2):
+                out(j, n).wait()
 
 
 def stage(plan, wave, entries, a_hbm, *refs):
@@ -475,8 +484,8 @@
         [
             pltpu.VMEM((plan.slots, G, R, bs), F32),
             pltpu.VMEM((G, R, LANES), F32),
-            DMA((plan.slots,)),
-            DMA((plan.slots + 1,)),
+            DMA((plan.slots, 2)),
+            DMA((plan.slots + 1, 2)),
         ],
     )(entries, b_pieces)
     got = exchange(pieces)

time: 69.3 us -> 69.3 us (level)
  the two profiles are of different devices: /device:TPU:1 before, /device:TPU:0 now
where the time goes in v7:
time: 69.3 us; the launch traced here: 69.7 us
  waiting for transfers between devices  39 us (56%)
  starting transfers between devices  18.2 us (26%)
  Pallas kernels  11 us (16%)
  other arithmetic  0.77 us (1%)
    ppermute x6, waiting for transfers between devices, shift(): lax.ppermute(staged[o], ('col', 'depth'), list(perm(*plan.others[o])))  37.6 us
    all_to_all x2, starting transfers between devices, exchange(): return lax.all_to_all(pieces, plan.axes, 0, 0, tiled=True)  11.1 us
    ppermute x6, starting transfers between devices, shift(): lax.ppermute(staged[o], ('col', 'depth'), list(perm(*plan.others[o])))  7.11 us
    pallas_call x1, Pallas kernels, product(): call(functools.partial(multiply, plan, J, raw, len(lefts) // len(plan.oth...  2.64 us
    pallas_call x1, Pallas kernels, listed(): call(functools.partial(schedule, plan, J, *(None,) * first), (jax.ShapeDt...  2.18 us
    pallas_call x1, Pallas kernels, local(): call(functools.partial(prepare, plan), jax.ShapeDtypeStruct((G, R, width)...  1.97 us
  transfers between devices with their start and end apart: 9, of which 5 were waited for; matrix products, arithmetic and copies ran while one was open for 0% of the time, Pallas kernels for 6%

profile of v7, /device:TPU:0, one launch (start us, length us, event | category | flops | bytes accessed | tf_op | source)
XLA Modules:
  0.0 69.7 jit_solution(2713172172060761014)
XLA Ops:
  0.0 0.8 %pad_add_fusion.entries = s32[2,128]{1,0:T(2,128)S(1)} fusion(s32[2,4]{1,0:T(2,128)} %param.40, s32[1,4]{1,0:T(1,128)} %param.43, s32[1,4]{1,0:T(1,128)} %param.42), kind=kLoop, calls=%fused_computation.4 | loop fusion | flops 512 | bytes 1088 | tf_op jit(solution)/shard_map/add | solution.py:475
  0.8 2.0 %prepare.1 = f32[32,8,896]{2,1,0:T(8,128)} custom-call(s32[2,128]{1,0:T(2,128)S(1)} %pad_add_fusion.entries, f32[4,32,8,256]{3,2,1,0:T(8,128)} %bitcast.41), custom_call_target="tpu_custom_call" | custom-call | tf_op jit(solution)/shard_map/prepare/pallas_call | solution.py:479
  2.8 7.4 %all-to-all-start.9 = ((f32[32,8,896]{2,1,0:T(8,128)}), f32[32,8,896]{2,1,0:T(8,128)S(1)}, u32[]{:S(2)}, u32[]{:S(2)}) async-start(f32[32,8,896]{2,1,0:T(8,128)} %prepare.1), calls=%async_computation.9 | async-start | bytes 1835008 | tf_op jit(solution)/shard_map/all_to_all | solution.py:409
  10.2 0.0 copy-start.1
  10.2 0.0 copy-start.11
  10.3 1.3 %stage.1 = (f32[256,256]{1,0:T(8,128)S(1)}, f32[256,256]{1,0:T(8,128)S(1)}) custom-call(s32[2,128]{1,0:T(2,128)S(1)} %pad_add_fusion.entries, f32[2,4,256,256]{3,2,1,0:T(8,128)} %a_hbm.5), custom_call_target="tpu_custom_call" | custom-call | tf_op jit(solution)/shard_map/stage/pallas_call | solution.py:494
  11.5 1.8 %collective-permute-start.16 = (f32[256,256]{1,0:T(8,128)S(1)}, f32[256,256]{1,0:T(8,128)S(1)}, u32[]{:S(2)}, u32[]{:S(2)}) collective-permute-start(f32[256,256]{1,0:T(8,128)S(1)} %get-tuple-element.1068._), channel_id=1, source_target_pairs={{0,2},{1,3},{2,0},{3,1},{4,6},{5,7},{6,4},{7,5},{8,10},{9,11},{10,... | collective-permute-start | bytes 786440 | tf_op jit(solution)/shard_map/ppermute | solution.py:418
  13.4 1.5 %collective-permute-start.18 = (f32[256,256]{1,0:T(8,128)S(1)}, f32[256,256]{1,0:T(8,128)}, u32[]{:S(2)}, u32[]{:S(2)}) collective-permute-start(f32[256,256]{1,0:T(8,128)S(1)} %get-tuple-element.1069), channel_id=1, source_target_pairs={{0,3},{1,2},{2,1},{3,0},{4,7},{5,6},{6,5},{7,4},{8,11},{9,10},{10,... | collective-permute-start | bytes 786440 | tf_op jit(solution)/shard_map/ppermute | solution.py:418
  14.8 0.3 collective-permute-start.17
  15.1 1.0 %clear.1.refs_6_ = f32[1,4,256,256]{3,2,1,0:T(8,128)} custom-call(f32[256,256]{1,0:T(8,128)S(1)} %get-tuple-element.1068._), custom_call_target="tpu_custom_call" | custom-call | tf_op jit(solution)/shard_map/clear/pallas_call | solution.py:504
  16.1 11.4 %collective-permute-done.16.refs_0_ = f32[256,256]{1,0:T(8,128)S(1)} collective-permute-done((f32[256,256]{1,0:T(8,128)S(1)}, f32[256,256]{1,0:T(8,128)S(1)}, u32[]{:S(2)}, u32[]{:S(2)}) %collective-permute-start.16) | collective-permute-done | bytes 262176 | tf_op jit(solution)/shard_map/ppermute | solution.py:418
  27.6 7.9 %collective-permute-done.18.refs_2_ = f32[256,256]{1,0:T(8,128)} collective-permute-done((f32[256,256]{1,0:T(8,128)S(1)}, f32[256,256]{1,0:T(8,128)}, u32[]{:S(2)}, u32[]{:S(2)}) %collective-permute-start.18) | collective-permute-done | bytes 262176 | tf_op jit(solution)/shard_map/ppermute | solution.py:418
  35.5 2.2 %schedule.8 = (f32[32,3,8,256]{3,2,1,0:T(8,128)}, s32[1,128]{1,0:T(1,128)S(1)}, f32[4,32,128]{2,1,0:T(8,128)S(1)}) custom-call(f32[32,8,896]{2,1,0:T(8,128)S(1)} %all-to-all-done.9.tile_ref.got_ref, f32[32,8,896]{2,1,0:T(8,128)S(1)} %all-to-all-done.9.tile_ref.got_ref, bf16[128,640]{1,0:T(8,128)(2,1)S(1)} %copy-done.1, bf16[96,128]{1,0:T(8,128)(2,1)S(1)} %copy-done.12, ...), custom_call_target="tpu_custom_call" | custom-call | tf_op jit(solution)/shard_map/schedule/pallas_call | solution.py:426
  37.7 3.7 %all-to-all-start.10 = ((f32[32,3,8,256]{3,2,1,0:T(8,128)}), f32[32,3,8,256]{3,2,1,0:T(8,128)S(1)}, u32[]{:S(2)}, u32[]{:S(2)}) async-start(f32[32,3,8,256]{3,2,1,0:T(8,128)} %get-tuple-element.1077), calls=%async_computation.10 | async-start | bytes 1572864 | tf_op jit(solution)/shard_map/all_to_all | solution.py:409
  41.4 1.1 %settle.9 = (f32[256,256]{1,0:T(8,128)S(1)}, f32[256,256]{1,0:T(8,128)S(1)}, f32[256,256]{1,0:T(8,128)S(1)}, f32[32,128]{1,0:T(8,128)S(1)}) custom-call(f32[4,32,128]{2,1,0:T(8,128)S(1)} %get-tuple-element.1071.facts_ref, bf16[128,256]{1,0:T(8,128)(2,1)S(1)} %copy-done, bf16[160,128]{1,0:T(8,128)(2,1)S(1)} %copy-done.2, f32[2,4,256,256]{3,2,1,0:T(8,128)} %a_hbm.5), custom_call_target="tpu_custom_call" | custom-call | tf_op jit(solution)/shard_map/settle/pallas_call | solution.py:440
  42.5 1.8 %collective-permute-start.20 = (f32[256,256]{1,0:T(8,128)S(1)}, f32[256,256]{1,0:T(8,128)}, u32[]{:S(2)}, u32[]{:S(2)}) collective-permute-start(f32[256,256]{1,0:T(8,128)S(1)} %get-tuple-element.1078), channel_id=1, source_target_pairs={{0,1},{1,0},{2,3},{3,2},{4,5},{5,4},{6,7},{7,6},{8,9},{9,8},{10,11... | collective-permute-start | bytes 786440 | tf_op jit(solution)/shard_map/ppermute | solution.py:418
  44.3 1.5 %collective-permute-start.21 = (f32[256,256]{1,0:T(8,128)S(1)}, f32[256,256]{1,0:T(8,128)}, u32[]{:S(2)}, u32[]{:S(2)}) collective-permute-start(f32[256,256]{1,0:T(8,128)S(1)} %get-tuple-element.1079), channel_id=1, source_target_pairs={{0,3},{1,2},{2,1},{3,0},{4,7},{5,6},{6,5},{7,4},{8,11},{9,10},{10,... | collective-permute-start | bytes 786440 | tf_op jit(solution)/shard_map/ppermute | solution.py:418
  45.8 0.3 collective-permute-start.19
  46.1 18.0 %collective-permute-done.20.refs_4_ = f32[256,256]{1,0:T(8,128)} collective-permute-done((f32[256,256]{1,0:T(8,128)S(1)}, f32[256,256]{1,0:T(8,128)}, u32[]{:S(2)}, u32[]{:S(2)}) %collective-permute-start.20) | collective-permute-done | bytes 262176 | tf_op jit(solution)/shard_map/ppermute | solution.py:418
  64.1 0.2 collective-permute-done.19.refs_3_
  64.3 0.9 %judge.1 = (s32[1,128]{1,0:T(1,128)S(1)}, s32[1,128]{1,0:T(1,128)}, s32[1,128]{1,0:T(1,128)}, s32[2]{0:T(128)S(1)}) custom-call(f32[4,32,128]{2,1,0:T(8,128)S(1)} %get-tuple-element.1071.facts_ref, f32[32,128]{1,0:T(8,128)S(1)} %get-tuple-element.1072.place_ref, s32[1,128]{1,0:T(1,128)S(1)} %get-tuple-element.1073.rows_ref.rows, ...), custom_call_target="tpu_custom_call" | custom-call | tf_op jit(solution)/shard_map/judge/pallas_call | solution.py:453
  65.2 1.4 %collective-permute-done.22.theirs = f32[32,3,8,256]{3,2,1,0:T(8,128)S(1)} collective-permute-done((f32[32,3,8,256]{3,2,1,0:T(8,128)S(1)}, f32[32,3,8,256]{3,2,1,0:T(8,128)S(1)}, u32[]{:S(2)}, u32[]{:S(2)}) %collective-permute-start.22) | collective-permute-done | bytes 786464 | tf_op jit(solution)/shard_map/ppermute | solution.py:421
  66.6 2.6 %multiply.16 = f32[1,4,256,256]{3,2,1,0:T(8,128)} custom-call(s32[1,128]{1,0:T(1,128)S(1)} %get-tuple-element.1073.rows_ref.rows, s32[1,128]{1,0:T(1,128)S(1)} %get-tuple-element.1076.left, f32[32,3,8,256]{3,2,1,0:T(8,128)S(1)} %all-to-all-done.10.mine, f32[32,3,8,256]{3,2,1,0:T(8,128)S(1)} %collective-permute-done.22.theirs, ...), custom_call_target="tpu_custom_call", output_to_operand_aliasing={{}: (11, {})} | custom-call | tf_op jit(solution)/shard_map/multiply/pallas_call | solution.py:456
  69.3 0.2 conditional.1
  (17 shorter events, 0.0 us)
Async XLA Ops:
  2.8 32.7 %all-to-all-start.9 = ((f32[32,8,896]{2,1,0:T(8,128)}), f32[32,8,896]{2,1,0:T(8,128)S(1)}, u32[]{:S(2)}, u32[]{:S(2)}) async-start(f32[32,8,896]{2,1,0:T(8,128)} %prepare.1), calls=%async_computation.9 | async-start | bytes 1835008 | tf_op jit(solution)/shard_map/all_to_all | solution.py:409
  10.2 25.3 %copy-start.1 = (bf16[128,640]{1,0:T(8,128)(2,1)S(1)}, bf16[128,640]{1,0:T(8,128)(2,1)}, u32[]{:S(2)}) copy-start(bf16[128,640]{1,0:T(8,128)(2,1)} %constant.267.clone.refs_0_) | copy-start | bytes 491524
  10.2 25.3 %copy-start.11 = (bf16[128,128]{1,0:T(8,128)(2,1)S(1)}, bf16[128,128]{1,0:T(8,128)(2,1)}, u32[]{:S(2)}) copy-start(bf16[128,128]{1,0:T(8,128)(2,1)} %constant.269.clone.refs_2_) | copy-start | bytes 98308
  10.2 25.3 %copy-start.12 = (bf16[96,128]{1,0:T(8,128)(2,1)S(1)}, bf16[96,128]{1,0:T(8,128)(2,1)}, u32[]{:S(2)}) copy-start(bf16[96,128]{1,0:T(8,128)(2,1)} %constant.268.clone.refs_1_) | copy-start | bytes 73732
  10.2 25.3 %copy-start.13 = (bf16[32,96]{1,0:T(8,128)(2,1)S(1)}, bf16[32,96]{1,0:T(8,128)(2,1)}, u32[]{:S(2)}) copy-start(bf16[32,96]{1,0:T(8,128)(2,1)} %constant.270.clone.refs_3_) | copy-start | bytes 18436
  11.5 16.0 %collective-permute-start.16 = (f32[256,256]{1,0:T(8,128)S(1)}, f32[256,256]{1,0:T(8,128)S(1)}, u32[]{:S(2)}, u32[]{:S(2)}) collective-permute-start(f32[256,256]{1,0:T(8,128)S(1)} %get-tuple-element.1068._), channel_id=1, source_target_pairs={{0,2},{1,3},{2,0},{3,1},{4,6},{5,7},{6,4},{7,5},{8,10},{9,11},{10,... | collective-permute-start | bytes 786440 | tf_op jit(solution)/shard_map/ppermute | solution.py:418
  13.4 22.1 %collective-permute-start.18 = (f32[256,256]{1,0:T(8,128)S(1)}, f32[256,256]{1,0:T(8,128)}, u32[]{:S(2)}, u32[]{:S(2)}) collective-permute-start(f32[256,256]{1,0:T(8,128)S(1)} %get-tuple-element.1069), channel_id=1, source_target_pairs={{0,3},{1,2},{2,1},{3,0},{4,7},{5,6},{6,5},{7,4},{8,11},{9,10},{10,... | collective-permute-start | bytes 786440 | tf_op jit(solution)/shard_map/ppermute | solution.py:418
  14.8 20.7 %collective-permute-start.17 = (f32[256,256]{1,0:T(8,128)S(1)}, f32[256,256]{1,0:T(8,128)}, u32[]{:S(2)}, u32[]{:S(2)}) collective-permute-start(f32[256,256]{1,0:T(8,128)S(1)} %get-tuple-element.1069), channel_id=1, source_target_pairs={{0,1},{1,0},{2,3},{3,2},{4,5},{5,4},{6,7},{7,6},{8,9},{9,8},{10,11... | collective-permute-start | bytes 786440 | tf_op jit(solution)/shard_map/ppermute | solution.py:418
  16.1 25.3 %copy-start = (bf16[128,256]{1,0:T(8,128)(2,1)S(1)}, bf16[128,256]{1,0:T(8,128)(2,1)}, u32[]{:S(2)}) copy-start(bf16[128,256]{1,0:T(8,128)(2,1)} %constant.271.clone.inner) | copy-start | bytes 196612
  16.1 25.3 %copy-start.2 = (bf16[160,128]{1,0:T(8,128)(2,1)S(1)}, bf16[160,128]{1,0:T(8,128)(2,1)}, u32[]{:S(2)}) copy-start(bf16[160,128]{1,0:T(8,128)(2,1)} %constant.272.clone.chunk) | copy-start | bytes 122884
  37.7 26.6 %all-to-all-start.10 = ((f32[32,3,8,256]{3,2,1,0:T(8,128)}), f32[32,3,8,256]{3,2,1,0:T(8,128)S(1)}, u32[]{:S(2)}, u32[]{:S(2)}) async-start(f32[32,3,8,256]{3,2,1,0:T(8,128)} %get-tuple-element.1077), calls=%async_computation.10 | async-start | bytes 1572864 | tf_op jit(solution)/shard_map/all_to_all | solution.py:409
  42.5 21.6 %collective-permute-start.20 = (f32[256,256]{1,0:T(8,128)S(1)}, f32[256,256]{1,0:T(8,128)}, u32[]{:S(2)}, u32[]{:S(2)}) collective-permute-start(f32[256,256]{1,0:T(8,128)S(1)} %get-tuple-element.1078), channel_id=1, source_target_pairs={{0,1},{1,0},{2,3},{3,2},{4,5},{5,4},{6,7},{7,6},{8,9},{9,8},{10,11... | collective-permute-start | bytes 786440 | tf_op jit(solution)/shard_map/ppermute | solution.py:418
  44.3 19.7 %collective-permute-start.21 = (f32[256,256]{1,0:T(8,128)S(1)}, f32[256,256]{1,0:T(8,128)}, u32[]{:S(2)}, u32[]{:S(2)}) collective-permute-start(f32[256,256]{1,0:T(8,128)S(1)} %get-tuple-element.1079), channel_id=1, source_target_pairs={{0,3},{1,2},{2,1},{3,0},{4,7},{5,6},{6,5},{7,4},{8,11},{9,10},{10,... | collective-permute-start | bytes 786440 | tf_op jit(solution)/shard_map/ppermute | solution.py:418
  45.8 18.5 %collective-permute-start.19 = (f32[256,256]{1,0:T(8,128)S(1)}, f32[256,256]{1,0:T(8,128)}, u32[]{:S(2)}, u32[]{:S(2)}) collective-permute-start(f32[256,256]{1,0:T(8,128)S(1)} %get-tuple-element.1074._), channel_id=1, source_target_pairs={{0,2},{1,3},{2,0},{3,1},{4,6},{5,7},{6,4},{7,5},{8,10},{9,11},{10,... | collective-permute-start | bytes 786440 | tf_op jit(solution)/shard_map/ppermute | solution.py:418
  64.3 2.3 %collective-permute-start.22 = (f32[32,3,8,256]{3,2,1,0:T(8,128)S(1)}, f32[32,3,8,256]{3,2,1,0:T(8,128)S(1)}, u32[]{:S(2)}, u32[]{:S(2)}) collective-permute-start(f32[32,3,8,256]{3,2,1,0:T(8,128)S(1)} %all-to-all-done.10.mine), channel_id=1, source_target_pairs={{0,4},{4,0},{8,12},{12,8},{16,20},{20,16},{24,28},{28,24},{1,5},{5... | collective-permute-start | bytes 2359304 | tf_op jit(solution)/shard_map/ppermute | solution.py:421
  66.6 2.7 %copy-start.24 = (f32[32,96]{1,0:T(8,128)S(1)}, f32[32,96]{1,0:T(8,128)}, u32[]{:S(2)}) copy-start(f32[32,96]{1,0:T(8,128)} %constant.276.clone) | copy-start | bytes 36868
